TPU v7x, 32 devices: a whole 2x2x4 slice. The times are simulated.
32 devices in a mesh: seg: 8 (over y, x, core), head: 4 (over z).
Axes of the slice: x: 2, y: 2, z: 4, core: 2. Of those that a mesh axis runs over, the one named last changes fastest.
Arguments:
- query_feat: float32 [1792, 25600], P('head', 'seg'), may hold values from -6 to 6
- key_feat: float32 [1792, 25600], P('head', 'seg'), may hold values from -6 to 6
- value_feat: float32 [1792, 25600], P('head', 'seg'), may hold values from -5.5 to 5.5
- grad_out: float32 [1792, 25600], P('head', 'seg'), may hold values from -6 to 6
- spatial_weight: float32 [3, 3, 1792], replicated, may hold values from -2 to 2
- temporal_weight: float32 [3, 1792], replicated, may hold values from -3.5 to 3.5
Outputs:
- grad_query: float32 [1792, 25600], P('head', 'seg')
- grad_key: float32 [1792, 25600], P('head', 'seg')
- grad_value: float32 [1792, 25600], P('head', 'seg')
- mixed: float32 [32, 20, 40, 1792], P('seg', None, 'head')
All inputs are finite; a program needn't handle non-finite values.
Results may differ from a plain program's by a relative error of at most 0.00008.
Values sent between devices are 32-bit elements; how exact they have to be, the bound alone decides.
No kernel may reach another device: no remote copies, remote signals or barrier semaphores. Data moves between devices by JAX's collectives and lax.ppermute only.
A program may use at most 128 MiB of HBM per device.

v0:
```python
import functools

import jax
import jax.numpy as jnp
from jax import lax
from jax.experimental import pallas as pl
from jax.experimental.pallas import tpu as pltpu
from jax.sharding import PartitionSpec as P

HEAD_SIZE = 112
ROWS = 20
COLS = 40
LANES = 128
AUG = -(-(HEAD_SIZE + 1) // LANES) * LANES
BLOCK = 4
VMEM = 56 * 1024 * 1024

f32 = jnp.float32
bf16 = jnp.bfloat16


def split(x):
    high = x.astype(bf16)
    return high, (x - high.astype(f32)).astype(bf16)


def dot(a, b, dims):
    return lax.dot_general(a, b, (dims, ((), ())), preferred_element_type=f32)


def stacked(x):
    high, low = split(x)
    return jnp.concatenate([high, low], axis=0)


def over_tokens(a, b):
    rows, cols = a.shape[0], b.shape[0]
    whole = dot(stacked(a), stacked(b), ((1,), (1,)))
    top, low = whole[:rows], whole[rows:, :cols]
    return top[:, :cols] + (top[:, cols:] + low)


def prepared(state):
    high, low = split(state)
    top = jnp.concatenate([high, high], axis=1)
    return jnp.concatenate([top, jnp.concatenate([low, jnp.zeros_like(low)], axis=1)], axis=0)


def times(pieces, x):
    high, low = split(x)
    spare = jnp.zeros((AUG - HEAD_SIZE, x.shape[1]), bf16)
    whole = dot(pieces, jnp.concatenate([high, spare, low, spare], axis=0), ((1,), (0,)))
    return whole[:HEAD_SIZE] + whole[HEAD_SIZE:]


def windows(frames, span, tokens):
    out = []
    for f in range(frames):
        first, last = f * span, (f + 1) * span
        low = first // LANES * LANES
        high = min(-(-last // LANES) * LANES, tokens)
        out.append((low, high, first, last))
    return out


def inside(window):
    low, high, first, last = window
    lane = lax.broadcasted_iota(jnp.int32, (1, high - low), 1) + low
    return (lane >= first) & (lane < last)


def cost(flops, data):
    return pl.CostEstimate(flops=1, bytes_accessed=1, transcendentals=0)


def params(count=1):
    return pltpu.CompilerParams(
        dimension_semantics=("arbitrary",) * count, vmem_limit_bytes=VMEM
    )


def states_kernel(wins, key_ref, value_ref, local_ref, total_ref):
    total = jnp.zeros((HEAD_SIZE, AUG), f32)
    for f, win in enumerate(wins):
        low, high, _, _ = win
        feat = jnp.where(inside(win), jnp.exp(key_ref[:, low:high]), 0.0)
        ones = jnp.ones((AUG - HEAD_SIZE, high - low), f32)
        value = jnp.concatenate([value_ref[:, low:high], ones], axis=0)
        part = over_tokens(feat, value)
        local_ref[0, f] = part
        total = total + part
    total_ref[0] = total


def local_states(key_feat, value_feat, frames, heads):
    tokens = key_feat.shape[1]
    wins = windows(frames, ROWS * COLS, tokens)
    block = pl.BlockSpec((HEAD_SIZE, tokens), lambda h: (h, 0))
    return pl.pallas_call(
        functools.partial(states_kernel, wins),
        grid=(heads,),
        in_specs=[block, block],
        out_specs=[
            pl.BlockSpec((1, frames, HEAD_SIZE, AUG), lambda h: (h, 0, 0, 0)),
            pl.BlockSpec((1, HEAD_SIZE, AUG), lambda h: (h, 0, 0)),
        ],
        out_shape=[
            jax.ShapeDtypeStruct((heads, frames, HEAD_SIZE, AUG), f32),
            jax.ShapeDtypeStruct((heads, HEAD_SIZE, AUG), f32),
        ],
        compiler_params=params(),
        cost_estimate=cost(6 * heads * tokens * AUG * AUG, 8 * heads * HEAD_SIZE * tokens),
        name="local_states",
    )(key_feat, value_feat)


def xor_move(array, axis, by):
    count = lax.axis_size(axis)
    return lax.ppermute(array, axis, [(i, i ^ by) for i in range(count)])


def joined_kernel(reverse, steps, *refs):
    blocks, out_ref = refs[: len(steps)], refs[-1]
    place = lax.axis_index("seg")
    total = jnp.zeros(out_ref.shape, f32)
    for by, block in zip(steps, blocks):
        ahead = (place ^ by) > place if reverse else (place ^ by) < place
        total = total + jnp.where(ahead, block[...], 0.0)
    out_ref[...] = total


def joined(reverse, steps, blocks, after):
    one = blocks[0]
    block = pl.BlockSpec(one.shape, lambda: (0,) * one.ndim)
    return pl.pallas_call(
        functools.partial(joined_kernel, reverse, steps),
        in_specs=[block] * len(blocks) + [pl.BlockSpec(memory_space=pl.ANY)] * len(after),
        out_specs=block,
        out_shape=jax.ShapeDtypeStruct(one.shape, f32),
        name="joined",
    )(*blocks, *after)


def entering(total, reverse, after):
    count = lax.axis_size("seg")
    odd = (lax.axis_index("seg") & 1) == 1
    half = total.shape[0] // 2
    mate = xor_move(total, "seg", 1)
    mine = jnp.where(odd, total[half:] + mate[half:], total[:half] + mate[:half])
    steps = tuple(range(2, count, 2))
    blocks = [xor_move(mine, "seg", by) for by in steps]
    part = joined(reverse, steps, blocks, after)
    return part, xor_move(part, "seg", 1), mate


def whole_state(parts, reverse):
    part, other, mate = parts
    odd = (lax.axis_index("seg") & 1) == 1
    full = jnp.where(
        odd, jnp.concatenate([other, part], axis=0), jnp.concatenate([part, other], axis=0)
    )
    late = jnp.logical_not(odd) if reverse else odd
    return full + jnp.where(late, mate, 0.0)


def turn_kernel(query_ref, out_ref):
    out_ref[...] = jnp.exp(query_ref[...]).T


def turned(query_feat):
    chans, tokens = query_feat.shape
    step = 640 if tokens % 640 == 0 else tokens
    return pl.pallas_call(
        turn_kernel,
        grid=(tokens // step,),
        in_specs=[pl.BlockSpec((chans, step), lambda i: (0, i))],
        out_specs=pl.BlockSpec((step, chans), lambda i: (i, 0)),
        out_shape=jax.ShapeDtypeStruct((tokens, chans), f32),
        compiler_params=params(),
        cost_estimate=cost(0, 8 * chans * tokens),
        name="turned",
    )(query_feat)


def forward_kernel(
    start, frames, heads, head_devs, part_ref, other_ref, mate_ref, local_ref, spatial_ref,
    temporal_ref, prev_ref, cur_ref, next_ref, *rest
):
    late_ref, early_ref, halo_ref, bd_high, bd_low, weight_ref = rest[-6:]
    chans = heads * HEAD_SIZE
    wide = bd_high.shape[2]
    width = COLS // head_devs
    half = BLOCK // 2
    step = pl.program_id(0)

    @pl.when(step == 0)
    def _():
        me = lax.axis_index("head")
        odd = (lax.axis_index("seg") & 1) == 1
        weight_ref[...] = jnp.zeros_like(weight_ref)
        for z in range(head_devs):

            @pl.when(me == z)
            def _():
                at = slice(z * chans, (z + 1) * chans)
                for r in range(3):
                    weight_ref[3 * r : 3 * r + 3, :chans] = spatial_ref[r, :, at]
                weight_ref[9:12, :chans] = temporal_ref[:, at]

        lane = lax.broadcasted_iota(jnp.int32, (HEAD_SIZE, LANES), 1)
        last = wide // LANES - 1
        for h in range(heads):
            first, second = part_ref, other_ref
            if h >= heads // 2:
                first, second = second, first
            g = h % (heads // 2)
            state = jnp.where(odd, second[g] + mate_ref[h], first[g])
            tile, shift = divmod(h * HEAD_SIZE, LANES)
            over = shift + HEAD_SIZE - LANES
            at = pl.ds(h * HEAD_SIZE, HEAD_SIZE)
            for f in range(frames):
                state = state + local_ref[h, f]
                moved = pltpu.roll(state, shift, 1) if shift else state
                sums = state[:, HEAD_SIZE : HEAD_SIZE + 1]
                for t in range(last + 1):
                    value = None
                    if t == tile:
                        value = jnp.where((lane >= shift) & (lane < shift + HEAD_SIZE), moved, 0.0)
                    elif t == tile + 1 and over > 0:
                        value = jnp.where(lane < over, moved, 0.0)
                    if t == last:
                        value = jnp.zeros_like(state) if value is None else value
                        value = jnp.where(lane == chans - last * LANES + h, sums, value)
                    span = slice(t * LANES, (t + 1) * LANES)
                    if value is None:
                        bd_high[f, at, span] = jnp.zeros((HEAD_SIZE, LANES), bf16)
                        bd_low[f, at, span] = jnp.zeros((HEAD_SIZE, LANES), bf16)
                    else:
                        bd_high[f, at, span], bd_low[f, at, span] = split(value)

    block = start + step
    top = jnp.where(block == 0, 0.0, 1.0)
    bottom = jnp.where(block == ROWS // BLOCK - 1, 0.0, 1.0)
    count = (BLOCK + 2) * COLS
    mids = BLOCK * COLS
    column = lax.broadcasted_iota(jnp.int32, (count, 1), 0) % COLS
    head_of = lax.broadcasted_iota(jnp.int32, (1, wide), 1) // HEAD_SIZE

    def active(f):
        feat = jnp.concatenate([prev_ref[f], cur_ref[f], next_ref[f]], axis=0)
        high, low = split(feat)
        numer = dot(high, bd_low[f], ((1,), (0,))) + dot(low, bd_high[f], ((1,), (0,)))
        numer = numer + dot(high, bd_high[f], ((1,), (0,)))
        inverse = 1.0 / numer[:, chans : chans + heads]
        scale = inverse[:, heads - 1 : heads]
        for h in range(heads - 2, -1, -1):
            scale = jnp.where(head_of <= h, inverse[:, h : h + 1], scale)
        att = numer * scale
        att = jnp.concatenate([att[:COLS] * top, att[COLS:-COLS], att[-COLS:] * bottom], axis=0)
        left = jnp.where(column == 0, 0.0, pltpu.roll(att, 1, 0))
        right = jnp.where(column == COLS - 1, 0.0, pltpu.roll(att, count - 1, 0))
        total = jnp.zeros((mids, wide), f32)
        for r in range(3):
            for c, side in enumerate((left, att, right)):
                total = total + weight_ref[3 * r + c : 3 * r + c + 1, :] * side[r * COLS : r * COLS + mids]
        return total / (1.0 + jnp.exp(-total))

    taps = [weight_ref[9 + i : 10 + i, :] for i in range(3)]
    acts = [active(f) for f in range(frames)]

    def put(ref, k, value):
        for z in range(head_devs):
            for r in range(BLOCK):
                rows = value[r * COLS + z * width : r * COLS + (z + 1) * width, :chans]
                ref[z, r % half, :, k, (r // half) * chans : (r // half + 1) * chans] = rows

    for f in range(2, frames):
        put(late_ref, f - 2, taps[0] * acts[f] + taps[1] * acts[f - 1] + taps[2] * acts[f - 2])
    put(early_ref, 0, taps[0] * acts[0])
    put(early_ref, 1, taps[0] * acts[1] + taps[1] * acts[0])
    put(halo_ref, 0, taps[1] * acts[-1] + taps[2] * acts[-2])
    put(halo_ref, 1, taps[2] * acts[-1])


def forward(parts, local, weights, feat, start, steps, head_devs, after):
    heads, frames = local.shape[:2]
    chans = heads * HEAD_SIZE
    wide = -(-(chans + heads) // LANES) * LANES
    parts = list(parts)
    width = COLS // head_devs
    half = BLOCK // 2
    last = ROWS // BLOCK

    def whole(a):
        return pl.BlockSpec(a.shape, lambda i: (0,) * a.ndim)

    def out(count):
        shape = (head_devs, steps * half, width, count, 2 * chans)
        spec = pl.BlockSpec((head_devs, half, width, count, 2 * chans), lambda i: (0, i, 0, 0, 0))
        return jax.ShapeDtypeStruct(shape, f32), spec

    outs = [out(frames - 2), out(2), out(2)]
    feat = feat.reshape(frames, ROWS * COLS, chans)
    return pl.pallas_call(
        functools.partial(forward_kernel, start, frames, heads, head_devs),
        grid=(steps,),
        in_specs=[
                *[whole(p) for p in parts],
                whole(local),
                *[whole(w) for w in weights],
                pl.BlockSpec(
                    (frames, COLS, chans),
                    lambda i: (0, jnp.maximum((start + i) * BLOCK - 1, 0), 0),
                ),
                pl.BlockSpec((frames, BLOCK * COLS, chans), lambda i: (0, start + i, 0)),
                pl.BlockSpec(
                    (frames, COLS, chans),
                    lambda i: (0, jnp.minimum((start + i + 1) * BLOCK, ROWS - 1), 0),
                ),
            ]
            + [pl.BlockSpec(memory_space=pl.ANY)] * len(after),
        out_specs=[spec for _, spec in outs],
        scratch_shapes=[
                pltpu.VMEM((frames, chans, wide), bf16),
                pltpu.VMEM((frames, chans, wide), bf16),
                pltpu.VMEM((16, wide), f32),
        ],
        out_shape=[shape for shape, _ in outs],
        compiler_params=params(),
        cost_estimate=cost(6 * steps * 960 * wide * wide, steps * 8000000),
        name="forward_rows",
    )(*parts, local, *weights, feat, feat, feat, *after)


def query_kernel(wins, query_ref, grad_ref, before_ref, local_ref, *rest):
    out_ref, part_ref, total_ref = rest[-3:]
    state = before_ref[0]
    total = jnp.zeros((HEAD_SIZE, AUG), f32)
    for f, win in enumerate(wins):
        low, high, _, _ = win
        keep = inside(win)
        state = state + local_ref[0, f]
        sums = state[:, HEAD_SIZE : HEAD_SIZE + 1]
        feat = jnp.exp(query_ref[:, low:high])
        inverse = 1.0 / jnp.sum(feat * sums, axis=0, keepdims=True)
        numer = grad_ref[:, low:high] * inverse
        moved = times(prepared(state), numer)
        denom = -jnp.sum(feat * moved, axis=0, keepdims=True) * inverse
        grad = (moved + sums * denom) * feat
        if low == 0:
            out_ref[:, low:high] = grad
        else:
            out_ref[:, low:high] = jnp.where(keep, grad, out_ref[:, low:high])
        spare = jnp.zeros((AUG - HEAD_SIZE - 8, high - low), f32)
        both = jnp.concatenate([numer, jnp.broadcast_to(denom, (8, high - low)), spare], axis=0)
        both = jnp.where(keep, both, 0.0)
        part = over_tokens(feat, both)
        part_ref[0, f] = part
        total = total + part
    total_ref[0] = total


def query_grads(query_feat, grad_out, before, local, after):
    tokens = query_feat.shape[1]
    heads, frames = local.shape[:2]
    wins = windows(frames, ROWS * COLS, tokens)
    block = pl.BlockSpec((HEAD_SIZE, tokens), lambda h: (h, 0))
    one = pl.BlockSpec((1, HEAD_SIZE, AUG), lambda h: (h, 0, 0))
    each = pl.BlockSpec((1, frames, HEAD_SIZE, AUG), lambda h: (h, 0, 0, 0))
    return pl.pallas_call(
        functools.partial(query_kernel, wins),
        grid=(heads,),
        in_specs=[block, block, one, each] + [pl.BlockSpec(memory_space=pl.ANY)] * len(after),
        out_specs=[block, each, one],
        out_shape=[
            jax.ShapeDtypeStruct(query_feat.shape, f32),
            jax.ShapeDtypeStruct(local.shape, f32),
            jax.ShapeDtypeStruct(before.shape, f32),
        ],
        compiler_params=params(),
        cost_estimate=cost(12 * heads * tokens * AUG * AUG, 12 * heads * HEAD_SIZE * tokens),
        name="query_grads",
    )(query_feat, grad_out, before, local, *after)


def key_kernel(wins, key_ref, value_ref, after_ref, part_ref, *rest):
    grad_key_ref, grad_value_ref = rest[-2:]
    state = after_ref[0]
    for f in range(len(wins) - 1, -1, -1):
        low, high, _, _ = wins[f]
        keep = inside(wins[f])
        state = state + part_ref[0, f]
        feat = jnp.exp(key_ref[:, low:high])
        value = value_ref[:, low:high]
        sums = state[:, HEAD_SIZE : HEAD_SIZE + 1]
        grad_key = (times(prepared(state), value) + sums) * feat
        turn = jnp.concatenate([state, jnp.zeros((AUG - HEAD_SIZE, AUG), f32)], axis=0).T
        grad_value = times(prepared(turn[:HEAD_SIZE]), feat)
        if f == len(wins) - 1:
            grad_key_ref[:, low:high] = grad_key
            grad_value_ref[:, low:high] = grad_value
        else:
            grad_key_ref[:, low:high] = jnp.where(keep, grad_key, grad_key_ref[:, low:high])
            grad_value_ref[:, low:high] = jnp.where(keep, grad_value, grad_value_ref[:, low:high])


def key_grads(key_feat, value_feat, later, part, after):
    tokens = key_feat.shape[1]
    heads, frames = part.shape[:2]
    wins = windows(frames, ROWS * COLS, tokens)
    block = pl.BlockSpec((HEAD_SIZE, tokens), lambda h: (h, 0))
    return pl.pallas_call(
        functools.partial(key_kernel, wins),
        grid=(heads,),
        in_specs=[
            block,
            block,
            pl.BlockSpec((1, HEAD_SIZE, AUG), lambda h: (h, 0, 0)),
            pl.BlockSpec((1, frames, HEAD_SIZE, AUG), lambda h: (h, 0, 0, 0)),
        ]
        + [pl.BlockSpec(memory_space=pl.ANY)] * len(after),
        out_specs=[block, block],
        out_shape=[jax.ShapeDtypeStruct(key_feat.shape, f32)] * 2,
        compiler_params=params(),
        cost_estimate=cost(12 * heads * tokens * AUG * AUG, 16 * heads * HEAD_SIZE * tokens),
        name="key_grads",
    )(key_feat, value_feat, later, part, *after)


def topped_kernel(early_ref, halo_ref, *rest):
    rest[-1][...] = early_ref[...] + halo_ref[...]


def topped(early, halo, after):
    block = pl.BlockSpec((1, *early.shape[1:]), lambda z: (z, 0, 0, 0, 0))
    return pl.pallas_call(
        topped_kernel,
        grid=(early.shape[0],),
        in_specs=[block, block] + [pl.BlockSpec(memory_space=pl.ANY)] * len(after),
        out_specs=block,
        out_shape=jax.ShapeDtypeStruct(early.shape, f32),
        compiler_params=params(),
        cost_estimate=cost(0, 0),
        name="topped",
    )(early, halo, *after)


def place_kernel(chans, early_ref, late_ref, *rest):
    out_ref = rest[-1]
    half = BLOCK // 2
    for first, ref in ((0, early_ref), (2, late_ref)):
        for r in range(half):
            for j in range(ref.shape[0]):
                value = ref[j, r]
                for side in range(2):
                    out_ref[
                        r + side * half, :, first : first + value.shape[1], j * chans : (j + 1) * chans
                    ] = value[:, :, side * chans : (side + 1) * chans]


def placed(early, late, filled, start, steps, chans):
    half = BLOCK // 2
    width = early.shape[2]
    frames = early.shape[3] + late.shape[3]
    total = early.shape[0] * chans

    def spec(a):
        return pl.BlockSpec((a.shape[0], half, *a.shape[2:]), lambda i: (0, i, 0, 0, 0))

    extra = [] if filled is None else [filled]
    return pl.pallas_call(
        functools.partial(place_kernel, chans),
        grid=(steps,),
        in_specs=[spec(early), spec(late)] + [pl.BlockSpec(memory_space=pl.ANY)] * len(extra),
        out_specs=pl.BlockSpec((BLOCK, width, frames, total), lambda i: (start + i, 0, 0, 0)),
        out_shape=jax.ShapeDtypeStruct((ROWS, width, frames, total), f32),
        input_output_aliases={2: 0} if extra else {},
        compiler_params=params(),
        cost_estimate=cost(0, steps * 2400000),
        name="placed",
    )(early, late, *extra)


def body(query_feat, key_feat, value_feat, grad_out, spatial_weight, temporal_weight):
    chans, tokens = query_feat.shape
    frames = tokens // (ROWS * COLS)
    heads = chans // HEAD_SIZE
    head_devs = lax.axis_size("head")
    segs = lax.axis_size("seg")
    local, totals = local_states(key_feat, value_feat, frames, heads)
    feat = turned(query_feat)
    parts = entering(totals, False, [feat])

    def sent(a):
        return lax.all_to_all(a, "head", split_axis=0, concat_axis=0, tiled=True)

    spans = [(0, 1), (1, ROWS // BLOCK - 1)]
    late, early, halo = [], [], []
    after = []
    for start, steps in spans:
        a, b, c = forward(parts, local, (spatial_weight, temporal_weight), feat, start, steps, head_devs, after)
        late.append(sent(a))
        early.append(b)
        halo.append(c)
        after = [c]
    pairs = [(i, i + 1) for i in range(segs - 1)]
    moved = [lax.ppermute(c, "seg", pairs) for c in halo]

    before = whole_state(parts, False)
    grad_query, part, back = query_grads(query_feat, grad_out, before, local, [late[0], halo[-1]])
    later = whole_state(entering(back, True, []), True)
    grad_key, grad_value = key_grads(key_feat, value_feat, later, part, [])

    last = sent(topped(early[1], moved[1], [grad_key]))
    first = sent(topped(early[0], moved[0], [late[1]]))
    mixed = placed(last, late[1], None, *spans[1], chans)
    mixed = placed(first, late[0], mixed, *spans[0], chans)
    return grad_query, grad_key, grad_value, jnp.transpose(mixed, (2, 0, 1, 3))


def solution(mesh):
    in_specs = (P("head", "seg"), P("head", "seg"), P("head", "seg"), P("head", "seg"), P(), P())
    out_specs = (P("head", "seg"), P("head", "seg"), P("head", "seg"), P("seg", None, "head", None))
    return jax.shard_map(body, mesh=mesh, in_specs=in_specs, out_specs=out_specs, check_vma=False)
```

profile of v0, /device:TPU:0, one launch (start us, length us, event | category | flops | bytes accessed | tf_op | source)
XLA Modules:
  0.0 202.5 jit_solution(14041008299034205403)
XLA Ops:
  0.6 7.2 %local_states.1 = (f32[4,4,112,128]{3,2,1,0:T(8,128)}, f32[4,112,128]{2,1,0:T(8,128)}) custom-call(f32[448,3200]{1,0:T(8,128)} %key_ref.3, f32[448,3200]{1,0:T(8,128)} %value_ref.3), custom_call_target="tpu_custom_call" | custom-call | flops 1 | bytes 1 | tf_op jit(solution)/shard_map/local_states/pallas_call | solution.py:99
  10.7 3.9 %collective-permute-start.3 = (f32[2,112,128]{2,1,0:T(8,128)S(1)}, f32[2,112,128]{2,1,0:T(8,128)S(1)}, u32[]{:S(2)}, u32[]{:S(2)}) collective-permute-start(f32[2,112,128]{2,1,0:T(8,128)S(1)} %fusion.3), channel_id=1, source_target_pairs={{0,24},{4,28},{8,16},{12,20},{16,8},{20,12},{24,0},{28,4},{1,25},{... | collective-permute-start | bytes 344072 | tf_op jit(solution)/shard_map/ppermute | solution.py:119
  15.2 7.8 %turned.1.refs_3_ = f32[3200,448]{1,0:T(8,128)} custom-call(f32[448,3200]{1,0:T(8,128)} %query_ref.3), custom_call_target="tpu_custom_call" | custom-call | flops 1 | bytes 1 | tf_op jit(solution)/shard_map/turned/pallas_call | solution.py:173
  24.4 1.7 joined.2.part_ref
  28.3 7.3 %forward_rows.2 = (f32[4,2,10,2,896]{4,3,2,1,0:T(2,128)}, f32[4,2,10,2,896]{4,3,2,1,0:T(2,128)}, f32[4,2,10,2,896]{4,3,2,1,0:T(2,128)}) custom-call(f32[2,112,128]{2,1,0:T(8,128)} %joined.2.part_ref, f32[2,112,128]{2,1,0:T(8,128)} %copy-done.6, f32[4,112,128]{2,1,0:T(8,128)} %copy-done.2, f32[4,4,112,128]{3,2,1,0:T(8,128)} %get-tuple-element.18.local_ref, ...), custom_call_target="tpu_custom_call" | custom-call | flops 1 | bytes 1 | tf_op jit(solution)/shard_map/forward_rows/pallas_call | solution.py:304
  35.5 5.3 %all-to-all-start = ((f32[4,2,10,2,896]{4,3,2,1,0:T(2,128)}), f32[4,2,10,2,896]{4,3,2,1,0:T(2,128)S(1)}, u32[]{:S(2)}, u32[]{:S(2)}) async-start(f32[4,2,10,2,896]{4,3,2,1,0:T(2,128)} %get-tuple-element.19), calls=%async_computation | async-start | bytes 1146880 | tf_op jit(solution)/shard_map/all_to_all | solution.py:495
  40.9 19.6 %forward_rows.3 = (f32[4,8,10,2,896]{4,3,2,1,0:T(2,128)}, f32[4,8,10,2,896]{4,3,2,1,0:T(2,128)}, f32[4,8,10,2,896]{4,3,2,1,0:T(2,128)}) custom-call(f32[2,112,128]{2,1,0:T(8,128)} %joined.2.part_ref, f32[2,112,128]{2,1,0:T(8,128)} %copy-done.6, f32[4,112,128]{2,1,0:T(8,128)} %copy-done.2, f32[4,4,112,128]{3,2,1,0:T(8,128)} %get-tuple-element.18.local_ref, ...), custom_call_target="tpu_custom_call" | custom-call | flops 1 | bytes 1 | tf_op jit(solution)/shard_map/forward_rows/pallas_call | solution.py:304
  60.5 5.1 %all-to-all-start.1 = ((f32[4,8,10,2,896]{4,3,2,1,0:T(2,128)}), f32[4,8,10,2,896]{4,3,2,1,0:T(2,128)S(1)}, u32[]{:S(2)}, u32[]{:S(2)}) async-start(f32[4,8,10,2,896]{4,3,2,1,0:T(2,128)} %get-tuple-element.28), calls=%async_computation.1 | async-start | bytes 4587520 | tf_op jit(solution)/shard_map/all_to_all | solution.py:495
  65.6 2.7 %collective-permute-start.11 = (f32[4,8,10,2,896]{4,3,2,1,0:T(2,128)}, f32[4,8,10,2,896]{4,3,2,1,0:T(2,128)}, u32[]{:S(2)}, u32[]{:S(2)}) collective-permute-start(f32[4,8,10,2,896]{4,3,2,1,0:T(2,128)} %get-tuple-element.21.rest_1_), channel_id=1, source_target_pairs={{0,4},{4,8},{8,12},{12,16},{16,20},{20,24},{24,28},{1,5},{5,9},{9,... | collective-permute-start | bytes 6881288 | tf_op jit(solution)/shard_map/ppermute | solution.py:507
  69.0 9.8 %query_grads.1 = (f32[448,3200]{1,0:T(8,128)}, f32[4,4,112,128]{3,2,1,0:T(8,128)}, f32[4,112,128]{2,1,0:T(8,128)}) custom-call(f32[448,3200]{1,0:T(8,128)} %query_ref.3, f32[448,3200]{1,0:T(8,128)} %grad_ref.1, f32[4,112,128]{2,1,0:T(8,128)} %fusion.before_ref, f32[4,4,112,128]{3,2,1,0:T(8,128)} %get-tuple-element.18.local_ref, ...), custom_call_target="tpu_custom_call" | custom-call | flops 1 | bytes 1 | tf_op jit(solution)/shard_map/query_grads/pallas_call | solution.py:370
  83.4 1.7 collective-permute-start.7
  85.7 3.4 %collective-permute-done.8.refs_2_ = f32[2,112,128]{2,1,0:T(8,128)S(1)} collective-permute-done((f32[2,112,128]{2,1,0:T(8,128)S(1)}, f32[2,112,128]{2,1,0:T(8,128)S(1)}, u32[]{:S(2)}, u32[]{:S(2)}) %collective-permute-start.8) | collective-permute-done | bytes 114720 | tf_op jit(solution)/shard_map/ppermute | solution.py:119
  89.2 11.0 %collective-permute-done.7.refs_1_ = f32[2,112,128]{2,1,0:T(8,128)S(1)} collective-permute-done((f32[2,112,128]{2,1,0:T(8,128)S(1)}, f32[2,112,128]{2,1,0:T(8,128)S(1)}, u32[]{:S(2)}, u32[]{:S(2)}) %collective-permute-start.7) | collective-permute-done | bytes 114720 | tf_op jit(solution)/shard_map/ppermute | solution.py:119
  104.6 1.7 fusion.1.after_ref
  106.3 10.4 %key_grads.1 = (f32[448,3200]{1,0:T(8,128)}, f32[448,3200]{1,0:T(8,128)}) custom-call(f32[448,3200]{1,0:T(8,128)} %key_ref.3, f32[448,3200]{1,0:T(8,128)} %value_ref.3, f32[4,112,128]{2,1,0:T(8,128)} %fusion.1.after_ref, f32[4,4,112,128]{3,2,1,0:T(8,128)} %get-tuple-element.24.part_ref), custom_call_target="tpu_custom_call" | custom-call | flops 1 | bytes 1 | tf_op jit(solution)/shard_map/key_grads/pallas_call | solution.py:412
  116.8 4.4 %topped.3 = f32[4,8,10,2,896]{4,3,2,1,0:T(2,128)} custom-call(f32[4,8,10,2,896]{4,3,2,1,0:T(2,128)} %get-tuple-element.29.early_ref, f32[4,8,10,2,896]{4,3,2,1,0:T(2,128)} %collective-permute-done.11.halo_ref, f32[448,3200]{1,0:T(8,128)} %get-tuple-element.14.rest_0_), custom_call_target="tpu_custom_call" | custom-call | flops 1 | bytes 1 | tf_op jit(solution)/shard_map/topped/pallas_call | solution.py:436
  121.2 5.1 %all-to-all-start.3 = ((f32[4,8,10,2,896]{4,3,2,1,0:T(2,128)}), f32[4,8,10,2,896]{4,3,2,1,0:T(2,128)}, u32[]{:S(2)}, u32[]{:S(2)}) async-start(f32[4,8,10,2,896]{4,3,2,1,0:T(2,128)} %topped.3), calls=%async_computation.3 | async-start | bytes 4587520 | tf_op jit(solution)/shard_map/all_to_all | solution.py:495
  126.3 1.9 collective-permute-start.10
  130.5 3.3 %topped.2 = f32[4,2,10,2,896]{4,3,2,1,0:T(2,128)} custom-call(f32[4,2,10,2,896]{4,3,2,1,0:T(2,128)} %get-tuple-element.27.early_ref, f32[4,2,10,2,896]{4,3,2,1,0:T(2,128)} %copy-done.8, f32[4,8,10,2,896]{4,3,2,1,0:T(2,128)} %copy-done), custom_call_target="tpu_custom_call" | custom-call | flops 1 | bytes 1 | tf_op jit(solution)/shard_map/topped/pallas_call | solution.py:436
  133.9 45.6 %all-to-all-done.3.early_ref = f32[4,8,10,2,896]{4,3,2,1,0:T(2,128)} async-done(((f32[4,8,10,2,896]{4,3,2,1,0:T(2,128)}), f32[4,8,10,2,896]{4,3,2,1,0:T(2,128)}, u32[]{:S(2)}, u32[]{:S(2)}) %all-to-all-start.3) | async-done | bytes 2293792 | tf_op jit(solution)/shard_map/all_to_all | solution.py:495
  179.4 3.5 %all-to-all-start.2 = ((f32[4,2,10,2,896]{4,3,2,1,0:T(2,128)}), f32[4,2,10,2,896]{4,3,2,1,0:T(2,128)S(1)}, u32[]{:S(2)}, u32[]{:S(2)}) async-start(f32[4,2,10,2,896]{4,3,2,1,0:T(2,128)} %topped.2), calls=%async_computation.2 | async-start | bytes 1146880 | tf_op jit(solution)/shard_map/all_to_all | solution.py:495
  182.9 7.4 %placed.2.rest_0_ = f32[20,10,4,1792]{3,2,1,0:T(4,128)} custom-call(f32[4,8,10,2,896]{4,3,2,1,0:T(2,128)} %all-to-all-done.3.early_ref, f32[4,8,10,2,896]{4,3,2,1,0:T(2,128)} %copy-done), custom_call_target="tpu_custom_call" | custom-call | flops 1 | bytes 1 | tf_op jit(solution)/shard_map/placed/pallas_call | solution.py:471
  190.3 8.0 %all-to-all-done.2.early_ref = f32[4,2,10,2,896]{4,3,2,1,0:T(2,128)S(1)} async-done(((f32[4,2,10,2,896]{4,3,2,1,0:T(2,128)}), f32[4,2,10,2,896]{4,3,2,1,0:T(2,128)S(1)}, u32[]{:S(2)}, u32[]{:S(2)}) %all-to-all-start.2) | async-done | bytes 573472 | tf_op jit(solution)/shard_map/all_to_all | solution.py:495
  199.1 3.3 %placed.3 = f32[20,10,4,1792]{3,2,1,0:T(4,128)} custom-call(f32[4,2,10,2,896]{4,3,2,1,0:T(2,128)} %copy-done.4, f32[4,2,10,2,896]{4,3,2,1,0:T(2,128)} %copy-done.1, f32[20,10,4,1792]{3,2,1,0:T(4,128)} %placed.2.rest_0_), custom_call_target="tpu_custom_call", output_to_operand_aliasing={{}: (2, {})} | custom-call | flops 1 | bytes 1 | tf_op jit(solution)/shard_map/placed/pallas_call | solution.py:471
  (56 shorter events, 20.6 us)
Async XLA Ops:
  7.8 1.8 collective-permute-start
  9.6 13.4 %copy-start.2 = (f32[4,112,128]{2,1,0:T(8,128)}, f32[4,112,128]{2,1,0:T(8,128)S(1)}, u32[]{:S(2)}) copy-start(f32[4,112,128]{2,1,0:T(8,128)S(1)} %collective-permute-done.mate_ref) | copy-start | bytes 688132
  10.7 12.4 %collective-permute-start.3 = (f32[2,112,128]{2,1,0:T(8,128)S(1)}, f32[2,112,128]{2,1,0:T(8,128)S(1)}, u32[]{:S(2)}, u32[]{:S(2)}) collective-permute-start(f32[2,112,128]{2,1,0:T(8,128)S(1)} %fusion.3), channel_id=1, source_target_pairs={{0,24},{4,28},{8,16},{12,20},{16,8},{20,12},{24,0},{28,4},{1,25},{... | collective-permute-start | bytes 344072 | tf_op jit(solution)/shard_map/ppermute | solution.py:119
  14.6 8.5 %collective-permute-start.2 = (f32[2,112,128]{2,1,0:T(8,128)S(1)}, f32[2,112,128]{2,1,0:T(8,128)S(1)}, u32[]{:S(2)}, u32[]{:S(2)}) collective-permute-start(f32[2,112,128]{2,1,0:T(8,128)S(1)} %fusion.3), channel_id=1, source_target_pairs={{0,16},{4,20},{8,24},{12,28},{16,0},{20,4},{24,8},{28,12},{1,17},{... | collective-permute-start | bytes 344072 | tf_op jit(solution)/shard_map/ppermute | solution.py:119
  15.1 8.0 %collective-permute-start.1 = (f32[2,112,128]{2,1,0:T(8,128)S(1)}, f32[2,112,128]{2,1,0:T(8,128)S(1)}, u32[]{:S(2)}, u32[]{:S(2)}) collective-permute-start(f32[2,112,128]{2,1,0:T(8,128)S(1)} %fusion.3), channel_id=1, source_target_pairs={{0,8},{4,12},{8,0},{12,4},{16,24},{20,28},{24,16},{28,20},{1,9},{5... | collective-permute-start | bytes 344072 | tf_op jit(solution)/shard_map/ppermute | solution.py:119
  26.1 1.5 collective-permute-start.4
  35.5 24.9 %all-to-all-start = ((f32[4,2,10,2,896]{4,3,2,1,0:T(2,128)}), f32[4,2,10,2,896]{4,3,2,1,0:T(2,128)S(1)}, u32[]{:S(2)}, u32[]{:S(2)}) async-start(f32[4,2,10,2,896]{4,3,2,1,0:T(2,128)} %get-tuple-element.19), calls=%async_computation | async-start | bytes 1146880 | tf_op jit(solution)/shard_map/all_to_all | solution.py:495
  40.9 27.4 %copy-start.3 = (f32[4,112,128]{2,1,0:T(8,128)S(1)}, f32[4,112,128]{2,1,0:T(8,128)}, u32[]{:S(2)}) copy-start(f32[4,112,128]{2,1,0:T(8,128)} %copy-done.2) | copy-start | bytes 688132
  40.9 27.4 %copy-start.5 = (f32[2,112,128]{2,1,0:T(8,128)S(1)}, f32[2,112,128]{2,1,0:T(8,128)}, u32[]{:S(2)}) copy-start(f32[2,112,128]{2,1,0:T(8,128)} %joined.2.part_ref) | copy-start | bytes 344068
  40.9 27.4 %copy-start.7 = (f32[2,112,128]{2,1,0:T(8,128)S(1)}, f32[2,112,128]{2,1,0:T(8,128)}, u32[]{:S(2)}) copy-start(f32[2,112,128]{2,1,0:T(8,128)} %copy-done.6) | copy-start | bytes 344068
  60.5 8.6 %copy-start.1 = (f32[4,2,10,2,896]{4,3,2,1,0:T(2,128)}, f32[4,2,10,2,896]{4,3,2,1,0:T(2,128)S(1)}, u32[]{:S(2)}) copy-start(f32[4,2,10,2,896]{4,3,2,1,0:T(2,128)S(1)} %all-to-all-done.rest_0_.late_ref) | copy-start | bytes 1720324
  60.5 60.7 %all-to-all-start.1 = ((f32[4,8,10,2,896]{4,3,2,1,0:T(2,128)}), f32[4,8,10,2,896]{4,3,2,1,0:T(2,128)S(1)}, u32[]{:S(2)}, u32[]{:S(2)}) async-start(f32[4,8,10,2,896]{4,3,2,1,0:T(2,128)} %get-tuple-element.28), calls=%async_computation.1 | async-start | bytes 4587520 | tf_op jit(solution)/shard_map/all_to_all | solution.py:495
  65.6 51.2 %collective-permute-start.11 = (f32[4,8,10,2,896]{4,3,2,1,0:T(2,128)}, f32[4,8,10,2,896]{4,3,2,1,0:T(2,128)}, u32[]{:S(2)}, u32[]{:S(2)}) collective-permute-start(f32[4,8,10,2,896]{4,3,2,1,0:T(2,128)} %get-tuple-element.21.rest_1_), channel_id=1, source_target_pairs={{0,4},{4,8},{8,12},{12,16},{16,20},{20,24},{24,28},{1,5},{5,9},{9,... | collective-permute-start | bytes 6881288 | tf_op jit(solution)/shard_map/ppermute | solution.py:507
  78.8 2.4 %collective-permute-start.5 = (f32[4,112,128]{2,1,0:T(8,128)}, f32[4,112,128]{2,1,0:T(8,128)S(1)}, u32[]{:S(2)}, u32[]{:S(2)}) collective-permute-start(f32[4,112,128]{2,1,0:T(8,128)} %get-tuple-element.23), channel_id=1, source_target_pairs={{0,4},{4,0},{8,12},{12,8},{16,20},{20,16},{24,28},{28,24},{1,5},{5... | collective-permute-start | bytes 688136 | tf_op jit(solution)/shard_map/ppermute | solution.py:119
  82.2 7.0 %collective-permute-start.8 = (f32[2,112,128]{2,1,0:T(8,128)S(1)}, f32[2,112,128]{2,1,0:T(8,128)S(1)}, u32[]{:S(2)}, u32[]{:S(2)}) collective-permute-start(f32[2,112,128]{2,1,0:T(8,128)S(1)} %fusion.2), channel_id=1, source_target_pairs={{0,24},{4,28},{8,16},{12,20},{16,8},{20,12},{24,0},{28,4},{1,25},{... | collective-permute-start | bytes 344072 | tf_op jit(solution)/shard_map/ppermute | solution.py:119
  83.4 16.7 %collective-permute-start.7 = (f32[2,112,128]{2,1,0:T(8,128)S(1)}, f32[2,112,128]{2,1,0:T(8,128)S(1)}, u32[]{:S(2)}, u32[]{:S(2)}) collective-permute-start(f32[2,112,128]{2,1,0:T(8,128)S(1)} %fusion.2), channel_id=1, source_target_pairs={{0,16},{4,20},{8,24},{12,28},{16,0},{20,4},{24,8},{28,12},{1,17},{... | collective-permute-start | bytes 344072 | tf_op jit(solution)/shard_map/ppermute | solution.py:119
  85.2 14.9 %collective-permute-start.6 = (f32[2,112,128]{2,1,0:T(8,128)S(1)}, f32[2,112,128]{2,1,0:T(8,128)S(1)}, u32[]{:S(2)}, u32[]{:S(2)}) collective-permute-start(f32[2,112,128]{2,1,0:T(8,128)S(1)} %fusion.2), channel_id=1, source_target_pairs={{0,8},{4,12},{8,0},{12,4},{16,24},{20,28},{24,16},{28,20},{1,9},{5... | collective-permute-start | bytes 344072 | tf_op jit(solution)/shard_map/ppermute | solution.py:119
  89.1 11.0 %copy-start.10 = (f32[2,112,128]{2,1,0:T(8,128)}, f32[2,112,128]{2,1,0:T(8,128)S(1)}, u32[]{:S(2)}) copy-start(f32[2,112,128]{2,1,0:T(8,128)S(1)} %collective-permute-done.8.refs_2_) | copy-start | bytes 344068
  103.1 1.5 collective-permute-start.9
  116.8 9.5 %copy-start.9 = (f32[4,2,10,2,896]{4,3,2,1,0:T(2,128)S(1)}, f32[4,2,10,2,896]{4,3,2,1,0:T(2,128)}, u32[]{:S(2)}) copy-start(f32[4,2,10,2,896]{4,3,2,1,0:T(2,128)} %get-tuple-element.20.rest_0_) | copy-start | bytes 1720324
  121.2 8.6 %copy-start = (f32[4,8,10,2,896]{4,3,2,1,0:T(2,128)}, f32[4,8,10,2,896]{4,3,2,1,0:T(2,128)S(1)}, u32[]{:S(2)}) copy-start(f32[4,8,10,2,896]{4,3,2,1,0:T(2,128)S(1)} %all-to-all-done.1.rest_0_.late_ref) | copy-start | bytes 6881284
  121.2 58.3 %all-to-all-start.3 = ((f32[4,8,10,2,896]{4,3,2,1,0:T(2,128)}), f32[4,8,10,2,896]{4,3,2,1,0:T(2,128)}, u32[]{:S(2)}, u32[]{:S(2)}) async-start(f32[4,8,10,2,896]{4,3,2,1,0:T(2,128)} %topped.3), calls=%async_computation.3 | async-start | bytes 4587520 | tf_op jit(solution)/shard_map/all_to_all | solution.py:495
  126.3 3.5 %collective-permute-start.10 = (f32[4,2,10,2,896]{4,3,2,1,0:T(2,128)S(1)}, f32[4,2,10,2,896]{4,3,2,1,0:T(2,128)S(1)}, u32[]{:S(2)}, u32[]{:S(2)}) collective-permute-start(f32[4,2,10,2,896]{4,3,2,1,0:T(2,128)S(1)} %copy-done.9), channel_id=1, source_target_pairs={{0,4},{4,8},{8,12},{12,16},{16,20},{20,24},{24,28},{1,5},{5,9},{9,... | collective-permute-start | bytes 1720328 | tf_op jit(solution)/shard_map/ppermute | solution.py:507
  179.4 18.8 %all-to-all-start.2 = ((f32[4,2,10,2,896]{4,3,2,1,0:T(2,128)}), f32[4,2,10,2,896]{4,3,2,1,0:T(2,128)S(1)}, u32[]{:S(2)}, u32[]{:S(2)}) async-start(f32[4,2,10,2,896]{4,3,2,1,0:T(2,128)} %topped.2), calls=%async_computation.2 | async-start | bytes 1146880 | tf_op jit(solution)/shard_map/all_to_all | solution.py:495
  (8 other events, 5.5 us)
where the time goes:
time: 204 us; the launch traced here: 202 us
  Pallas kernels  83.9 us (41%)
  waiting for transfers between devices  75 us (37%)
  starting transfers between devices  33.5 us (16%)
  local copies, waits for them, and re-layouts  4.88 us (2%)
  other arithmetic  4.47 us (2%)
    all_to_all x4, waiting for transfers between devices, sent(): return lax.all_to_all(a, 'head', split_axis=0, concat_axis=0, tiled=True)  53.5 us
    pallas_call x2, Pallas kernels, forward(): pl.pallas_call(functools.partial(forward_kernel, start, frames, heads, he...  26.9 us
    ppermute x10, waiting for transfers between devices, xor_move(): return lax.ppermute(array, axis, [(i, i ^ by) for i in range(count)])  19.9 us
    all_to_all x4, starting transfers between devices, sent(): return lax.all_to_all(a, 'head', split_axis=0, concat_axis=0, tiled=True)  19.1 us
    pallas_call x2, Pallas kernels, placed(): pl.pallas_call(functools.partial(place_kernel, chans), grid=(steps,), in_...  10.7 us
    pallas_call x1, Pallas kernels, key_grads(): pl.pallas_call(functools.partial(key_kernel, wins), grid=(heads,), in_spe...  10.4 us
    ppermute x10, starting transfers between devices, xor_move(): return lax.ppermute(array, axis, [(i, i ^ by) for i in range(count)])  9.83 us
    pallas_call x1, Pallas kernels, query_grads(): pl.pallas_call(functools.partial(query_kernel, wins), grid=(heads,), in_s...  9.79 us
  transfers between devices with their start and end apart: 16, of which 9 were waited for; matrix products, arithmetic and copies ran while one was open for 2% of the time, Pallas kernels for 32%

commit v1 on v0

--- a/solution.py
+++ b/solution.py
@@ -13,7 +13,6 @@
 LANES = 128
 AUG = -(-(HEAD_SIZE + 1) // LANES) * LANES
 BLOCK = 4
-VMEM = 56 * 1024 * 1024
 
 f32 = jnp.float32
 bf16 = jnp.bfloat16
@@ -69,47 +68,73 @@
     return (lane >= first) & (lane < last)
 
 
+def in_hbm(shape):
+    return pltpu.HBM(shape, f32)
+
+
 def cost(flops, data):
     return pl.CostEstimate(flops=1, bytes_accessed=1, transcendentals=0)
 
 
-def params(count=1):
+def params(mib):
     return pltpu.CompilerParams(
-        dimension_semantics=("arbitrary",) * count, vmem_limit_bytes=VMEM
+        dimension_semantics=("arbitrary",), vmem_limit_bytes=mib * 1024 * 1024
     )
 
 
-def states_kernel(wins, key_ref, value_ref, local_ref, total_ref):
-    total = jnp.zeros((HEAD_SIZE, AUG), f32)
-    for f, win in enumerate(wins):
-        low, high, _, _ = win
-        feat = jnp.where(inside(win), jnp.exp(key_ref[:, low:high]), 0.0)
-        ones = jnp.ones((AUG - HEAD_SIZE, high - low), f32)
-        value = jnp.concatenate([value_ref[:, low:high], ones], axis=0)
-        part = over_tokens(feat, value)
-        local_ref[0, f] = part
-        total = total + part
-    total_ref[0] = total
+def states_kernel(wins, heads, key_any, value_any, local_ref, total_ref, key_buf, value_buf, sems):
+    middle = wins[(len(wins) - 1) // 2][1]
+    halves = (slice(0, middle), slice(middle, wins[-1][1]))
+
+    def copies(h, half):
+        at = pl.ds(h * HEAD_SIZE, HEAD_SIZE)
+        pairs = ((key_any, key_buf), (value_any, value_buf))
+        return [
+            pltpu.make_async_copy(
+                src.at[at, halves[half]], dst.at[h, :, halves[half]], sems.at[i, half, h]
+            )
+            for i, (src, dst) in enumerate(pairs)
+        ]
+
+    halved = 2 if middle < wins[-1][1] else 1
+    for h in range(heads):
+        for half in range(halved):
+            for copy in copies(h, half):
+                copy.start()
+    for h in range(heads):
+        total = jnp.zeros((HEAD_SIZE, AUG), f32)
+        for f, win in enumerate(wins):
+            for half in range(halved):
+                if f == (0, (len(wins) - 1) // 2 + 1)[half]:
+                    for copy in copies(h, half):
+                        copy.wait()
+            low, high, _, _ = win
+            feat = jnp.where(inside(win), jnp.exp(key_buf[h, :, low:high]), 0.0)
+            ones = jnp.ones((AUG - HEAD_SIZE, high - low), f32)
+            value = jnp.concatenate([value_buf[h, :, low:high], ones], axis=0)
+            part = over_tokens(feat, value)
+            local_ref[h, f] = part
+            total = total + part
+        total_ref[h] = total
 
 
 def local_states(key_feat, value_feat, frames, heads):
     tokens = key_feat.shape[1]
     wins = windows(frames, ROWS * COLS, tokens)
-    block = pl.BlockSpec((HEAD_SIZE, tokens), lambda h: (h, 0))
-    return pl.pallas_call(
-        functools.partial(states_kernel, wins),
-        grid=(heads,),
-        in_specs=[block, block],
-        out_specs=[
-            pl.BlockSpec((1, frames, HEAD_SIZE, AUG), lambda h: (h, 0, 0, 0)),
-            pl.BlockSpec((1, HEAD_SIZE, AUG), lambda h: (h, 0, 0)),
-        ],
+    return pl.pallas_call(
+        functools.partial(states_kernel, wins, heads),
+        in_specs=[pl.BlockSpec(memory_space=pltpu.HBM)] * 2,
         out_shape=[
             jax.ShapeDtypeStruct((heads, frames, HEAD_SIZE, AUG), f32),
             jax.ShapeDtypeStruct((heads, HEAD_SIZE, AUG), f32),
         ],
-        compiler_params=params(),
-        cost_estimate=cost(6 * heads * tokens * AUG * AUG, 8 * heads * HEAD_SIZE * tokens),
+        scratch_shapes=[
+            pltpu.VMEM((heads, HEAD_SIZE, tokens), f32),
+            pltpu.VMEM((heads, HEAD_SIZE, tokens), f32),
+            pltpu.SemaphoreType.DMA((2, 2, heads)),
+        ],
+        compiler_params=pltpu.CompilerParams(vmem_limit_bytes=56 * 1024 * 1024),
+        cost_estimate=cost(0, 0),
         name="local_states",
     )(key_feat, value_feat)
 
@@ -134,9 +159,10 @@
     block = pl.BlockSpec(one.shape, lambda: (0,) * one.ndim)
     return pl.pallas_call(
         functools.partial(joined_kernel, reverse, steps),
-        in_specs=[block] * len(blocks) + [pl.BlockSpec(memory_space=pl.ANY)] * len(after),
+        in_specs=[block] * len(blocks) + [pl.BlockSpec(memory_space=pltpu.HBM)] * len(after),
         out_specs=block,
         out_shape=jax.ShapeDtypeStruct(one.shape, f32),
+        compiler_params=pltpu.CompilerParams(vmem_limit_bytes=8 * 1024 * 1024),
         name="joined",
     )(*blocks, *after)
 
@@ -164,20 +190,27 @@
 
 
 def turn_kernel(query_ref, out_ref):
-    out_ref[...] = jnp.exp(query_ref[...]).T
+    chans = query_ref.shape[0]
+    out_ref[:, :chans] = jnp.exp(query_ref[...]).T
+    out_ref[:, chans:] = jnp.zeros((out_ref.shape[0], out_ref.shape[1] - chans), f32)
+
+
+def padded(chans):
+    return -(-(chans + chans // HEAD_SIZE) // LANES) * LANES
 
 
 def turned(query_feat):
     chans, tokens = query_feat.shape
+    wide = padded(chans)
     step = 640 if tokens % 640 == 0 else tokens
     return pl.pallas_call(
         turn_kernel,
         grid=(tokens // step,),
         in_specs=[pl.BlockSpec((chans, step), lambda i: (0, i))],
-        out_specs=pl.BlockSpec((step, chans), lambda i: (i, 0)),
-        out_shape=jax.ShapeDtypeStruct((tokens, chans), f32),
-        compiler_params=params(),
-        cost_estimate=cost(0, 8 * chans * tokens),
+        out_specs=pl.BlockSpec((step, wide), lambda i: (i, 0)),
+        out_shape=jax.ShapeDtypeStruct((tokens, wide), f32),
+        compiler_params=params(24),
+        cost_estimate=cost(0, 0),
         name="turned",
     )(query_feat)
 
@@ -186,11 +219,10 @@
     start, frames, heads, head_devs, part_ref, other_ref, mate_ref, local_ref, spatial_ref,
     temporal_ref, prev_ref, cur_ref, next_ref, *rest
 ):
-    late_ref, early_ref, halo_ref, bd_high, bd_low, weight_ref = rest[-6:]
+    late_ref, early_ref, halo_ref, mix_ref, weight_ref, att_ref = rest[-6:]
     chans = heads * HEAD_SIZE
-    wide = bd_high.shape[2]
+    wide = weight_ref.shape[1]
     width = COLS // head_devs
-    half = BLOCK // 2
     step = pl.program_id(0)
 
     @pl.when(step == 0)
@@ -207,6 +239,10 @@
                     weight_ref[3 * r : 3 * r + 3, :chans] = spatial_ref[r, :, at]
                 weight_ref[9:12, :chans] = temporal_ref[:, at]
 
+        for f in range(frames):
+            for k in range(3):
+                spare = pl.ds(k * wide + chans, wide - chans)
+                mix_ref[f, spare, :] = jnp.zeros((wide - chans, wide), bf16)
         lane = lax.broadcasted_iota(jnp.int32, (HEAD_SIZE, LANES), 1)
         last = wide // LANES - 1
         for h in range(heads):
@@ -217,7 +253,7 @@
             state = jnp.where(odd, second[g] + mate_ref[h], first[g])
             tile, shift = divmod(h * HEAD_SIZE, LANES)
             over = shift + HEAD_SIZE - LANES
-            at = pl.ds(h * HEAD_SIZE, HEAD_SIZE)
+            at = [pl.ds(k * wide + h * HEAD_SIZE, HEAD_SIZE) for k in range(3)]
             for f in range(frames):
                 state = state + local_ref[h, f]
                 moved = pltpu.roll(state, shift, 1) if shift else state
@@ -233,74 +269,80 @@
                         value = jnp.where(lane == chans - last * LANES + h, sums, value)
                     span = slice(t * LANES, (t + 1) * LANES)
                     if value is None:
-                        bd_high[f, at, span] = jnp.zeros((HEAD_SIZE, LANES), bf16)
-                        bd_low[f, at, span] = jnp.zeros((HEAD_SIZE, LANES), bf16)
+                        high = low = jnp.zeros((HEAD_SIZE, LANES), bf16)
                     else:
-                        bd_high[f, at, span], bd_low[f, at, span] = split(value)
+                        high, low = split(value)
+                    mix_ref[f, at[0], span] = low
+                    mix_ref[f, at[1], span] = high
+                    mix_ref[f, at[2], span] = high
 
     block = start + step
     top = jnp.where(block == 0, 0.0, 1.0)
     bottom = jnp.where(block == ROWS // BLOCK - 1, 0.0, 1.0)
     count = (BLOCK + 2) * COLS
-    mids = BLOCK * COLS
-    column = lax.broadcasted_iota(jnp.int32, (count, 1), 0) % COLS
-    head_of = lax.broadcasted_iota(jnp.int32, (1, wide), 1) // HEAD_SIZE
-
-    def active(f):
-        feat = jnp.concatenate([prev_ref[f], cur_ref[f], next_ref[f]], axis=0)
-        high, low = split(feat)
-        numer = dot(high, bd_low[f], ((1,), (0,))) + dot(low, bd_high[f], ((1,), (0,)))
-        numer = numer + dot(high, bd_high[f], ((1,), (0,)))
+    lane = lax.broadcasted_iota(jnp.int32, (1, LANES), 1)
+    for f in range(frames):
+        high, low = split(jnp.concatenate([prev_ref[f], cur_ref[f], next_ref[f]], axis=0))
+        pieces = jnp.concatenate([high, low, high], axis=1)
+        numer = dot(pieces, mix_ref[f], ((1,), (0,)))
         inverse = 1.0 / numer[:, chans : chans + heads]
-        scale = inverse[:, heads - 1 : heads]
-        for h in range(heads - 2, -1, -1):
-            scale = jnp.where(head_of <= h, inverse[:, h : h + 1], scale)
-        att = numer * scale
-        att = jnp.concatenate([att[:COLS] * top, att[COLS:-COLS], att[-COLS:] * bottom], axis=0)
-        left = jnp.where(column == 0, 0.0, pltpu.roll(att, 1, 0))
-        right = jnp.where(column == COLS - 1, 0.0, pltpu.roll(att, count - 1, 0))
-        total = jnp.zeros((mids, wide), f32)
-        for r in range(3):
-            for c, side in enumerate((left, att, right)):
-                total = total + weight_ref[3 * r + c : 3 * r + c + 1, :] * side[r * COLS : r * COLS + mids]
-        return total / (1.0 + jnp.exp(-total))
-
-    taps = [weight_ref[9 + i : 10 + i, :] for i in range(3)]
-    acts = [active(f) for f in range(frames)]
-
-    def put(ref, k, value):
-        for z in range(head_devs):
-            for r in range(BLOCK):
-                rows = value[r * COLS + z * width : r * COLS + (z + 1) * width, :chans]
-                ref[z, r % half, :, k, (r // half) * chans : (r // half + 1) * chans] = rows
-
-    for f in range(2, frames):
-        put(late_ref, f - 2, taps[0] * acts[f] + taps[1] * acts[f - 1] + taps[2] * acts[f - 2])
-    put(early_ref, 0, taps[0] * acts[0])
-    put(early_ref, 1, taps[0] * acts[1] + taps[1] * acts[0])
-    put(halo_ref, 0, taps[1] * acts[-1] + taps[2] * acts[-2])
-    put(halo_ref, 1, taps[2] * acts[-1])
+        for t in range(wide // LANES):
+            first = t * LANES // HEAD_SIZE
+            final = min(((t + 1) * LANES - 1) // HEAD_SIZE, heads - 1)
+            scale = inverse[:, final : final + 1]
+            for h in range(final - 1, first - 1, -1):
+                scale = jnp.where(lane < (h + 1) * HEAD_SIZE - t * LANES, inverse[:, h : h + 1], scale)
+            span = slice(t * LANES, (t + 1) * LANES)
+            att = numer[:, span] * scale
+            att_ref[f, :COLS, span] = att[:COLS] * top
+            att_ref[f, COLS : count - COLS, span] = att[COLS:-COLS]
+            att_ref[f, count - COLS :, span] = att[-COLS:] * bottom
+
+    column = lax.broadcasted_iota(jnp.int32, (COLS, 1), 0)
+    for t in range(-(-chans // LANES)):
+        span = slice(t * LANES, (t + 1) * LANES)
+        used = min(LANES, chans - t * LANES)
+        taps = [weight_ref[9 + i : 10 + i, span] for i in range(3)]
+        for r in range(BLOCK):
+            act = []
+            for f in range(frames):
+                rows = [att_ref[f, (r + k) * COLS : (r + k + 1) * COLS, span] for k in range(3)]
+                sides = []
+                for c in range(3):
+                    weight = [weight_ref[3 * k + c : 3 * k + c + 1, span] for k in range(3)]
+                    sides.append(weight[0] * rows[0] + weight[1] * rows[1] + weight[2] * rows[2])
+                left = jnp.where(column == 0, 0.0, pltpu.roll(sides[0], 1, 0))
+                right = jnp.where(column == COLS - 1, 0.0, pltpu.roll(sides[2], COLS - 1, 0))
+                total = sides[1] + (left + right)
+                act.append(total / (1.0 + jnp.exp(-total)))
+            late = [taps[0] * act[f] + taps[1] * act[f - 1] + taps[2] * act[f - 2] for f in range(2, frames)]
+            early = [taps[0] * act[0], taps[0] * act[1] + taps[1] * act[0]]
+            halo = [taps[1] * act[-1] + taps[2] * act[-2], taps[2] * act[-1]]
+            for ref, values in ((late_ref, late), (early_ref, early), (halo_ref, halo)):
+                for k, value in enumerate(values):
+                    low = k * chans + t * LANES
+                    for z in range(head_devs):
+                        ref[z, 0, r * width : (r + 1) * width, low : low + used] = value[
+                            z * width : (z + 1) * width, :used
+                        ]
 
 
 def forward(parts, local, weights, feat, start, steps, head_devs, after):
     heads, frames = local.shape[:2]
     chans = heads * HEAD_SIZE
-    wide = -(-(chans + heads) // LANES) * LANES
+    wide = padded(chans)
     parts = list(parts)
     width = COLS // head_devs
-    half = BLOCK // 2
-    last = ROWS // BLOCK
-
     def whole(a):
         return pl.BlockSpec(a.shape, lambda i: (0,) * a.ndim)
 
     def out(count):
-        shape = (head_devs, steps * half, width, count, 2 * chans)
-        spec = pl.BlockSpec((head_devs, half, width, count, 2 * chans), lambda i: (0, i, 0, 0, 0))
-        return jax.ShapeDtypeStruct(shape, f32), spec
+        shape = (head_devs, steps, BLOCK * width, count * chans)
+        spec = pl.BlockSpec((head_devs, 1, *shape[2:]), lambda i: (0, i, 0, 0))
+        return in_hbm(shape), spec
 
     outs = [out(frames - 2), out(2), out(2)]
-    feat = feat.reshape(frames, ROWS * COLS, chans)
+    feat = feat.reshape(frames, ROWS * COLS, wide)
     return pl.pallas_call(
         functools.partial(forward_kernel, start, frames, heads, head_devs),
         grid=(steps,),
@@ -309,24 +351,24 @@
                 whole(local),
                 *[whole(w) for w in weights],
                 pl.BlockSpec(
-                    (frames, COLS, chans),
+                    (frames, COLS, wide),
                     lambda i: (0, jnp.maximum((start + i) * BLOCK - 1, 0), 0),
                 ),
-                pl.BlockSpec((frames, BLOCK * COLS, chans), lambda i: (0, start + i, 0)),
+                pl.BlockSpec((frames, BLOCK * COLS, wide), lambda i: (0, start + i, 0)),
                 pl.BlockSpec(
-                    (frames, COLS, chans),
+                    (frames, COLS, wide),
                     lambda i: (0, jnp.minimum((start + i + 1) * BLOCK, ROWS - 1), 0),
                 ),
             ]
-            + [pl.BlockSpec(memory_space=pl.ANY)] * len(after),
+            + [pl.BlockSpec(memory_space=pltpu.HBM)] * len(after),
         out_specs=[spec for _, spec in outs],
         scratch_shapes=[
-                pltpu.VMEM((frames, chans, wide), bf16),
-                pltpu.VMEM((frames, chans, wide), bf16),
+                pltpu.VMEM((frames, 3 * wide, wide), bf16),
                 pltpu.VMEM((16, wide), f32),
+                pltpu.VMEM((frames, (BLOCK + 2) * COLS, wide), f32),
         ],
         out_shape=[shape for shape, _ in outs],
-        compiler_params=params(),
+        compiler_params=params(28 if steps == 1 else 58),
         cost_estimate=cost(6 * steps * 960 * wide * wide, steps * 8000000),
         name="forward_rows",
     )(*parts, local, *weights, feat, feat, feat, *after)
@@ -370,14 +412,14 @@
     return pl.pallas_call(
         functools.partial(query_kernel, wins),
         grid=(heads,),
-        in_specs=[block, block, one, each] + [pl.BlockSpec(memory_space=pl.ANY)] * len(after),
+        in_specs=[block, block, one, each] + [pl.BlockSpec(memory_space=pltpu.HBM)] * len(after),
         out_specs=[block, each, one],
         out_shape=[
-            jax.ShapeDtypeStruct(query_feat.shape, f32),
+            in_hbm(query_feat.shape),
             jax.ShapeDtypeStruct(local.shape, f32),
             jax.ShapeDtypeStruct(before.shape, f32),
         ],
-        compiler_params=params(),
+        compiler_params=params(58),
         cost_estimate=cost(12 * heads * tokens * AUG * AUG, 12 * heads * HEAD_SIZE * tokens),
         name="query_grads",
     )(query_feat, grad_out, before, local, *after)
@@ -418,67 +460,79 @@
             pl.BlockSpec((1, HEAD_SIZE, AUG), lambda h: (h, 0, 0)),
             pl.BlockSpec((1, frames, HEAD_SIZE, AUG), lambda h: (h, 0, 0, 0)),
         ]
-        + [pl.BlockSpec(memory_space=pl.ANY)] * len(after),
+        + [pl.BlockSpec(memory_space=pltpu.HBM)] * len(after),
         out_specs=[block, block],
-        out_shape=[jax.ShapeDtypeStruct(key_feat.shape, f32)] * 2,
-        compiler_params=params(),
+        out_shape=[in_hbm(key_feat.shape)] * 2,
+        compiler_params=params(58),
         cost_estimate=cost(12 * heads * tokens * AUG * AUG, 16 * heads * HEAD_SIZE * tokens),
         name="key_grads",
     )(key_feat, value_feat, later, part, *after)
 
 
-def topped_kernel(early_ref, halo_ref, *rest):
-    rest[-1][...] = early_ref[...] + halo_ref[...]
+def topped_kernel(count, me_ref, *refs):
+    for early_ref, halo_ref, out_ref in zip(refs, refs[count : 2 * count], refs[-count:]):
+        out_ref[...] = early_ref[0] + halo_ref[0]
 
 
 def topped(early, halo, after):
-    block = pl.BlockSpec((1, *early.shape[1:]), lambda z: (z, 0, 0, 0, 0))
-    return pl.pallas_call(
-        topped_kernel,
-        grid=(early.shape[0],),
-        in_specs=[block, block] + [pl.BlockSpec(memory_space=pl.ANY)] * len(after),
-        out_specs=block,
-        out_shape=jax.ShapeDtypeStruct(early.shape, f32),
-        compiler_params=params(),
+    count, steps = early.shape[:2]
+    me = lax.axis_index("head").astype(jnp.int32).reshape(1)
+
+    def block(s):
+        return pl.BlockSpec((1, 1, *early.shape[2:]), lambda i, me: (me[0] ^ s, i, 0, 0))
+
+    return pl.pallas_call(
+        functools.partial(topped_kernel, count),
+        grid_spec=pltpu.PrefetchScalarGridSpec(
+            num_scalar_prefetch=1,
+            grid=(steps,),
+            in_specs=[block(s) for s in range(count)] * 2
+            + [pl.BlockSpec(memory_space=pltpu.HBM)] * len(after),
+            out_specs=[pl.BlockSpec((1, *early.shape[2:]), lambda i, me: (i, 0, 0))] * count,
+        ),
+        out_shape=[in_hbm(early.shape[1:])] * count,
+        compiler_params=params(58),
         cost_estimate=cost(0, 0),
         name="topped",
-    )(early, halo, *after)
-
-
-def place_kernel(chans, early_ref, late_ref, *rest):
-    out_ref = rest[-1]
-    half = BLOCK // 2
-    for first, ref in ((0, early_ref), (2, late_ref)):
-        for r in range(half):
-            for j in range(ref.shape[0]):
-                value = ref[j, r]
-                for side in range(2):
-                    out_ref[
-                        r + side * half, :, first : first + value.shape[1], j * chans : (j + 1) * chans
-                    ] = value[:, :, side * chans : (side + 1) * chans]
+    )(me, *[early] * count, *[halo] * count, *after)
+
+
+def place_kernel(chans, count, *refs):
+    late_ref, out_ref = refs[count], refs[-1]
+    me = lax.axis_index("head")
+    found = [ref[0] for ref in refs[:count]]
+    bit = 1
+    while bit < count:
+        swap = (me & bit) != 0
+        found = [jnp.where(swap, found[s ^ bit], found[s]) for s in range(count)]
+        bit *= 2
+    first = 0
+    for blocks in (found, [late_ref[j, 0] for j in range(count)]):
+        for k in range(blocks[0].shape[1] // chans):
+            pieces = [block[:, k * chans : (k + 1) * chans] for block in blocks]
+            out_ref[:, first, :] = jnp.concatenate(pieces, axis=1)
+            first += 1
 
 
 def placed(early, late, filled, start, steps, chans):
-    half = BLOCK // 2
-    width = early.shape[2]
-    frames = early.shape[3] + late.shape[3]
-    total = early.shape[0] * chans
-
-    def spec(a):
-        return pl.BlockSpec((a.shape[0], half, *a.shape[2:]), lambda i: (0, i, 0, 0, 0))
-
+    count = len(early)
+    rows = late.shape[2]
+    frames = (early[0].shape[2] + late.shape[3]) // chans
+    total = count * chans
     extra = [] if filled is None else [filled]
     return pl.pallas_call(
-        functools.partial(place_kernel, chans),
+        functools.partial(place_kernel, chans, count),
         grid=(steps,),
-        in_specs=[spec(early), spec(late)] + [pl.BlockSpec(memory_space=pl.ANY)] * len(extra),
-        out_specs=pl.BlockSpec((BLOCK, width, frames, total), lambda i: (start + i, 0, 0, 0)),
-        out_shape=jax.ShapeDtypeStruct((ROWS, width, frames, total), f32),
-        input_output_aliases={2: 0} if extra else {},
-        compiler_params=params(),
+        in_specs=[pl.BlockSpec((1, *a.shape[1:]), lambda i: (i, 0, 0)) for a in early]
+        + [pl.BlockSpec((count, 1, *late.shape[2:]), lambda i: (0, i, 0, 0))]
+        + [pl.BlockSpec(memory_space=pl.ANY)] * len(extra),
+        out_specs=pl.BlockSpec((rows, frames, total), lambda i: (start + i, 0, 0)),
+        out_shape=jax.ShapeDtypeStruct((rows * (ROWS // BLOCK), frames, total), f32),
+        input_output_aliases={count + 1: 0} if extra else {},
+        compiler_params=params(28),
         cost_estimate=cost(0, steps * 2400000),
         name="placed",
-    )(early, late, *extra)
+    )(*early, late, *extra)
 
 
 def body(query_feat, key_feat, value_feat, grad_out, spatial_weight, temporal_weight):
@@ -511,10 +565,14 @@
     later = whole_state(entering(back, True, []), True)
     grad_key, grad_value = key_grads(key_feat, value_feat, later, part, [])
 
-    last = sent(topped(early[1], moved[1], [grad_key]))
-    first = sent(topped(early[0], moved[0], [late[1]]))
+    def exchanged(blocks):
+        return [blocks[0]] + [xor_move(a, "head", s) for s, a in enumerate(blocks) if s]
+
+    last = exchanged(topped(early[1], moved[1], [grad_query]))
+    first = exchanged(topped(early[0], moved[0], [grad_key]))
     mixed = placed(last, late[1], None, *spans[1], chans)
     mixed = placed(first, late[0], mixed, *spans[0], chans)
+    mixed = mixed.reshape(ROWS, COLS // head_devs, *mixed.shape[1:])
     return grad_query, grad_key, grad_value, jnp.transpose(mixed, (2, 0, 1, 3))
 
 

time: 204 us -> 169 us (0.83)
  waiting for transfers between devices: 75 us -> 47.7 us
  Pallas kernels: 83.9 us -> 65.7 us
  starting transfers between devices: 33.5 us -> 49 us
  local copies, waits for them, and re-layouts: 4.88 us -> 2.81 us
    all_to_all x4 -> x2, waiting for transfers between devices: 53.5 us -> 0.01 us  [sent(): return lax.all_to_all(a, 'head', split_axis=0, concat_axis=0, tiled=True)]
    ppermute x10 -> x16, waiting for transfers between devices: 19.9 us -> 47.6 us  [xor_move(): return lax.ppermute(array, axis, [(i, i ^ by) for i in range(count)])]
    ppermute x10 -> x16, starting transfers between devices: 9.83 us -> 33 us  [xor_move(): return lax.ppermute(array, axis, [(i, i ^ by) for i in range(count)])]
    all_to_all x4 -> x2, starting transfers between devices: 19.1 us -> 10.5 us  [sent(): return lax.all_to_all(a, 'head', split_axis=0, concat_axis=0, tiled=True)]
    pallas_call x1, Pallas kernels: 7.83 us -> 2.52 us  [turned(): pl.pallas_call(turn_kernel, grid=(tokens // step,), in_specs=[pl.BlockSpe...]
    pallas_call x5, Pallas kernels: 25.7 us -> 20.5 us  [the longest x2 7.27 us: placed(): pl.pallas_call(functools.partial(place_kernel, chans, count), grid=(steps...]
    pallas_call x2, Pallas kernels: 26.9 us -> 22.4 us  [forward(): pl.pallas_call(functools.partial(forward_kernel, start, frames, heads, he...]
    pallas_call x2, Pallas kernels: 3.34 us -> 0.06 us  [joined(): pl.pallas_call(functools.partial(joined_kernel, reverse, steps), in_specs...]
  transfers between devices with their start and end apart: 16 -> 20, of which waited for: 9 -> 8; matrix products, arithmetic and copies ran while one was open for 2% -> 1% of each run, Pallas kernels for 32% -> 31%
where the time goes in v1:
time: 169 us; the launch traced here: 168 us
  Pallas kernels  65.7 us (39%)
  starting transfers between devices  49 us (29%)
  waiting for transfers between devices  47.7 us (28%)
  local copies, waits for them, and re-layouts  2.81 us (2%)
  other arithmetic  2.54 us (2%)
    ppermute x16, waiting for transfers between devices, xor_move(): return lax.ppermute(array, axis, [(i, i ^ by) for i in range(count)])  47.6 us
    ppermute x16, starting transfers between devices, xor_move(): return lax.ppermute(array, axis, [(i, i ^ by) for i in range(count)])  33 us
    pallas_call x2, Pallas kernels, forward(): pl.pallas_call(functools.partial(forward_kernel, start, frames, heads, he...  22.4 us
    all_to_all x2, starting transfers between devices, sent(): return lax.all_to_all(a, 'head', split_axis=0, concat_axis=0, tiled=True)  10.5 us
    pallas_call x1, Pallas kernels, key_grads(): pl.pallas_call(functools.partial(key_kernel, wins), grid=(heads,), in_spe...  10.4 us
    pallas_call x1, Pallas kernels, query_grads(): pl.pallas_call(functools.partial(query_kernel, wins), grid=(heads,), in_s...  9.77 us
    pallas_call x2, Pallas kernels, placed(): pl.pallas_call(functools.partial(place_kernel, chans, count), grid=(steps...  7.27 us
    pallas_call x2, Pallas kernels, topped(): pl.pallas_call(functools.partial(topped_kernel, count), grid_spec=pltpu.P...  6.75 us
  transfers between devices with their start and end apart: 20, of which 8 were waited for; matrix products, arithmetic and copies ran while one was open for 1% of the time, Pallas kernels for 31%

profile of v1, /device:TPU:0, one launch (start us, length us, event | category | flops | bytes accessed | tf_op | source)
XLA Modules:
  0.0 168.4 jit_solution(5846982760568093030)
XLA Ops:
  0.6 6.5 %local_states.1 = (f32[4,4,112,128]{3,2,1,0:T(8,128)}, f32[4,112,128]{2,1,0:T(8,128)}) custom-call(f32[448,3200]{1,0:T(8,128)} %key_ref.1, f32[448,3200]{1,0:T(8,128)} %value_ref.1), custom_call_target="tpu_custom_call" | custom-call | flops 1 | bytes 1 | tf_op jit(solution)/shard_map/local_states/pallas_call | solution.py:124
  7.6 1.3 collective-permute-done.mate_ref
  10.0 3.9 %collective-permute-start.3 = (f32[2,112,128]{2,1,0:T(8,128)S(1)}, f32[2,112,128]{2,1,0:T(8,128)S(1)}, u32[]{:S(2)}, u32[]{:S(2)}) collective-permute-start(f32[2,112,128]{2,1,0:T(8,128)S(1)} %fusion.3), channel_id=1, source_target_pairs={{0,24},{4,28},{8,16},{12,20},{16,8},{20,12},{24,0},{28,4},{1,25},{... | collective-permute-start | bytes 344072 | tf_op jit(solution)/shard_map/ppermute | solution.py:144
  14.6 2.6 %copy-done.1 = f32[448,3200]{1,0:T(8,128)S(1)} copy-done((f32[448,3200]{1,0:T(8,128)S(1)}, f32[448,3200]{1,0:T(8,128)}, u32[]{:S(2)}) %copy-start.1) | copy-done | bytes 5734424
  17.2 2.5 %turned.1.refs_3_ = f32[3200,512]{1,0:T(8,128)S(1)} custom-call(f32[448,3200]{1,0:T(8,128)S(1)} %copy-done.1), custom_call_target="tpu_custom_call" | custom-call | flops 1 | bytes 1 | tf_op jit(solution)/shard_map/turned/pallas_call | solution.py:206
  21.6 4.9 %forward_rows.2 = (f32[4,1,40,896]{3,2,1,0:T(8,128)}, f32[4,1,40,896]{3,2,1,0:T(8,128)}, f32[4,1,40,896]{3,2,1,0:T(8,128)}) custom-call(f32[2,112,128]{2,1,0:T(8,128)S(1)} %joined.2.part_ref, f32[2,112,128]{2,1,0:T(8,128)S(1)} %collective-permute-done.4.other_ref, f32[4,112,128]{2,1,0:T(8,128)S(1)} %collective-permute-done.mate_ref, ...), custom_call_target="tpu_custom_call" | custom-call | flops 1 | bytes 1 | tf_op jit(solution)/shard_map/forward_rows/pallas_call | solution.py:346
  26.6 5.4 %all-to-all-start = ((f32[4,1,40,896]{3,2,1,0:T(8,128)}), f32[4,1,40,896]{3,2,1,0:T(8,128)S(1)}, u32[]{:S(2)}, u32[]{:S(2)}) async-start(f32[4,1,40,896]{3,2,1,0:T(8,128)} %get-tuple-element.27), calls=%async_computation | async-start | bytes 1146880 | tf_op jit(solution)/shard_map/all_to_all | solution.py:549
  32.0 17.4 %forward_rows.3 = (f32[4,4,40,896]{3,2,1,0:T(8,128)}, f32[4,4,40,896]{3,2,1,0:T(8,128)}, f32[4,4,40,896]{3,2,1,0:T(8,128)}) custom-call(f32[2,112,128]{2,1,0:T(8,128)} %copy-done.7, f32[2,112,128]{2,1,0:T(8,128)} %copy-done.9, f32[4,112,128]{2,1,0:T(8,128)} %copy-done.5, f32[4,4,112,128]{3,2,1,0:T(8,128)} %get-tuple-element.26.local_ref, ...), custom_call_target="tpu_custom_call" | custom-call | flops 1 | bytes 1 | tf_op jit(solution)/shard_map/forward_rows/pallas_call | solution.py:346
  49.4 5.2 %all-to-all-start.1 = ((f32[4,4,40,896]{3,2,1,0:T(8,128)}), f32[4,4,40,896]{3,2,1,0:T(8,128)S(1)}, u32[]{:S(2)}, u32[]{:S(2)}) async-start(f32[4,4,40,896]{3,2,1,0:T(8,128)} %get-tuple-element.45), calls=%async_computation.1 | async-start | bytes 4587520 | tf_op jit(solution)/shard_map/all_to_all | solution.py:549
  54.6 2.7 %collective-permute-start.14 = (f32[4,4,40,896]{3,2,1,0:T(8,128)}, f32[4,4,40,896]{3,2,1,0:T(8,128)}, u32[]{:S(2)}, u32[]{:S(2)}) collective-permute-start(f32[4,4,40,896]{3,2,1,0:T(8,128)} %get-tuple-element.29.rest_1_), channel_id=1, source_target_pairs={{0,4},{4,8},{8,12},{12,16},{16,20},{20,24},{24,28},{1,5},{5,9},{9,... | collective-permute-start | bytes 6881288 | tf_op jit(solution)/shard_map/ppermute | solution.py:561
  58.0 9.8 %query_grads.1 = (f32[448,3200]{1,0:T(8,128)}, f32[4,4,112,128]{3,2,1,0:T(8,128)}, f32[4,112,128]{2,1,0:T(8,128)}) custom-call(f32[448,3200]{1,0:T(8,128)} %query_ref.3, f32[448,3200]{1,0:T(8,128)} %grad_ref.1, f32[4,112,128]{2,1,0:T(8,128)} %fusion.before_ref, f32[4,4,112,128]{3,2,1,0:T(8,128)} %get-tuple-element.26.local_ref, f32[4,1,40,896]{3,2,1,0:T(8,128)} %copy-done.3, ...), custom_call_target="tpu_custom_call" | custom-call | flops 1 | bytes 1 | tf_op jit(solution)/shard_map/query_grads/pallas_call | solution.py:412
  68.6 2.7 %collective-permute-start.10 = (f32[4,1,40,896]{3,2,1,0:T(8,128)}, f32[4,1,40,896]{3,2,1,0:T(8,128)}, u32[]{:S(2)}, u32[]{:S(2)}) collective-permute-start(f32[4,1,40,896]{3,2,1,0:T(8,128)} %get-tuple-element.28.rest_0_), channel_id=1, source_target_pairs={{0,4},{4,8},{8,12},{12,16},{16,20},{20,24},{24,28},{1,5},{5,9},{9,... | collective-permute-start | bytes 1720328 | tf_op jit(solution)/shard_map/ppermute | solution.py:561
  71.3 4.5 %topped.3 = (f32[4,40,896]{2,1,0:T(8,128)}, f32[4,40,896]{2,1,0:T(8,128)}, f32[4,40,896]{2,1,0:T(8,128)}, f32[4,40,896]{2,1,0:T(8,128)}) custom-call(s32[1]{0:T(128)} %bitcast.1.me_ref, f32[4,4,40,896]{3,2,1,0:T(8,128)} %get-tuple-element.40.refs_0_.refs_1_.refs_2_.refs_3_, f32[4,4,40,896]{3,2,1,0:T(8,128)} %get-tuple-element.40.refs_0_.refs_1_.refs_2_.refs_3_, ...), custom_call_target="tpu_custom_call" | custom-call | flops 1 | bytes 1 | tf_op jit(solution)/shard_map/topped/pallas_call | solution.py:484
  75.8 2.1 %collective-permute-start.15 = (f32[4,40,896]{2,1,0:T(8,128)}, f32[4,40,896]{2,1,0:T(8,128)}, u32[]{:S(2)}, u32[]{:S(2)}) collective-permute-start(f32[4,40,896]{2,1,0:T(8,128)} %get-tuple-element.42), channel_id=1, source_target_pairs={{0,1},{1,0},{2,3},{3,2},{4,5},{5,4},{6,7},{7,6},{8,9},{9,8},{10,11... | collective-permute-start | bytes 1720328 | tf_op jit(solution)/shard_map/ppermute | solution.py:144
  77.9 15.5 %collective-permute-start.8 = (f32[2,112,128]{2,1,0:T(8,128)S(1)}, f32[2,112,128]{2,1,0:T(8,128)S(1)}, u32[]{:S(2)}, u32[]{:S(2)}) collective-permute-start(f32[2,112,128]{2,1,0:T(8,128)S(1)} %fusion.2), channel_id=1, source_target_pairs={{0,24},{4,28},{8,16},{12,20},{16,8},{20,12},{24,0},{28,4},{1,25},{... | collective-permute-start | bytes 344072 | tf_op jit(solution)/shard_map/ppermute | solution.py:144
  94.9 2.2 %collective-permute-done.8.refs_2_ = f32[2,112,128]{2,1,0:T(8,128)S(1)} collective-permute-done((f32[2,112,128]{2,1,0:T(8,128)S(1)}, f32[2,112,128]{2,1,0:T(8,128)S(1)}, u32[]{:S(2)}, u32[]{:S(2)}) %collective-permute-start.8) | collective-permute-done | bytes 114720 | tf_op jit(solution)/shard_map/ppermute | solution.py:144
  97.1 2.4 %collective-permute-start.16 = (f32[4,40,896]{2,1,0:T(8,128)}, f32[4,40,896]{2,1,0:T(8,128)}, u32[]{:S(2)}, u32[]{:S(2)}) collective-permute-start(f32[4,40,896]{2,1,0:T(8,128)} %get-tuple-element.43), channel_id=1, source_target_pairs={{0,2},{1,3},{2,0},{3,1},{4,6},{5,7},{6,4},{7,5},{8,10},{9,11},{10,... | collective-permute-start | bytes 1720328 | tf_op jit(solution)/shard_map/ppermute | solution.py:144
  102.8 10.4 %key_grads.1 = (f32[448,3200]{1,0:T(8,128)}, f32[448,3200]{1,0:T(8,128)}) custom-call(f32[448,3200]{1,0:T(8,128)} %key_ref.1, f32[448,3200]{1,0:T(8,128)} %value_ref.1, f32[4,112,128]{2,1,0:T(8,128)} %fusion.1.after_ref, f32[4,4,112,128]{3,2,1,0:T(8,128)} %get-tuple-element.32.part_ref), custom_call_target="tpu_custom_call" | custom-call | flops 1 | bytes 1 | tf_op jit(solution)/shard_map/key_grads/pallas_call | solution.py:454
  113.2 2.3 %topped.2 = (f32[1,40,896]{2,1,0:T(8,128)}, f32[1,40,896]{2,1,0:T(8,128)}, f32[1,40,896]{2,1,0:T(8,128)}, f32[1,40,896]{2,1,0:T(8,128)}) custom-call(s32[1]{0:T(128)} %bitcast.1.me_ref, f32[4,1,40,896]{3,2,1,0:T(8,128)} %get-tuple-element.35.refs_0_.refs_1_.refs_2_.refs_3_, f32[4,1,40,896]{3,2,1,0:T(8,128)} %get-tuple-element.35.refs_0_.refs_1_.refs_2_.refs_3_, ...), custom_call_target="tpu_custom_call" | custom-call | flops 1 | bytes 1 | tf_op jit(solution)/shard_map/topped/pallas_call | solution.py:484
  116.1 2.6 %collective-permute-start.12 = (f32[1,40,896]{2,1,0:T(8,128)}, f32[1,40,896]{2,1,0:T(8,128)}, u32[]{:S(2)}, u32[]{:S(2)}) collective-permute-start(f32[1,40,896]{2,1,0:T(8,128)} %get-tuple-element.38), channel_id=1, source_target_pairs={{0,2},{1,3},{2,0},{3,1},{4,6},{5,7},{6,4},{7,5},{8,10},{9,11},{10,... | collective-permute-start | bytes 430088 | tf_op jit(solution)/shard_map/ppermute | solution.py:144
  119.9 30.8 %collective-permute-done.16.refs_2_ = f32[4,40,896]{2,1,0:T(8,128)} collective-permute-done((f32[4,40,896]{2,1,0:T(8,128)}, f32[4,40,896]{2,1,0:T(8,128)}, u32[]{:S(2)}, u32[]{:S(2)}) %collective-permute-start.16) | collective-permute-done | bytes 573472 | tf_op jit(solution)/shard_map/ppermute | solution.py:144
  150.7 4.9 %placed.2.refs_5_ = f32[200,4,1792]{2,1,0:T(4,128)} custom-call(f32[4,40,896]{2,1,0:T(8,128)S(1)} %copy-done.11, f32[4,40,896]{2,1,0:T(8,128)} %collective-permute-done.15.refs_1_, f32[4,40,896]{2,1,0:T(8,128)} %collective-permute-done.16.refs_2_, f32[4,40,896]{2,1,0:T(8,128)} %collective-permute-done.17.refs_3_, f32[4,4,40,896]{3,2,1,0:T(8,128)S(1)} %all-to-all-done.1.refs_4_), custom_call_target="tpu_custom_call" | custom-call | flops 1 | bytes 1 | tf_op jit(solution)/shard_map/placed/pallas_call | solution.py:523
  155.6 10.5 %collective-permute-done.12.refs_2_ = f32[1,40,896]{2,1,0:T(8,128)} collective-permute-done((f32[1,40,896]{2,1,0:T(8,128)}, f32[1,40,896]{2,1,0:T(8,128)}, u32[]{:S(2)}, u32[]{:S(2)}) %collective-permute-start.12) | collective-permute-done | bytes 143392 | tf_op jit(solution)/shard_map/ppermute | solution.py:144
  166.0 2.4 %placed.3 = f32[200,4,1792]{2,1,0:T(4,128)} custom-call(f32[1,40,896]{2,1,0:T(8,128)S(1)} %copy-done.13, f32[1,40,896]{2,1,0:T(8,128)} %collective-permute-done.11.refs_1_, f32[1,40,896]{2,1,0:T(8,128)} %collective-permute-done.12.refs_2_, f32[1,40,896]{2,1,0:T(8,128)} %collective-permute-done.13.refs_3_, ...), custom_call_target="tpu_custom_call", output_to_operand_aliasing={{}: (5, {})} | custom-call | flops 1 | bytes 1 | tf_op jit(solution)/shard_map/placed/pallas_call | solution.py:523
  (64 shorter events, 12.3 us)
Async XLA Ops:
  7.1 1.8 %collective-permute-start = (f32[4,112,128]{2,1,0:T(8,128)}, f32[4,112,128]{2,1,0:T(8,128)S(1)}, u32[]{:S(2)}, u32[]{:S(2)}) collective-permute-start(f32[4,112,128]{2,1,0:T(8,128)} %get-tuple-element.25), channel_id=1, source_target_pairs={{0,4},{4,0},{8,12},{12,8},{16,20},{20,16},{24,28},{28,24},{1,5},{5... | collective-permute-start | bytes 688136 | tf_op jit(solution)/shard_map/ppermute | solution.py:144
  10.0 9.7 %collective-permute-start.3 = (f32[2,112,128]{2,1,0:T(8,128)S(1)}, f32[2,112,128]{2,1,0:T(8,128)S(1)}, u32[]{:S(2)}, u32[]{:S(2)}) collective-permute-start(f32[2,112,128]{2,1,0:T(8,128)S(1)} %fusion.3), channel_id=1, source_target_pairs={{0,24},{4,28},{8,16},{12,20},{16,8},{20,12},{24,0},{28,4},{1,25},{... | collective-permute-start | bytes 344072 | tf_op jit(solution)/shard_map/ppermute | solution.py:144
  13.9 5.9 %collective-permute-start.2 = (f32[2,112,128]{2,1,0:T(8,128)S(1)}, f32[2,112,128]{2,1,0:T(8,128)S(1)}, u32[]{:S(2)}, u32[]{:S(2)}) collective-permute-start(f32[2,112,128]{2,1,0:T(8,128)S(1)} %fusion.3), channel_id=1, source_target_pairs={{0,16},{4,20},{8,24},{12,28},{16,0},{20,4},{24,8},{28,12},{1,17},{... | collective-permute-start | bytes 344072 | tf_op jit(solution)/shard_map/ppermute | solution.py:144
  14.4 5.6 %collective-permute-start.1 = (f32[2,112,128]{2,1,0:T(8,128)S(1)}, f32[2,112,128]{2,1,0:T(8,128)S(1)}, u32[]{:S(2)}, u32[]{:S(2)}) collective-permute-start(f32[2,112,128]{2,1,0:T(8,128)S(1)} %fusion.3), channel_id=1, source_target_pairs={{0,8},{4,12},{8,0},{12,4},{16,24},{20,28},{24,16},{28,20},{1,9},{5... | collective-permute-start | bytes 344072 | tf_op jit(solution)/shard_map/ppermute | solution.py:144
  20.1 1.4 collective-permute-start.4
  26.6 22.8 %all-to-all-start = ((f32[4,1,40,896]{3,2,1,0:T(8,128)}), f32[4,1,40,896]{3,2,1,0:T(8,128)S(1)}, u32[]{:S(2)}, u32[]{:S(2)}) async-start(f32[4,1,40,896]{3,2,1,0:T(8,128)} %get-tuple-element.27), calls=%async_computation | async-start | bytes 1146880 | tf_op jit(solution)/shard_map/all_to_all | solution.py:549
  32.0 25.3 %copy-start.8 = (f32[2,112,128]{2,1,0:T(8,128)S(1)}, f32[2,112,128]{2,1,0:T(8,128)}, u32[]{:S(2)}) copy-start(f32[2,112,128]{2,1,0:T(8,128)} %copy-done.7) | copy-start | bytes 344068
  32.0 25.3 %copy-start.10 = (f32[2,112,128]{2,1,0:T(8,128)S(1)}, f32[2,112,128]{2,1,0:T(8,128)}, u32[]{:S(2)}) copy-start(f32[2,112,128]{2,1,0:T(8,128)} %copy-done.9) | copy-start | bytes 344068
  49.4 101.2 %all-to-all-start.1 = ((f32[4,4,40,896]{3,2,1,0:T(8,128)}), f32[4,4,40,896]{3,2,1,0:T(8,128)S(1)}, u32[]{:S(2)}, u32[]{:S(2)}) async-start(f32[4,4,40,896]{3,2,1,0:T(8,128)} %get-tuple-element.45), calls=%async_computation.1 | async-start | bytes 4587520 | tf_op jit(solution)/shard_map/all_to_all | solution.py:549
  54.6 16.7 %collective-permute-start.14 = (f32[4,4,40,896]{3,2,1,0:T(8,128)}, f32[4,4,40,896]{3,2,1,0:T(8,128)}, u32[]{:S(2)}, u32[]{:S(2)}) collective-permute-start(f32[4,4,40,896]{3,2,1,0:T(8,128)} %get-tuple-element.29.rest_1_), channel_id=1, source_target_pairs={{0,4},{4,8},{8,12},{12,16},{16,20},{20,24},{24,28},{1,5},{5,9},{9,... | collective-permute-start | bytes 6881288 | tf_op jit(solution)/shard_map/ppermute | solution.py:561
  67.8 10.1 %collective-permute-start.5 = (f32[4,112,128]{2,1,0:T(8,128)}, f32[4,112,128]{2,1,0:T(8,128)S(1)}, u32[]{:S(2)}, u32[]{:S(2)}) collective-permute-start(f32[4,112,128]{2,1,0:T(8,128)} %get-tuple-element.31), channel_id=1, source_target_pairs={{0,4},{4,0},{8,12},{12,8},{16,20},{20,16},{24,28},{28,24},{1,5},{5... | collective-permute-start | bytes 688136 | tf_op jit(solution)/shard_map/ppermute | solution.py:144
  68.6 44.6 %collective-permute-start.10 = (f32[4,1,40,896]{3,2,1,0:T(8,128)}, f32[4,1,40,896]{3,2,1,0:T(8,128)}, u32[]{:S(2)}, u32[]{:S(2)}) collective-permute-start(f32[4,1,40,896]{3,2,1,0:T(8,128)} %get-tuple-element.28.rest_0_), channel_id=1, source_target_pairs={{0,4},{4,8},{8,12},{12,16},{16,20},{20,24},{24,28},{1,5},{5,9},{9,... | collective-permute-start | bytes 1720328 | tf_op jit(solution)/shard_map/ppermute | solution.py:561
  75.8 42.8 %collective-permute-start.15 = (f32[4,40,896]{2,1,0:T(8,128)}, f32[4,40,896]{2,1,0:T(8,128)}, u32[]{:S(2)}, u32[]{:S(2)}) collective-permute-start(f32[4,40,896]{2,1,0:T(8,128)} %get-tuple-element.42), channel_id=1, source_target_pairs={{0,1},{1,0},{2,3},{3,2},{4,5},{5,4},{6,7},{7,6},{8,9},{9,8},{10,11... | collective-permute-start | bytes 1720328 | tf_op jit(solution)/shard_map/ppermute | solution.py:144
  77.9 19.1 %collective-permute-start.8 = (f32[2,112,128]{2,1,0:T(8,128)S(1)}, f32[2,112,128]{2,1,0:T(8,128)S(1)}, u32[]{:S(2)}, u32[]{:S(2)}) collective-permute-start(f32[2,112,128]{2,1,0:T(8,128)S(1)} %fusion.2), channel_id=1, source_target_pairs={{0,24},{4,28},{8,16},{12,20},{16,8},{20,12},{24,0},{28,4},{1,25},{... | collective-permute-start | bytes 344072 | tf_op jit(solution)/shard_map/ppermute | solution.py:144
  93.5 6.0 %collective-permute-start.7 = (f32[2,112,128]{2,1,0:T(8,128)S(1)}, f32[2,112,128]{2,1,0:T(8,128)S(1)}, u32[]{:S(2)}, u32[]{:S(2)}) collective-permute-start(f32[2,112,128]{2,1,0:T(8,128)S(1)} %fusion.2), channel_id=1, source_target_pairs={{0,16},{4,20},{8,24},{12,28},{16,0},{20,4},{24,8},{28,12},{1,17},{... | collective-permute-start | bytes 344072 | tf_op jit(solution)/shard_map/ppermute | solution.py:144
  94.0 6.7 %collective-permute-start.6 = (f32[2,112,128]{2,1,0:T(8,128)S(1)}, f32[2,112,128]{2,1,0:T(8,128)S(1)}, u32[]{:S(2)}, u32[]{:S(2)}) collective-permute-start(f32[2,112,128]{2,1,0:T(8,128)S(1)} %fusion.2), channel_id=1, source_target_pairs={{0,8},{4,12},{8,0},{12,4},{16,24},{20,28},{24,16},{28,20},{1,9},{5... | collective-permute-start | bytes 344072 | tf_op jit(solution)/shard_map/ppermute | solution.py:144
  97.1 53.6 %collective-permute-start.16 = (f32[4,40,896]{2,1,0:T(8,128)}, f32[4,40,896]{2,1,0:T(8,128)}, u32[]{:S(2)}, u32[]{:S(2)}) collective-permute-start(f32[4,40,896]{2,1,0:T(8,128)} %get-tuple-element.43), channel_id=1, source_target_pairs={{0,2},{1,3},{2,0},{3,1},{4,6},{5,7},{6,4},{7,5},{8,10},{9,11},{10,... | collective-permute-start | bytes 1720328 | tf_op jit(solution)/shard_map/ppermute | solution.py:144
  99.4 51.2 %collective-permute-start.17 = (f32[4,40,896]{2,1,0:T(8,128)}, f32[4,40,896]{2,1,0:T(8,128)}, u32[]{:S(2)}, u32[]{:S(2)}) collective-permute-start(f32[4,40,896]{2,1,0:T(8,128)} %get-tuple-element.44), channel_id=1, source_target_pairs={{0,3},{1,2},{2,1},{3,0},{4,7},{5,6},{6,5},{7,4},{8,11},{9,10},{10,... | collective-permute-start | bytes 1720328 | tf_op jit(solution)/shard_map/ppermute | solution.py:144
  100.7 1.4 collective-permute-start.9
  113.2 37.4 %copy-start.11 = (f32[4,40,896]{2,1,0:T(8,128)S(1)}, f32[4,40,896]{2,1,0:T(8,128)}, u32[]{:S(2)}) copy-start(f32[4,40,896]{2,1,0:T(8,128)} %get-tuple-element.41.refs_0_) | copy-start | bytes 1720324
  115.5 50.5 %copy-start.4 = (f32[4,1,40,896]{3,2,1,0:T(8,128)S(1)}, f32[4,1,40,896]{3,2,1,0:T(8,128)}, u32[]{:S(2)}) copy-start(f32[4,1,40,896]{3,2,1,0:T(8,128)} %copy-done.3) | copy-start | bytes 1720324
  115.5 40.1 %collective-permute-start.11 = (f32[1,40,896]{2,1,0:T(8,128)}, f32[1,40,896]{2,1,0:T(8,128)}, u32[]{:S(2)}, u32[]{:S(2)}) collective-permute-start(f32[1,40,896]{2,1,0:T(8,128)} %get-tuple-element.37), channel_id=1, source_target_pairs={{0,1},{1,0},{2,3},{3,2},{4,5},{5,4},{6,7},{7,6},{8,9},{9,8},{10,11... | collective-permute-start | bytes 430088 | tf_op jit(solution)/shard_map/ppermute | solution.py:144
  116.1 50.0 %collective-permute-start.12 = (f32[1,40,896]{2,1,0:T(8,128)}, f32[1,40,896]{2,1,0:T(8,128)}, u32[]{:S(2)}, u32[]{:S(2)}) collective-permute-start(f32[1,40,896]{2,1,0:T(8,128)} %get-tuple-element.38), channel_id=1, source_target_pairs={{0,2},{1,3},{2,0},{3,1},{4,6},{5,7},{6,4},{7,5},{8,10},{9,11},{10,... | collective-permute-start | bytes 430088 | tf_op jit(solution)/shard_map/ppermute | solution.py:144
  118.7 47.4 %collective-permute-start.13 = (f32[1,40,896]{2,1,0:T(8,128)}, f32[1,40,896]{2,1,0:T(8,128)}, u32[]{:S(2)}, u32[]{:S(2)}) collective-permute-start(f32[1,40,896]{2,1,0:T(8,128)} %get-tuple-element.39), channel_id=1, source_target_pairs={{0,3},{1,2},{2,1},{3,0},{4,7},{5,6},{6,5},{7,4},{8,11},{9,10},{10,... | collective-permute-start | bytes 430088 | tf_op jit(solution)/shard_map/ppermute | solution.py:144
  (12 other events, 95.1 us)

commit v2 on v1

--- a/solution.py
+++ b/solution.py
@@ -189,19 +189,28 @@
     return full + jnp.where(late, mate, 0.0)
 
 
+PAIR = 2 * HEAD_SIZE
+GROUP = -(-(PAIR + 2) // LANES) * LANES
+
+
+def grouped(chans):
+    return -(-chans // PAIR) * GROUP
+
+
 def turn_kernel(query_ref, out_ref):
     chans = query_ref.shape[0]
-    out_ref[:, :chans] = jnp.exp(query_ref[...]).T
-    out_ref[:, chans:] = jnp.zeros((out_ref.shape[0], out_ref.shape[1] - chans), f32)
-
-
-def padded(chans):
-    return -(-(chans + chans // HEAD_SIZE) // LANES) * LANES
+    for g in range(-(-chans // PAIR)):
+        last = min((g + 1) * PAIR, chans)
+        used = g * GROUP + last - g * PAIR
+        out_ref[:, g * GROUP : used] = jnp.exp(query_ref[g * PAIR : last, :]).T
+        out_ref[:, used : (g + 1) * GROUP] = jnp.zeros(
+            (out_ref.shape[0], (g + 1) * GROUP - used), f32
+        )
 
 
 def turned(query_feat):
     chans, tokens = query_feat.shape
-    wide = padded(chans)
+    wide = grouped(chans)
     step = 640 if tokens % 640 == 0 else tokens
     return pl.pallas_call(
         turn_kernel,
@@ -219,11 +228,31 @@
     start, frames, heads, head_devs, part_ref, other_ref, mate_ref, local_ref, spatial_ref,
     temporal_ref, prev_ref, cur_ref, next_ref, *rest
 ):
-    late_ref, early_ref, halo_ref, mix_ref, weight_ref, att_ref = rest[-6:]
+    late_ref, act_ref, weight_ref, mix_ref, att_ref = rest[-5:]
     chans = heads * HEAD_SIZE
     wide = weight_ref.shape[1]
     width = COLS // head_devs
+    groups = [(g, min((g + 1) * PAIR, chans) - g * PAIR) for g in range(wide // GROUP)]
     step = pl.program_id(0)
+    lane = lax.broadcasted_iota(jnp.int32, (1, LANES), 1)
+    count = (BLOCK + 2) * COLS
+    kept = 2 * COLS
+
+    def attend(f, first, feat):
+        rows = feat.shape[0]
+        high, low = split(feat)
+        for g, used in groups:
+            at = slice(g * GROUP, (g + 1) * GROUP)
+            pieces = jnp.concatenate([high[:, at], low[:, at], high[:, at]], axis=1)
+            numer = dot(pieces, mix_ref[f, g], ((1,), (0,)))
+            inverse = 1.0 / numer[:, PAIR : PAIR + 2]
+            for t in range(GROUP // LANES):
+                scale = jnp.where(lane < HEAD_SIZE - t * LANES, inverse[:, :1], inverse[:, 1:])
+                if used <= HEAD_SIZE:
+                    scale = inverse[:, :1]
+                span = slice(t * LANES, (t + 1) * LANES)
+                home = slice(g * GROUP + t * LANES, g * GROUP + (t + 1) * LANES)
+                att_ref[f, first : first + rows, home] = numer[:, span] * scale
 
     @pl.when(step == 0)
     def _():
@@ -234,74 +263,71 @@
 
             @pl.when(me == z)
             def _():
-                at = slice(z * chans, (z + 1) * chans)
-                for r in range(3):
-                    weight_ref[3 * r : 3 * r + 3, :chans] = spatial_ref[r, :, at]
-                weight_ref[9:12, :chans] = temporal_ref[:, at]
-
+                for g, used in groups:
+                    low = z * chans + g * PAIR
+                    at, home = slice(low, low + used), slice(g * GROUP, g * GROUP + used)
+                    for r in range(3):
+                        weight_ref[3 * r : 3 * r + 3, home] = spatial_ref[r, :, at]
+                    weight_ref[9:12, home] = temporal_ref[:, at]
+
+        whole = lax.broadcasted_iota(jnp.int32, (HEAD_SIZE, LANES), 1)
         for f in range(frames):
-            for k in range(3):
-                spare = pl.ds(k * wide + chans, wide - chans)
-                mix_ref[f, spare, :] = jnp.zeros((wide - chans, wide), bf16)
-        lane = lax.broadcasted_iota(jnp.int32, (HEAD_SIZE, LANES), 1)
-        last = wide // LANES - 1
+            for g, _ in groups:
+                for k in range(3):
+                    spare = pl.ds(k * GROUP + PAIR, GROUP - PAIR)
+                    mix_ref[f, g, spare, :] = jnp.zeros((GROUP - PAIR, GROUP), bf16)
         for h in range(heads):
             first, second = part_ref, other_ref
             if h >= heads // 2:
                 first, second = second, first
-            g = h % (heads // 2)
-            state = jnp.where(odd, second[g] + mate_ref[h], first[g])
-            tile, shift = divmod(h * HEAD_SIZE, LANES)
-            over = shift + HEAD_SIZE - LANES
-            at = [pl.ds(k * wide + h * HEAD_SIZE, HEAD_SIZE) for k in range(3)]
+            state = jnp.where(odd, second[h % (heads // 2)] + mate_ref[h], first[h % (heads // 2)])
+            g, i = divmod(h, 2)
+            shift = i * HEAD_SIZE
+            at = [pl.ds(k * GROUP + shift, HEAD_SIZE) for k in range(3)]
             for f in range(frames):
                 state = state + local_ref[h, f]
                 moved = pltpu.roll(state, shift, 1) if shift else state
                 sums = state[:, HEAD_SIZE : HEAD_SIZE + 1]
-                for t in range(last + 1):
-                    value = None
-                    if t == tile:
-                        value = jnp.where((lane >= shift) & (lane < shift + HEAD_SIZE), moved, 0.0)
-                    elif t == tile + 1 and over > 0:
-                        value = jnp.where(lane < over, moved, 0.0)
-                    if t == last:
-                        value = jnp.zeros_like(state) if value is None else value
-                        value = jnp.where(lane == chans - last * LANES + h, sums, value)
+                for t in range(GROUP // LANES):
+                    place = whole + t * LANES
+                    value = jnp.where((place >= shift) & (place < shift + HEAD_SIZE), moved, 0.0)
+                    value = jnp.where(place == PAIR + i, sums, value)
                     span = slice(t * LANES, (t + 1) * LANES)
-                    if value is None:
-                        high = low = jnp.zeros((HEAD_SIZE, LANES), bf16)
-                    else:
-                        high, low = split(value)
-                    mix_ref[f, at[0], span] = low
-                    mix_ref[f, at[1], span] = high
-                    mix_ref[f, at[2], span] = high
-
-    block = start + step
-    top = jnp.where(block == 0, 0.0, 1.0)
-    bottom = jnp.where(block == ROWS // BLOCK - 1, 0.0, 1.0)
-    count = (BLOCK + 2) * COLS
-    lane = lax.broadcasted_iota(jnp.int32, (1, LANES), 1)
+                    high, low = split(value)
+                    mix_ref[f, g, at[0], span] = low
+                    mix_ref[f, g, at[1], span] = high
+                    mix_ref[f, g, at[2], span] = high
+        if heads % 2:
+            for f in range(frames):
+                for k in range(3):
+                    mix_ref[f, groups[-1][0], pl.ds(k * GROUP + HEAD_SIZE, HEAD_SIZE), :] = jnp.zeros(
+                        (HEAD_SIZE, GROUP), bf16
+                    )
+        for f in range(frames):
+            attend(f, 0, jnp.concatenate([prev_ref[f], cur_ref[f, :COLS]], axis=0))
+            if start == 0:
+                att_ref[f, :COLS, :] = jnp.zeros((COLS, wide), f32)
+
+    @pl.when(step > 0)
+    def _():
+        for f in range(frames):
+            att_ref[f, :kept, :] = att_ref[f, count - kept :, :]
+
     for f in range(frames):
-        high, low = split(jnp.concatenate([prev_ref[f], cur_ref[f], next_ref[f]], axis=0))
-        pieces = jnp.concatenate([high, low, high], axis=1)
-        numer = dot(pieces, mix_ref[f], ((1,), (0,)))
-        inverse = 1.0 / numer[:, chans : chans + heads]
-        for t in range(wide // LANES):
-            first = t * LANES // HEAD_SIZE
-            final = min(((t + 1) * LANES - 1) // HEAD_SIZE, heads - 1)
-            scale = inverse[:, final : final + 1]
-            for h in range(final - 1, first - 1, -1):
-                scale = jnp.where(lane < (h + 1) * HEAD_SIZE - t * LANES, inverse[:, h : h + 1], scale)
-            span = slice(t * LANES, (t + 1) * LANES)
-            att = numer[:, span] * scale
-            att_ref[f, :COLS, span] = att[:COLS] * top
-            att_ref[f, COLS : count - COLS, span] = att[COLS:-COLS]
-            att_ref[f, count - COLS :, span] = att[-COLS:] * bottom
+        attend(f, kept, jnp.concatenate([cur_ref[f, COLS:], next_ref[f]], axis=0))
+
+    @pl.when(start + step == ROWS // BLOCK - 1)
+    def _():
+        for f in range(frames):
+            att_ref[f, count - COLS :, :] = jnp.zeros((COLS, wide), f32)
 
     column = lax.broadcasted_iota(jnp.int32, (COLS, 1), 0)
-    for t in range(-(-chans // LANES)):
+    for t in range(wide // LANES):
         span = slice(t * LANES, (t + 1) * LANES)
-        used = min(LANES, chans - t * LANES)
+        g, inner = t * LANES // GROUP, t * LANES % GROUP
+        used = min(LANES, groups[g][1] - inner)
+        if used <= 0:
+            continue
         taps = [weight_ref[9 + i : 10 + i, span] for i in range(3)]
         for r in range(BLOCK):
             act = []
@@ -315,22 +341,67 @@
                 right = jnp.where(column == COLS - 1, 0.0, pltpu.roll(sides[2], COLS - 1, 0))
                 total = sides[1] + (left + right)
                 act.append(total / (1.0 + jnp.exp(-total)))
+                act_ref[f, r * COLS : (r + 1) * COLS, span] = act[f]
             late = [taps[0] * act[f] + taps[1] * act[f - 1] + taps[2] * act[f - 2] for f in range(2, frames)]
+            put(late_ref, late, chans, g * PAIR + inner, used, r)
+
+
+def put(ref, values, chans, channel, used, r):
+    width = ref.shape[2] // BLOCK
+    home = slice(r * width, (r + 1) * width)
+    for k, value in enumerate(values):
+        low = k * chans + channel
+        shift = low % LANES
+        cut = min(used, LANES - shift)
+        if shift:
+            value = pltpu.roll(value, shift, 1)
+        for z in range(ref.shape[0]):
+            rows = value[z * width : (z + 1) * width]
+            ref[z, 0, home, low : low + cut] = rows[:, shift : shift + cut]
+            if used > cut:
+                ref[z, 0, home, low + cut : low + used] = rows[:, : used - cut]
+
+
+def early_kernel(chans, act_ref, weight_ref, early_ref, halo_ref):
+    frames, _, wide = act_ref.shape
+    for t in range(wide // LANES):
+        span = slice(t * LANES, (t + 1) * LANES)
+        g, inner = t * LANES // GROUP, t * LANES % GROUP
+        used = min(LANES, min((g + 1) * PAIR, chans) - g * PAIR - inner)
+        if used <= 0:
+            continue
+        taps = [weight_ref[9 + i : 10 + i, span] for i in range(3)]
+        for r in range(BLOCK):
+            act = [act_ref[f, r * COLS : (r + 1) * COLS, span] for f in range(frames)]
             early = [taps[0] * act[0], taps[0] * act[1] + taps[1] * act[0]]
             halo = [taps[1] * act[-1] + taps[2] * act[-2], taps[2] * act[-1]]
-            for ref, values in ((late_ref, late), (early_ref, early), (halo_ref, halo)):
-                for k, value in enumerate(values):
-                    low = k * chans + t * LANES
-                    for z in range(head_devs):
-                        ref[z, 0, r * width : (r + 1) * width, low : low + used] = value[
-                            z * width : (z + 1) * width, :used
-                        ]
+            put(early_ref, early, chans, g * PAIR + inner, used, r)
+            put(halo_ref, halo, chans, g * PAIR + inner, used, r)
+
+
+def first_frames(act, weights, chans, head_devs):
+    frames, tokens, wide = act.shape
+    steps = tokens // (BLOCK * COLS)
+    shape = (head_devs, steps, BLOCK * COLS // head_devs, 2 * chans)
+    return pl.pallas_call(
+        functools.partial(early_kernel, chans),
+        grid=(steps,),
+        in_specs=[
+            pl.BlockSpec((frames, BLOCK * COLS, wide), lambda i: (0, i, 0)),
+            pl.BlockSpec(weights.shape, lambda i: (0, 0)),
+        ],
+        out_specs=[pl.BlockSpec((head_devs, 1, *shape[2:]), lambda i: (0, i, 0, 0))] * 2,
+        out_shape=[in_hbm(shape)] * 2,
+        compiler_params=params(58),
+        cost_estimate=cost(0, 0),
+        name="first_frames",
+    )(act, weights)
 
 
 def forward(parts, local, weights, feat, start, steps, head_devs, after):
     heads, frames = local.shape[:2]
     chans = heads * HEAD_SIZE
-    wide = padded(chans)
+    wide = grouped(chans)
     parts = list(parts)
     width = COLS // head_devs
     def whole(a):
@@ -341,7 +412,14 @@
         spec = pl.BlockSpec((head_devs, 1, *shape[2:]), lambda i: (0, i, 0, 0))
         return in_hbm(shape), spec
 
-    outs = [out(frames - 2), out(2), out(2)]
+    outs = [
+        out(frames - 2),
+        (
+            in_hbm((frames, steps * BLOCK * COLS, wide)),
+            pl.BlockSpec((frames, BLOCK * COLS, wide), lambda i: (0, i, 0)),
+        ),
+        (jax.ShapeDtypeStruct((16, wide), f32), pl.BlockSpec((16, wide), lambda i: (0, 0))),
+    ]
     feat = feat.reshape(frames, ROWS * COLS, wide)
     return pl.pallas_call(
         functools.partial(forward_kernel, start, frames, heads, head_devs),
@@ -352,7 +430,7 @@
                 *[whole(w) for w in weights],
                 pl.BlockSpec(
                     (frames, COLS, wide),
-                    lambda i: (0, jnp.maximum((start + i) * BLOCK - 1, 0), 0),
+                    lambda i: (0, max(start * BLOCK - 1, 0), 0),
                 ),
                 pl.BlockSpec((frames, BLOCK * COLS, wide), lambda i: (0, start + i, 0)),
                 pl.BlockSpec(
@@ -363,8 +441,7 @@
             + [pl.BlockSpec(memory_space=pltpu.HBM)] * len(after),
         out_specs=[spec for _, spec in outs],
         scratch_shapes=[
-                pltpu.VMEM((frames, 3 * wide, wide), bf16),
-                pltpu.VMEM((16, wide), f32),
+                pltpu.VMEM((frames, wide // GROUP, 3 * GROUP, GROUP), bf16),
                 pltpu.VMEM((frames, (BLOCK + 2) * COLS, wide), f32),
         ],
         out_shape=[shape for shape, _ in outs],
@@ -490,7 +567,7 @@
             + [pl.BlockSpec(memory_space=pltpu.HBM)] * len(after),
             out_specs=[pl.BlockSpec((1, *early.shape[2:]), lambda i, me: (i, 0, 0))] * count,
         ),
-        out_shape=[in_hbm(early.shape[1:])] * count,
+        out_shape=[in_hbm((steps, *early.shape[2:]))] * count,
         compiler_params=params(58),
         cost_estimate=cost(0, 0),
         name="topped",
@@ -529,8 +606,8 @@
         out_specs=pl.BlockSpec((rows, frames, total), lambda i: (start + i, 0, 0)),
         out_shape=jax.ShapeDtypeStruct((rows * (ROWS // BLOCK), frames, total), f32),
         input_output_aliases={count + 1: 0} if extra else {},
-        compiler_params=params(28),
-        cost_estimate=cost(0, steps * 2400000),
+        compiler_params=params(14 if steps == 1 else 28),
+        cost_estimate=cost(0, 0),
         name="placed",
     )(*early, late, *extra)
 
@@ -549,29 +626,34 @@
         return lax.all_to_all(a, "head", split_axis=0, concat_axis=0, tiled=True)
 
     spans = [(0, 1), (1, ROWS // BLOCK - 1)]
-    late, early, halo = [], [], []
-    after = []
+    late, acts, after = [], [], []
     for start, steps in spans:
-        a, b, c = forward(parts, local, (spatial_weight, temporal_weight), feat, start, steps, head_devs, after)
+        a, act, weights = forward(
+            parts, local, (spatial_weight, temporal_weight), feat, start, steps, head_devs, after
+        )
         late.append(sent(a))
-        early.append(b)
-        halo.append(c)
-        after = [c]
+        acts.append(act)
+        after = [act]
+    shares = [first_frames(act, weights, chans, head_devs) for act in acts]
     pairs = [(i, i + 1) for i in range(segs - 1)]
-    moved = [lax.ppermute(c, "seg", pairs) for c in halo]
+    moved = [lax.ppermute(halo, "seg", pairs) for _, halo in shares]
 
     before = whole_state(parts, False)
-    grad_query, part, back = query_grads(query_feat, grad_out, before, local, [late[0], halo[-1]])
+    after = [late[0], shares[0][1], shares[1][1]]
+    grad_query, part, back = query_grads(query_feat, grad_out, before, local, after)
     later = whole_state(entering(back, True, []), True)
     grad_key, grad_value = key_grads(key_feat, value_feat, later, part, [])
 
     def exchanged(blocks):
         return [blocks[0]] + [xor_move(a, "head", s) for s, a in enumerate(blocks) if s]
 
-    last = exchanged(topped(early[1], moved[1], [grad_query]))
-    first = exchanged(topped(early[0], moved[0], [grad_key]))
-    mixed = placed(last, late[1], None, *spans[1], chans)
-    mixed = placed(first, late[0], mixed, *spans[0], chans)
+    ties = [[grad_key], [grad_query]]
+    arrived = [
+        exchanged(topped(early, halo, tie)) for (early, _), halo, tie in zip(shares, moved, ties)
+    ]
+    mixed = None
+    for i in (1, 0):
+        mixed = placed(arrived[i], late[i], mixed, *spans[i], chans)
     mixed = mixed.reshape(ROWS, COLS // head_devs, *mixed.shape[1:])
     return grad_query, grad_key, grad_value, jnp.transpose(mixed, (2, 0, 1, 3))
 

time: 169 us -> 165 us (0.976)
  starting transfers between devices: 49 us -> 44.6 us
  waiting for transfers between devices: 47.7 us -> 43.8 us
  Pallas kernels: 65.7 us -> 69.5 us
    pallas_call x0 -> x2, Pallas kernels: none -> 8.3 us  [first_frames(): pl.pallas_call(functools.partial(early_kernel, chans), grid=(steps,), in_...]
    ppermute x16, waiting for transfers between devices: 47.6 us -> 42.2 us  [xor_move(): return lax.ppermute(array, axis, [(i, i ^ by) for i in range(count)])]
    pallas_call x2, Pallas kernels: 22.4 us -> 18 us  [forward(): pl.pallas_call(functools.partial(forward_kernel, start, frames, heads, he...]
    ppermute x16, starting transfers between devices: 33 us -> 30.3 us  [xor_move(): return lax.ppermute(array, axis, [(i, i ^ by) for i in range(count)])]
  transfers between devices with their start and end apart: 20 -> 20, of which waited for: 8 -> 8; matrix products, arithmetic and copies ran while one was open for 1% -> 1% of each run, Pallas kernels for 31% -> 34%
where the time goes in v2:
time: 165 us; the launch traced here: 164 us
  Pallas kernels  69.5 us (42%)
  starting transfers between devices  44.6 us (27%)
  waiting for transfers between devices  43.8 us (27%)
  local copies, waits for them, and re-layouts  2.81 us (2%)
  other arithmetic  2.53 us (2%)
    ppermute x16, waiting for transfers between devices, xor_move(): return lax.ppermute(array, axis, [(i, i ^ by) for i in range(count)])  42.2 us
    ppermute x16, starting transfers between devices, xor_move(): return lax.ppermute(array, axis, [(i, i ^ by) for i in range(count)])  30.3 us
    pallas_call x2, Pallas kernels, forward(): pl.pallas_call(functools.partial(forward_kernel, start, frames, heads, he...  18 us
    pallas_call x1, Pallas kernels, key_grads(): pl.pallas_call(functools.partial(key_kernel, wins), grid=(heads,), in_spe...  10.4 us
    pallas_call x1, Pallas kernels, query_grads(): pl.pallas_call(functools.partial(query_kernel, wins), grid=(heads,), in_s...  9.77 us
    all_to_all x2, starting transfers between devices, sent(): return lax.all_to_all(a, 'head', split_axis=0, concat_axis=0, tiled=True)  8.93 us
    pallas_call x2, Pallas kernels, first_frames(): pl.pallas_call(functools.partial(early_kernel, chans), grid=(steps,), in_...  8.3 us
    pallas_call x2, Pallas kernels, placed(): pl.pallas_call(functools.partial(place_kernel, chans, count), grid=(steps...  7.27 us
  transfers between devices with their start and end apart: 20, of which 8 were waited for; matrix products, arithmetic and copies ran while one was open for 1% of the time, Pallas kernels for 34%

profile of v2, /device:TPU:0, one launch (start us, length us, event | category | flops | bytes accessed | tf_op | source)
XLA Modules:
  0.0 164.2 jit_solution(8435061391469106817)
XLA Ops:
  0.6 6.5 %local_states.1 = (f32[4,4,112,128]{3,2,1,0:T(8,128)}, f32[4,112,128]{2,1,0:T(8,128)}) custom-call(f32[448,3200]{1,0:T(8,128)} %key_ref.1, f32[448,3200]{1,0:T(8,128)} %value_ref.1), custom_call_target="tpu_custom_call" | custom-call | flops 1 | bytes 1 | tf_op jit(solution)/shard_map/local_states/pallas_call | solution.py:124
  10.1 3.9 %collective-permute-start.3 = (f32[2,112,128]{2,1,0:T(8,128)S(1)}, f32[2,112,128]{2,1,0:T(8,128)S(1)}, u32[]{:S(2)}, u32[]{:S(2)}) collective-permute-start(f32[2,112,128]{2,1,0:T(8,128)S(1)} %fusion.3), channel_id=1, source_target_pairs={{0,24},{4,28},{8,16},{12,20},{16,8},{20,12},{24,0},{28,4},{1,25},{... | collective-permute-start | bytes 344072 | tf_op jit(solution)/shard_map/ppermute | solution.py:144
  14.6 2.6 %copy-done.1 = f32[448,3200]{1,0:T(8,128)S(1)} copy-done((f32[448,3200]{1,0:T(8,128)S(1)}, f32[448,3200]{1,0:T(8,128)}, u32[]{:S(2)}) %copy-start.1) | copy-done | bytes 5734424
  17.2 2.6 %turned.1.refs_3_ = f32[3200,512]{1,0:T(8,128)S(1)} custom-call(f32[448,3200]{1,0:T(8,128)S(1)} %copy-done.1), custom_call_target="tpu_custom_call" | custom-call | flops 1 | bytes 1 | tf_op jit(solution)/shard_map/turned/pallas_call | solution.py:215
  21.7 4.1 %forward_rows.2 = (f32[4,1,40,896]{3,2,1,0:T(8,128)}, f32[4,160,512]{2,1,0:T(8,128)}, f32[16,512]{1,0:T(8,128)}) custom-call(f32[2,112,128]{2,1,0:T(8,128)S(1)} %joined.2.part_ref, f32[2,112,128]{2,1,0:T(8,128)S(1)} %collective-permute-done.4.other_ref, f32[4,112,128]{2,1,0:T(8,128)S(1)} %collective-permute-done.mate_ref, f32[4,4,112,128]{3,2,1,0:T(8,128)S(1)} %copy-done.2, ...), custom_call_target="tpu_custom_call" | custom-call | flops 1 | bytes 1 | tf_op jit(solution)/shard_map/forward_rows/pallas_call | solution.py:424
  25.8 5.3 %all-to-all-start = ((f32[4,1,40,896]{3,2,1,0:T(8,128)}), f32[4,1,40,896]{3,2,1,0:T(8,128)S(1)}, u32[]{:S(2)}, u32[]{:S(2)}) async-start(f32[4,1,40,896]{3,2,1,0:T(8,128)} %get-tuple-element.30), calls=%async_computation | async-start | bytes 1146880 | tf_op jit(solution)/shard_map/all_to_all | solution.py:626
  31.1 13.8 %forward_rows.3 = (f32[4,4,40,896]{3,2,1,0:T(8,128)}, f32[4,640,512]{2,1,0:T(8,128)}, f32[16,512]{1,0:T(8,128)}) custom-call(f32[2,112,128]{2,1,0:T(8,128)} %copy-done.7, f32[2,112,128]{2,1,0:T(8,128)} %copy-done.9, f32[4,112,128]{2,1,0:T(8,128)} %copy-done.5, f32[4,4,112,128]{3,2,1,0:T(8,128)} %get-tuple-element.29.local_ref, f32[3,3,1792]{2,1,0:T(4,128)} %spatial_ref.3, ...), custom_call_target="tpu_custom_call" | custom-call | flops 1 | bytes 1 | tf_op jit(solution)/shard_map/forward_rows/pallas_call | solution.py:424
  46.6 3.6 %all-to-all-start.1 = ((f32[4,4,40,896]{3,2,1,0:T(8,128)}), f32[4,4,40,896]{3,2,1,0:T(8,128)S(1)}, u32[]{:S(2)}, u32[]{:S(2)}) async-start(f32[4,4,40,896]{3,2,1,0:T(8,128)} %get-tuple-element.51), calls=%async_computation.1 | async-start | bytes 4587520 | tf_op jit(solution)/shard_map/all_to_all | solution.py:626
  50.3 5.6 %first_frames.3 = (f32[4,4,40,896]{3,2,1,0:T(8,128)}, f32[4,4,40,896]{3,2,1,0:T(8,128)}) custom-call(f32[4,640,512]{2,1,0:T(8,128)} %get-tuple-element.34.act_ref, f32[16,512]{1,0:T(8,128)} %get-tuple-element.32.weight_ref), custom_call_target="tpu_custom_call" | custom-call | flops 1 | bytes 1 | tf_op jit(solution)/shard_map/first_frames/pallas_call | solution.py:386
  55.9 2.7 %collective-permute-start.14 = (f32[4,4,40,896]{3,2,1,0:T(8,128)}, f32[4,4,40,896]{3,2,1,0:T(8,128)}, u32[]{:S(2)}, u32[]{:S(2)}) collective-permute-start(f32[4,4,40,896]{3,2,1,0:T(8,128)} %get-tuple-element.35.rest_2_), channel_id=1, source_target_pairs={{0,4},{4,8},{8,12},{12,16},{16,20},{20,24},{24,28},{1,5},{5,9},{9,... | collective-permute-start | bytes 6881288 | tf_op jit(solution)/shard_map/ppermute | solution.py:639
  58.6 2.7 %first_frames.2 = (f32[4,1,40,896]{3,2,1,0:T(8,128)}, f32[4,1,40,896]{3,2,1,0:T(8,128)}) custom-call(f32[4,160,512]{2,1,0:T(8,128)} %get-tuple-element.31.rest_0_.act_ref, f32[16,512]{1,0:T(8,128)} %get-tuple-element.32.weight_ref), custom_call_target="tpu_custom_call" | custom-call | flops 1 | bytes 1 | tf_op jit(solution)/shard_map/first_frames/pallas_call | solution.py:386
  62.0 9.8 %query_grads.1 = (f32[448,3200]{1,0:T(8,128)}, f32[4,4,112,128]{3,2,1,0:T(8,128)}, f32[4,112,128]{2,1,0:T(8,128)}) custom-call(f32[448,3200]{1,0:T(8,128)} %query_ref.3, f32[448,3200]{1,0:T(8,128)} %grad_ref.1, f32[4,112,128]{2,1,0:T(8,128)} %fusion.before_ref, f32[4,4,112,128]{3,2,1,0:T(8,128)} %get-tuple-element.29.local_ref, f32[4,1,40,896]{3,2,1,0:T(8,128)} %copy-done.3, ...), custom_call_target="tpu_custom_call" | custom-call | flops 1 | bytes 1 | tf_op jit(solution)/shard_map/query_grads/pallas_call | solution.py:489
  72.8 2.8 %collective-permute-start.10 = (f32[4,1,40,896]{3,2,1,0:T(8,128)}, f32[4,1,40,896]{3,2,1,0:T(8,128)}, u32[]{:S(2)}, u32[]{:S(2)}) collective-permute-start(f32[4,1,40,896]{3,2,1,0:T(8,128)} %get-tuple-element.33.rest_1_), channel_id=1, source_target_pairs={{0,4},{4,8},{8,12},{12,16},{16,20},{20,24},{24,28},{1,5},{5,9},{9,... | collective-permute-start | bytes 1720328 | tf_op jit(solution)/shard_map/ppermute | solution.py:639
  75.5 4.5 %topped.3 = (f32[4,40,896]{2,1,0:T(8,128)}, f32[4,40,896]{2,1,0:T(8,128)}, f32[4,40,896]{2,1,0:T(8,128)}, f32[4,40,896]{2,1,0:T(8,128)}) custom-call(s32[1]{0:T(128)} %bitcast.1.me_ref, f32[4,4,40,896]{3,2,1,0:T(8,128)} %get-tuple-element.46.refs_0_.refs_1_.refs_2_.refs_3_, f32[4,4,40,896]{3,2,1,0:T(8,128)} %get-tuple-element.46.refs_0_.refs_1_.refs_2_.refs_3_, ...), custom_call_target="tpu_custom_call" | custom-call | flops 1 | bytes 1 | tf_op jit(solution)/shard_map/topped/pallas_call | solution.py:561
  82.1 12.6 %collective-permute-start.8 = (f32[2,112,128]{2,1,0:T(8,128)S(1)}, f32[2,112,128]{2,1,0:T(8,128)S(1)}, u32[]{:S(2)}, u32[]{:S(2)}) collective-permute-start(f32[2,112,128]{2,1,0:T(8,128)S(1)} %fusion.2), channel_id=1, source_target_pairs={{0,24},{4,28},{8,16},{12,20},{16,8},{20,12},{24,0},{28,4},{1,25},{... | collective-permute-start | bytes 344072 | tf_op jit(solution)/shard_map/ppermute | solution.py:144
  96.2 2.1 %collective-permute-done.8.refs_2_ = f32[2,112,128]{2,1,0:T(8,128)S(1)} collective-permute-done((f32[2,112,128]{2,1,0:T(8,128)S(1)}, f32[2,112,128]{2,1,0:T(8,128)S(1)}, u32[]{:S(2)}, u32[]{:S(2)}) %collective-permute-start.8) | collective-permute-done | bytes 114720 | tf_op jit(solution)/shard_map/ppermute | solution.py:144
  98.3 2.4 %collective-permute-start.16 = (f32[4,40,896]{2,1,0:T(8,128)}, f32[4,40,896]{2,1,0:T(8,128)}, u32[]{:S(2)}, u32[]{:S(2)}) collective-permute-start(f32[4,40,896]{2,1,0:T(8,128)} %get-tuple-element.49), channel_id=1, source_target_pairs={{0,2},{1,3},{2,0},{3,1},{4,6},{5,7},{6,4},{7,5},{8,10},{9,11},{10,... | collective-permute-start | bytes 1720328 | tf_op jit(solution)/shard_map/ppermute | solution.py:144
  104.0 10.4 %key_grads.1 = (f32[448,3200]{1,0:T(8,128)}, f32[448,3200]{1,0:T(8,128)}) custom-call(f32[448,3200]{1,0:T(8,128)} %key_ref.1, f32[448,3200]{1,0:T(8,128)} %value_ref.1, f32[4,112,128]{2,1,0:T(8,128)} %fusion.1.after_ref, f32[4,4,112,128]{3,2,1,0:T(8,128)} %get-tuple-element.38.part_ref), custom_call_target="tpu_custom_call" | custom-call | flops 1 | bytes 1 | tf_op jit(solution)/shard_map/key_grads/pallas_call | solution.py:531
  114.5 2.2 %topped.2 = (f32[1,40,896]{2,1,0:T(8,128)}, f32[1,40,896]{2,1,0:T(8,128)}, f32[1,40,896]{2,1,0:T(8,128)}, f32[1,40,896]{2,1,0:T(8,128)}) custom-call(s32[1]{0:T(128)} %bitcast.1.me_ref, f32[4,1,40,896]{3,2,1,0:T(8,128)} %get-tuple-element.41.refs_0_.refs_1_.refs_2_.refs_3_, f32[4,1,40,896]{3,2,1,0:T(8,128)} %get-tuple-element.41.refs_0_.refs_1_.refs_2_.refs_3_, ...), custom_call_target="tpu_custom_call" | custom-call | flops 1 | bytes 1 | tf_op jit(solution)/shard_map/topped/pallas_call | solution.py:561
  117.3 2.6 %collective-permute-start.12 = (f32[1,40,896]{2,1,0:T(8,128)}, f32[1,40,896]{2,1,0:T(8,128)}, u32[]{:S(2)}, u32[]{:S(2)}) collective-permute-start(f32[1,40,896]{2,1,0:T(8,128)} %get-tuple-element.44), channel_id=1, source_target_pairs={{0,2},{1,3},{2,0},{3,1},{4,6},{5,7},{6,4},{7,5},{8,10},{9,11},{10,... | collective-permute-start | bytes 430088 | tf_op jit(solution)/shard_map/ppermute | solution.py:144
  121.1 25.3 %collective-permute-done.16.refs_2_ = f32[4,40,896]{2,1,0:T(8,128)} collective-permute-done((f32[4,40,896]{2,1,0:T(8,128)}, f32[4,40,896]{2,1,0:T(8,128)}, u32[]{:S(2)}, u32[]{:S(2)}) %collective-permute-start.16) | collective-permute-done | bytes 573472 | tf_op jit(solution)/shard_map/ppermute | solution.py:144
  146.4 4.9 %placed.2.refs_5_ = f32[200,4,1792]{2,1,0:T(4,128)} custom-call(f32[4,40,896]{2,1,0:T(8,128)S(1)} %copy-done.11, f32[4,40,896]{2,1,0:T(8,128)} %collective-permute-done.15.refs_1_, f32[4,40,896]{2,1,0:T(8,128)} %collective-permute-done.16.refs_2_, f32[4,40,896]{2,1,0:T(8,128)} %collective-permute-done.17.refs_3_, f32[4,4,40,896]{3,2,1,0:T(8,128)S(1)} %all-to-all-done.1.refs_4_), custom_call_target="tpu_custom_call" | custom-call | flops 1 | bytes 1 | tf_op jit(solution)/shard_map/placed/pallas_call | solution.py:600
  151.3 10.5 %collective-permute-done.12.refs_2_ = f32[1,40,896]{2,1,0:T(8,128)} collective-permute-done((f32[1,40,896]{2,1,0:T(8,128)}, f32[1,40,896]{2,1,0:T(8,128)}, u32[]{:S(2)}, u32[]{:S(2)}) %collective-permute-start.12) | collective-permute-done | bytes 143392 | tf_op jit(solution)/shard_map/ppermute | solution.py:144
  161.8 2.4 %placed.3 = f32[200,4,1792]{2,1,0:T(4,128)} custom-call(f32[1,40,896]{2,1,0:T(8,128)S(1)} %copy-done.13, f32[1,40,896]{2,1,0:T(8,128)} %collective-permute-done.11.refs_1_, f32[1,40,896]{2,1,0:T(8,128)} %collective-permute-done.12.refs_2_, f32[1,40,896]{2,1,0:T(8,128)} %collective-permute-done.13.refs_3_, ...), custom_call_target="tpu_custom_call", output_to_operand_aliasing={{}: (5, {})} | custom-call | flops 1 | bytes 1 | tf_op jit(solution)/shard_map/placed/pallas_call | solution.py:600
  (66 shorter events, 17.5 us)
Async XLA Ops:
  7.2 1.8 %collective-permute-start = (f32[4,112,128]{2,1,0:T(8,128)}, f32[4,112,128]{2,1,0:T(8,128)S(1)}, u32[]{:S(2)}, u32[]{:S(2)}) collective-permute-start(f32[4,112,128]{2,1,0:T(8,128)} %get-tuple-element.28), channel_id=1, source_target_pairs={{0,4},{4,0},{8,12},{12,8},{16,20},{20,16},{24,28},{28,24},{1,5},{5... | collective-permute-start | bytes 688136 | tf_op jit(solution)/shard_map/ppermute | solution.py:144
  10.1 9.7 %collective-permute-start.3 = (f32[2,112,128]{2,1,0:T(8,128)S(1)}, f32[2,112,128]{2,1,0:T(8,128)S(1)}, u32[]{:S(2)}, u32[]{:S(2)}) collective-permute-start(f32[2,112,128]{2,1,0:T(8,128)S(1)} %fusion.3), channel_id=1, source_target_pairs={{0,24},{4,28},{8,16},{12,20},{16,8},{20,12},{24,0},{28,4},{1,25},{... | collective-permute-start | bytes 344072 | tf_op jit(solution)/shard_map/ppermute | solution.py:144
  13.9 5.9 %collective-permute-start.2 = (f32[2,112,128]{2,1,0:T(8,128)S(1)}, f32[2,112,128]{2,1,0:T(8,128)S(1)}, u32[]{:S(2)}, u32[]{:S(2)}) collective-permute-start(f32[2,112,128]{2,1,0:T(8,128)S(1)} %fusion.3), channel_id=1, source_target_pairs={{0,16},{4,20},{8,24},{12,28},{16,0},{20,4},{24,8},{28,12},{1,17},{... | collective-permute-start | bytes 344072 | tf_op jit(solution)/shard_map/ppermute | solution.py:144
  14.4 5.7 %collective-permute-start.1 = (f32[2,112,128]{2,1,0:T(8,128)S(1)}, f32[2,112,128]{2,1,0:T(8,128)S(1)}, u32[]{:S(2)}, u32[]{:S(2)}) collective-permute-start(f32[2,112,128]{2,1,0:T(8,128)S(1)} %fusion.3), channel_id=1, source_target_pairs={{0,8},{4,12},{8,0},{12,4},{16,24},{20,28},{24,16},{28,20},{1,9},{5... | collective-permute-start | bytes 344072 | tf_op jit(solution)/shard_map/ppermute | solution.py:144
  20.1 1.4 collective-permute-start.4
  25.8 20.8 %all-to-all-start = ((f32[4,1,40,896]{3,2,1,0:T(8,128)}), f32[4,1,40,896]{3,2,1,0:T(8,128)S(1)}, u32[]{:S(2)}, u32[]{:S(2)}) async-start(f32[4,1,40,896]{3,2,1,0:T(8,128)} %get-tuple-element.30), calls=%async_computation | async-start | bytes 1146880 | tf_op jit(solution)/shard_map/all_to_all | solution.py:626
  45.0 16.3 %copy-start.6 = (f32[4,112,128]{2,1,0:T(8,128)S(1)}, f32[4,112,128]{2,1,0:T(8,128)}, u32[]{:S(2)}) copy-start(f32[4,112,128]{2,1,0:T(8,128)} %copy-done.5) | copy-start | bytes 688132
  45.0 16.3 %copy-start.8 = (f32[2,112,128]{2,1,0:T(8,128)S(1)}, f32[2,112,128]{2,1,0:T(8,128)}, u32[]{:S(2)}) copy-start(f32[2,112,128]{2,1,0:T(8,128)} %copy-done.7) | copy-start | bytes 344068
  46.6 99.8 %all-to-all-start.1 = ((f32[4,4,40,896]{3,2,1,0:T(8,128)}), f32[4,4,40,896]{3,2,1,0:T(8,128)S(1)}, u32[]{:S(2)}, u32[]{:S(2)}) async-start(f32[4,4,40,896]{3,2,1,0:T(8,128)} %get-tuple-element.51), calls=%async_computation.1 | async-start | bytes 4587520 | tf_op jit(solution)/shard_map/all_to_all | solution.py:626
  55.9 19.6 %collective-permute-start.14 = (f32[4,4,40,896]{3,2,1,0:T(8,128)}, f32[4,4,40,896]{3,2,1,0:T(8,128)}, u32[]{:S(2)}, u32[]{:S(2)}) collective-permute-start(f32[4,4,40,896]{3,2,1,0:T(8,128)} %get-tuple-element.35.rest_2_), channel_id=1, source_target_pairs={{0,4},{4,8},{8,12},{12,16},{16,20},{20,24},{24,28},{1,5},{5,9},{9,... | collective-permute-start | bytes 6881288 | tf_op jit(solution)/shard_map/ppermute | solution.py:639
  71.8 10.3 %collective-permute-start.5 = (f32[4,112,128]{2,1,0:T(8,128)}, f32[4,112,128]{2,1,0:T(8,128)S(1)}, u32[]{:S(2)}, u32[]{:S(2)}) collective-permute-start(f32[4,112,128]{2,1,0:T(8,128)} %get-tuple-element.37), channel_id=1, source_target_pairs={{0,4},{4,0},{8,12},{12,8},{16,20},{20,16},{24,28},{28,24},{1,5},{5... | collective-permute-start | bytes 688136 | tf_op jit(solution)/shard_map/ppermute | solution.py:144
  72.8 41.7 %collective-permute-start.10 = (f32[4,1,40,896]{3,2,1,0:T(8,128)}, f32[4,1,40,896]{3,2,1,0:T(8,128)}, u32[]{:S(2)}, u32[]{:S(2)}) collective-permute-start(f32[4,1,40,896]{3,2,1,0:T(8,128)} %get-tuple-element.33.rest_1_), channel_id=1, source_target_pairs={{0,4},{4,8},{8,12},{12,16},{16,20},{20,24},{24,28},{1,5},{5,9},{9,... | collective-permute-start | bytes 1720328 | tf_op jit(solution)/shard_map/ppermute | solution.py:639
  80.0 39.9 %collective-permute-start.15 = (f32[4,40,896]{2,1,0:T(8,128)}, f32[4,40,896]{2,1,0:T(8,128)}, u32[]{:S(2)}, u32[]{:S(2)}) collective-permute-start(f32[4,40,896]{2,1,0:T(8,128)} %get-tuple-element.48), channel_id=1, source_target_pairs={{0,1},{1,0},{2,3},{3,2},{4,5},{5,4},{6,7},{7,6},{8,9},{9,8},{10,11... | collective-permute-start | bytes 1720328 | tf_op jit(solution)/shard_map/ppermute | solution.py:144
  82.1 16.2 %collective-permute-start.8 = (f32[2,112,128]{2,1,0:T(8,128)S(1)}, f32[2,112,128]{2,1,0:T(8,128)S(1)}, u32[]{:S(2)}, u32[]{:S(2)}) collective-permute-start(f32[2,112,128]{2,1,0:T(8,128)S(1)} %fusion.2), channel_id=1, source_target_pairs={{0,24},{4,28},{8,16},{12,20},{16,8},{20,12},{24,0},{28,4},{1,25},{... | collective-permute-start | bytes 344072 | tf_op jit(solution)/shard_map/ppermute | solution.py:144
  94.7 6.0 %collective-permute-start.7 = (f32[2,112,128]{2,1,0:T(8,128)S(1)}, f32[2,112,128]{2,1,0:T(8,128)S(1)}, u32[]{:S(2)}, u32[]{:S(2)}) collective-permute-start(f32[2,112,128]{2,1,0:T(8,128)S(1)} %fusion.2), channel_id=1, source_target_pairs={{0,16},{4,20},{8,24},{12,28},{16,0},{20,4},{24,8},{28,12},{1,17},{... | collective-permute-start | bytes 344072 | tf_op jit(solution)/shard_map/ppermute | solution.py:144
  95.2 6.7 %collective-permute-start.6 = (f32[2,112,128]{2,1,0:T(8,128)S(1)}, f32[2,112,128]{2,1,0:T(8,128)S(1)}, u32[]{:S(2)}, u32[]{:S(2)}) collective-permute-start(f32[2,112,128]{2,1,0:T(8,128)S(1)} %fusion.2), channel_id=1, source_target_pairs={{0,8},{4,12},{8,0},{12,4},{16,24},{20,28},{24,16},{28,20},{1,9},{5... | collective-permute-start | bytes 344072 | tf_op jit(solution)/shard_map/ppermute | solution.py:144
  98.3 48.1 %collective-permute-start.16 = (f32[4,40,896]{2,1,0:T(8,128)}, f32[4,40,896]{2,1,0:T(8,128)}, u32[]{:S(2)}, u32[]{:S(2)}) collective-permute-start(f32[4,40,896]{2,1,0:T(8,128)} %get-tuple-element.49), channel_id=1, source_target_pairs={{0,2},{1,3},{2,0},{3,1},{4,6},{5,7},{6,4},{7,5},{8,10},{9,11},{10,... | collective-permute-start | bytes 1720328 | tf_op jit(solution)/shard_map/ppermute | solution.py:144
  100.7 45.7 %collective-permute-start.17 = (f32[4,40,896]{2,1,0:T(8,128)}, f32[4,40,896]{2,1,0:T(8,128)}, u32[]{:S(2)}, u32[]{:S(2)}) collective-permute-start(f32[4,40,896]{2,1,0:T(8,128)} %get-tuple-element.50), channel_id=1, source_target_pairs={{0,3},{1,2},{2,1},{3,0},{4,7},{5,6},{6,5},{7,4},{8,11},{9,10},{10,... | collective-permute-start | bytes 1720328 | tf_op jit(solution)/shard_map/ppermute | solution.py:144
  101.9 1.4 collective-permute-start.9
  114.5 31.9 %copy-start.11 = (f32[4,40,896]{2,1,0:T(8,128)S(1)}, f32[4,40,896]{2,1,0:T(8,128)}, u32[]{:S(2)}) copy-start(f32[4,40,896]{2,1,0:T(8,128)} %get-tuple-element.47.refs_0_) | copy-start | bytes 1720324
  116.7 45.1 %copy-start.4 = (f32[4,1,40,896]{3,2,1,0:T(8,128)S(1)}, f32[4,1,40,896]{3,2,1,0:T(8,128)}, u32[]{:S(2)}) copy-start(f32[4,1,40,896]{3,2,1,0:T(8,128)} %copy-done.3) | copy-start | bytes 1720324
  116.7 34.6 %collective-permute-start.11 = (f32[1,40,896]{2,1,0:T(8,128)}, f32[1,40,896]{2,1,0:T(8,128)}, u32[]{:S(2)}, u32[]{:S(2)}) collective-permute-start(f32[1,40,896]{2,1,0:T(8,128)} %get-tuple-element.43), channel_id=1, source_target_pairs={{0,1},{1,0},{2,3},{3,2},{4,5},{5,4},{6,7},{7,6},{8,9},{9,8},{10,11... | collective-permute-start | bytes 430088 | tf_op jit(solution)/shard_map/ppermute | solution.py:144
  117.3 44.5 %collective-permute-start.12 = (f32[1,40,896]{2,1,0:T(8,128)}, f32[1,40,896]{2,1,0:T(8,128)}, u32[]{:S(2)}, u32[]{:S(2)}) collective-permute-start(f32[1,40,896]{2,1,0:T(8,128)} %get-tuple-element.44), channel_id=1, source_target_pairs={{0,2},{1,3},{2,0},{3,1},{4,6},{5,7},{6,4},{7,5},{8,10},{9,11},{10,... | collective-permute-start | bytes 430088 | tf_op jit(solution)/shard_map/ppermute | solution.py:144
  119.9 41.9 %collective-permute-start.13 = (f32[1,40,896]{2,1,0:T(8,128)}, f32[1,40,896]{2,1,0:T(8,128)}, u32[]{:S(2)}, u32[]{:S(2)}) collective-permute-start(f32[1,40,896]{2,1,0:T(8,128)} %get-tuple-element.45), channel_id=1, source_target_pairs={{0,3},{1,2},{2,1},{3,0},{4,7},{5,6},{6,5},{7,4},{8,11},{9,10},{10,... | collective-permute-start | bytes 430088 | tf_op jit(solution)/shard_map/ppermute | solution.py:144
  (12 other events, 90.3 us)

commit v3 on v2

--- a/solution.py
+++ b/solution.py
@@ -83,31 +83,22 @@
 
 
 def states_kernel(wins, heads, key_any, value_any, local_ref, total_ref, key_buf, value_buf, sems):
-    middle = wins[(len(wins) - 1) // 2][1]
-    halves = (slice(0, middle), slice(middle, wins[-1][1]))
-
-    def copies(h, half):
+    def copies(h):
         at = pl.ds(h * HEAD_SIZE, HEAD_SIZE)
         pairs = ((key_any, key_buf), (value_any, value_buf))
         return [
-            pltpu.make_async_copy(
-                src.at[at, halves[half]], dst.at[h, :, halves[half]], sems.at[i, half, h]
-            )
+            pltpu.make_async_copy(src.at[at, :], dst.at[h], sems.at[i, h])
             for i, (src, dst) in enumerate(pairs)
         ]
 
-    halved = 2 if middle < wins[-1][1] else 1
     for h in range(heads):
-        for half in range(halved):
-            for copy in copies(h, half):
-                copy.start()
+        for copy in copies(h):
+            copy.start()
     for h in range(heads):
+        for copy in copies(h):
+            copy.wait()
         total = jnp.zeros((HEAD_SIZE, AUG), f32)
         for f, win in enumerate(wins):
-            for half in range(halved):
-                if f == (0, (len(wins) - 1) // 2 + 1)[half]:
-                    for copy in copies(h, half):
-                        copy.wait()
             low, high, _, _ = win
             feat = jnp.where(inside(win), jnp.exp(key_buf[h, :, low:high]), 0.0)
             ones = jnp.ones((AUG - HEAD_SIZE, high - low), f32)
@@ -131,7 +122,7 @@
         scratch_shapes=[
             pltpu.VMEM((heads, HEAD_SIZE, tokens), f32),
             pltpu.VMEM((heads, HEAD_SIZE, tokens), f32),
-            pltpu.SemaphoreType.DMA((2, 2, heads)),
+            pltpu.SemaphoreType.DMA((2, heads)),
         ],
         compiler_params=pltpu.CompilerParams(vmem_limit_bytes=56 * 1024 * 1024),
         cost_estimate=cost(0, 0),
@@ -568,7 +559,7 @@
             out_specs=[pl.BlockSpec((1, *early.shape[2:]), lambda i, me: (i, 0, 0))] * count,
         ),
         out_shape=[in_hbm((steps, *early.shape[2:]))] * count,
-        compiler_params=params(58),
+        compiler_params=params(58 if steps > 1 else 12),
         cost_estimate=cost(0, 0),
         name="topped",
     )(me, *[early] * count, *[halo] * count, *after)
@@ -597,12 +588,14 @@
     frames = (early[0].shape[2] + late.shape[3]) // chans
     total = count * chans
     extra = [] if filled is None else [filled]
+    blocks = [pl.BlockSpec((1, *a.shape[1:]), lambda i: (i, 0, 0)) for a in early]
+    blocks.append(pl.BlockSpec((count, 1, *late.shape[2:]), lambda i: (0, i, 0, 0)))
+    if steps == 1:
+        blocks = [pl.BlockSpec(memory_space=pltpu.VMEM)] * (count + 1)
     return pl.pallas_call(
         functools.partial(place_kernel, chans, count),
         grid=(steps,),
-        in_specs=[pl.BlockSpec((1, *a.shape[1:]), lambda i: (i, 0, 0)) for a in early]
-        + [pl.BlockSpec((count, 1, *late.shape[2:]), lambda i: (0, i, 0, 0))]
-        + [pl.BlockSpec(memory_space=pl.ANY)] * len(extra),
+        in_specs=blocks + [pl.BlockSpec(memory_space=pl.ANY)] * len(extra),
         out_specs=pl.BlockSpec((rows, frames, total), lambda i: (start + i, 0, 0)),
         out_shape=jax.ShapeDtypeStruct((rows * (ROWS // BLOCK), frames, total), f32),
         input_output_aliases={count + 1: 0} if extra else {},

time: 165 us -> 165 us (level)
  local copies, waits for them, and re-layouts: 2.81 us -> 5.46 us
    unnamed x32 -> x36, local copies, waits for them, and re-layouts: 2.81 us -> 5.46 us
where the time goes in v3:
time: 165 us; the launch traced here: 164 us
  Pallas kernels  68 us (41%)
  starting transfers between devices  44.6 us (27%)
  waiting for transfers between devices  42.4 us (26%)
  local copies, waits for them, and re-layouts  5.46 us (3%)
  other arithmetic  2.54 us (2%)
    ppermute x16, waiting for transfers between devices, xor_move(): return lax.ppermute(array, axis, [(i, i ^ by) for i in range(count)])  40.8 us
    ppermute x16, starting transfers between devices, xor_move(): return lax.ppermute(array, axis, [(i, i ^ by) for i in range(count)])  31 us
    pallas_call x2, Pallas kernels, forward(): pl.pallas_call(functools.partial(forward_kernel, start, frames, heads, he...  18 us
    pallas_call x1, Pallas kernels, key_grads(): pl.pallas_call(functools.partial(key_kernel, wins), grid=(heads,), in_spe...  10.5 us
    pallas_call x1, Pallas kernels, query_grads(): pl.pallas_call(functools.partial(query_kernel, wins), grid=(heads,), in_s...  9.77 us
    all_to_all x2, starting transfers between devices, sent(): return lax.all_to_all(a, 'head', split_axis=0, concat_axis=0, tiled=True)  8.93 us
    pallas_call x2, Pallas kernels, first_frames(): pl.pallas_call(functools.partial(early_kernel, chans), grid=(steps,), in_...  8.3 us
    pallas_call x2, Pallas kernels, placed(): pl.pallas_call(functools.partial(place_kernel, chans, count), grid=(steps...  7.27 us
  transfers between devices with their start and end apart: 20, of which 8 were waited for; matrix products, arithmetic and copies ran while one was open for 1% of the time, Pallas kernels for 34%

profile of v3, /device:TPU:0, one launch (start us, length us, event | category | flops | bytes accessed | tf_op | source)
XLA Modules:
  0.0 163.9 jit_solution(12039696338200726818)
XLA Ops:
  0.6 6.2 %local_states.1 = (f32[4,4,112,128]{3,2,1,0:T(8,128)}, f32[4,112,128]{2,1,0:T(8,128)}) custom-call(f32[448,3200]{1,0:T(8,128)} %key_ref.1, f32[448,3200]{1,0:T(8,128)} %value_ref.1), custom_call_target="tpu_custom_call" | custom-call | flops 1 | bytes 1 | tf_op jit(solution)/shard_map/local_states/pallas_call | solution.py:115
  9.7 3.9 %collective-permute-start.3 = (f32[2,112,128]{2,1,0:T(8,128)S(1)}, f32[2,112,128]{2,1,0:T(8,128)S(1)}, u32[]{:S(2)}, u32[]{:S(2)}) collective-permute-start(f32[2,112,128]{2,1,0:T(8,128)S(1)} %fusion.3), channel_id=1, source_target_pairs={{0,24},{4,28},{8,16},{12,20},{16,8},{20,12},{24,0},{28,4},{1,25},{... | collective-permute-start | bytes 344072 | tf_op jit(solution)/shard_map/ppermute | solution.py:135
  14.3 2.6 %copy-done.1 = f32[448,3200]{1,0:T(8,128)S(1)} copy-done((f32[448,3200]{1,0:T(8,128)S(1)}, f32[448,3200]{1,0:T(8,128)}, u32[]{:S(2)}) %copy-start.1) | copy-done | bytes 5734424
  16.9 2.6 %turned.1.refs_3_ = f32[3200,512]{1,0:T(8,128)S(1)} custom-call(f32[448,3200]{1,0:T(8,128)S(1)} %copy-done.1), custom_call_target="tpu_custom_call" | custom-call | flops 1 | bytes 1 | tf_op jit(solution)/shard_map/turned/pallas_call | solution.py:206
  21.4 4.1 %forward_rows.2 = (f32[4,1,40,896]{3,2,1,0:T(8,128)}, f32[4,160,512]{2,1,0:T(8,128)}, f32[16,512]{1,0:T(8,128)}) custom-call(f32[2,112,128]{2,1,0:T(8,128)S(1)} %joined.2.part_ref, f32[2,112,128]{2,1,0:T(8,128)S(1)} %collective-permute-done.4.other_ref, f32[4,112,128]{2,1,0:T(8,128)S(1)} %collective-permute-done.mate_ref, f32[4,4,112,128]{3,2,1,0:T(8,128)S(1)} %copy-done.3, ...), custom_call_target="tpu_custom_call" | custom-call | flops 1 | bytes 1 | tf_op jit(solution)/shard_map/forward_rows/pallas_call | solution.py:415
  25.5 5.3 %all-to-all-start = ((f32[4,1,40,896]{3,2,1,0:T(8,128)}), f32[4,1,40,896]{3,2,1,0:T(8,128)S(1)}, u32[]{:S(2)}, u32[]{:S(2)}) async-start(f32[4,1,40,896]{3,2,1,0:T(8,128)} %get-tuple-element.30), calls=%async_computation | async-start | bytes 1146880 | tf_op jit(solution)/shard_map/all_to_all | solution.py:619
  30.8 13.8 %forward_rows.3 = (f32[4,4,40,896]{3,2,1,0:T(8,128)}, f32[4,640,512]{2,1,0:T(8,128)}, f32[16,512]{1,0:T(8,128)}) custom-call(f32[2,112,128]{2,1,0:T(8,128)} %copy-done.9, f32[2,112,128]{2,1,0:T(8,128)} %copy-done.11, f32[4,112,128]{2,1,0:T(8,128)} %copy-done.7, f32[4,4,112,128]{3,2,1,0:T(8,128)} %get-tuple-element.29.local_ref, f32[3,3,1792]{2,1,0:T(4,128)} %spatial_ref.3, ...), custom_call_target="tpu_custom_call" | custom-call | flops 1 | bytes 1 | tf_op jit(solution)/shard_map/forward_rows/pallas_call | solution.py:415
  46.3 3.6 %all-to-all-start.1 = ((f32[4,4,40,896]{3,2,1,0:T(8,128)}), f32[4,4,40,896]{3,2,1,0:T(8,128)S(1)}, u32[]{:S(2)}, u32[]{:S(2)}) async-start(f32[4,4,40,896]{3,2,1,0:T(8,128)} %get-tuple-element.51), calls=%async_computation.1 | async-start | bytes 4587520 | tf_op jit(solution)/shard_map/all_to_all | solution.py:619
  50.0 5.6 %first_frames.3 = (f32[4,4,40,896]{3,2,1,0:T(8,128)}, f32[4,4,40,896]{3,2,1,0:T(8,128)}) custom-call(f32[4,640,512]{2,1,0:T(8,128)} %get-tuple-element.34.act_ref, f32[16,512]{1,0:T(8,128)} %get-tuple-element.32.weight_ref), custom_call_target="tpu_custom_call" | custom-call | flops 1 | bytes 1 | tf_op jit(solution)/shard_map/first_frames/pallas_call | solution.py:377
  55.6 2.7 %collective-permute-start.14 = (f32[4,4,40,896]{3,2,1,0:T(8,128)}, f32[4,4,40,896]{3,2,1,0:T(8,128)}, u32[]{:S(2)}, u32[]{:S(2)}) collective-permute-start(f32[4,4,40,896]{3,2,1,0:T(8,128)} %get-tuple-element.35.rest_2_), channel_id=1, source_target_pairs={{0,4},{4,8},{8,12},{12,16},{16,20},{20,24},{24,28},{1,5},{5,9},{9,... | collective-permute-start | bytes 6881288 | tf_op jit(solution)/shard_map/ppermute | solution.py:632
  58.3 2.7 %first_frames.2 = (f32[4,1,40,896]{3,2,1,0:T(8,128)}, f32[4,1,40,896]{3,2,1,0:T(8,128)}) custom-call(f32[4,160,512]{2,1,0:T(8,128)} %get-tuple-element.31.rest_0_.act_ref, f32[16,512]{1,0:T(8,128)} %get-tuple-element.32.weight_ref), custom_call_target="tpu_custom_call" | custom-call | flops 1 | bytes 1 | tf_op jit(solution)/shard_map/first_frames/pallas_call | solution.py:377
  61.7 9.8 %query_grads.1 = (f32[448,3200]{1,0:T(8,128)}, f32[4,4,112,128]{3,2,1,0:T(8,128)}, f32[4,112,128]{2,1,0:T(8,128)}) custom-call(f32[448,3200]{1,0:T(8,128)} %query_ref.3, f32[448,3200]{1,0:T(8,128)} %grad_ref.1, f32[4,112,128]{2,1,0:T(8,128)} %fusion.before_ref, f32[4,4,112,128]{3,2,1,0:T(8,128)} %get-tuple-element.29.local_ref, f32[4,1,40,896]{3,2,1,0:T(8,128)} %copy-done.5, ...), custom_call_target="tpu_custom_call" | custom-call | flops 1 | bytes 1 | tf_op jit(solution)/shard_map/query_grads/pallas_call | solution.py:480
  74.4 4.5 %topped.3 = (f32[4,40,896]{2,1,0:T(8,128)}, f32[4,40,896]{2,1,0:T(8,128)}, f32[4,40,896]{2,1,0:T(8,128)}, f32[4,40,896]{2,1,0:T(8,128)}) custom-call(s32[1]{0:T(128)} %bitcast.1.me_ref, f32[4,4,40,896]{3,2,1,0:T(8,128)} %get-tuple-element.46.refs_0_.refs_1_.refs_2_.refs_3_, f32[4,4,40,896]{3,2,1,0:T(8,128)} %get-tuple-element.46.refs_0_.refs_1_.refs_2_.refs_3_, ...), custom_call_target="tpu_custom_call" | custom-call | flops 1 | bytes 1 | tf_op jit(solution)/shard_map/topped/pallas_call | solution.py:552
  78.9 2.0 %collective-permute-start.15 = (f32[4,40,896]{2,1,0:T(8,128)}, f32[4,40,896]{2,1,0:T(8,128)}, u32[]{:S(2)}, u32[]{:S(2)}) collective-permute-start(f32[4,40,896]{2,1,0:T(8,128)} %get-tuple-element.48), channel_id=1, source_target_pairs={{0,1},{1,0},{2,3},{3,2},{4,5},{5,4},{6,7},{7,6},{8,9},{9,8},{10,11... | collective-permute-start | bytes 1720328 | tf_op jit(solution)/shard_map/ppermute | solution.py:135
  81.0 13.4 %collective-permute-start.8 = (f32[2,112,128]{2,1,0:T(8,128)S(1)}, f32[2,112,128]{2,1,0:T(8,128)S(1)}, u32[]{:S(2)}, u32[]{:S(2)}) collective-permute-start(f32[2,112,128]{2,1,0:T(8,128)S(1)} %fusion.2), channel_id=1, source_target_pairs={{0,24},{4,28},{8,16},{12,20},{16,8},{20,12},{24,0},{28,4},{1,25},{... | collective-permute-start | bytes 344072 | tf_op jit(solution)/shard_map/ppermute | solution.py:135
  95.8 2.2 %collective-permute-done.8.refs_2_ = f32[2,112,128]{2,1,0:T(8,128)S(1)} collective-permute-done((f32[2,112,128]{2,1,0:T(8,128)S(1)}, f32[2,112,128]{2,1,0:T(8,128)S(1)}, u32[]{:S(2)}, u32[]{:S(2)}) %collective-permute-start.8) | collective-permute-done | bytes 114720 | tf_op jit(solution)/shard_map/ppermute | solution.py:135
  98.0 2.4 %collective-permute-start.16 = (f32[4,40,896]{2,1,0:T(8,128)}, f32[4,40,896]{2,1,0:T(8,128)}, u32[]{:S(2)}, u32[]{:S(2)}) collective-permute-start(f32[4,40,896]{2,1,0:T(8,128)} %get-tuple-element.49), channel_id=1, source_target_pairs={{0,2},{1,3},{2,0},{3,1},{4,6},{5,7},{6,4},{7,5},{8,10},{9,11},{10,... | collective-permute-start | bytes 1720328 | tf_op jit(solution)/shard_map/ppermute | solution.py:135
  103.7 10.5 %key_grads.1 = (f32[448,3200]{1,0:T(8,128)}, f32[448,3200]{1,0:T(8,128)}) custom-call(f32[448,3200]{1,0:T(8,128)} %key_ref.1, f32[448,3200]{1,0:T(8,128)} %value_ref.1, f32[4,112,128]{2,1,0:T(8,128)} %fusion.1.after_ref, f32[4,4,112,128]{3,2,1,0:T(8,128)} %get-tuple-element.38.part_ref), custom_call_target="tpu_custom_call" | custom-call | flops 1 | bytes 1 | tf_op jit(solution)/shard_map/key_grads/pallas_call | solution.py:522
  114.3 2.6 %copy-done.4 = f32[448,3200]{1,0:T(8,128)S(1)} copy-done((f32[448,3200]{1,0:T(8,128)S(1)}, f32[448,3200]{1,0:T(8,128)}, u32[]{:S(2)}) %copy-start.4) | copy-done | bytes 5734424
  118.4 2.6 %collective-permute-start.12 = (f32[1,40,896]{2,1,0:T(8,128)}, f32[1,40,896]{2,1,0:T(8,128)}, u32[]{:S(2)}, u32[]{:S(2)}) collective-permute-start(f32[1,40,896]{2,1,0:T(8,128)} %get-tuple-element.44), channel_id=1, source_target_pairs={{0,2},{1,3},{2,0},{3,1},{4,6},{5,7},{6,4},{7,5},{8,10},{9,11},{10,... | collective-permute-start | bytes 430088 | tf_op jit(solution)/shard_map/ppermute | solution.py:135
  122.2 23.9 %collective-permute-done.16.refs_2_ = f32[4,40,896]{2,1,0:T(8,128)} collective-permute-done((f32[4,40,896]{2,1,0:T(8,128)}, f32[4,40,896]{2,1,0:T(8,128)}, u32[]{:S(2)}, u32[]{:S(2)}) %collective-permute-start.16) | collective-permute-done | bytes 573472 | tf_op jit(solution)/shard_map/ppermute | solution.py:135
  146.1 4.9 %placed.2.refs_5_ = f32[200,4,1792]{2,1,0:T(4,128)} custom-call(f32[4,40,896]{2,1,0:T(8,128)S(1)} %copy-done.13, f32[4,40,896]{2,1,0:T(8,128)} %collective-permute-done.15.refs_1_, f32[4,40,896]{2,1,0:T(8,128)} %collective-permute-done.16.refs_2_, f32[4,40,896]{2,1,0:T(8,128)} %collective-permute-done.17.refs_3_, f32[4,4,40,896]{3,2,1,0:T(8,128)S(1)} %all-to-all-done.1.refs_4_), custom_call_target="tpu_custom_call" | custom-call | flops 1 | bytes 1 | tf_op jit(solution)/shard_map/placed/pallas_call | solution.py:595
  151.0 10.5 %collective-permute-done.12.refs_2_ = f32[1,40,896]{2,1,0:T(8,128)} collective-permute-done((f32[1,40,896]{2,1,0:T(8,128)}, f32[1,40,896]{2,1,0:T(8,128)}, u32[]{:S(2)}, u32[]{:S(2)}) %collective-permute-start.12) | collective-permute-done | bytes 143392 | tf_op jit(solution)/shard_map/ppermute | solution.py:135
  161.5 2.4 %placed.3 = f32[200,4,1792]{2,1,0:T(4,128)} custom-call(f32[1,40,896]{2,1,0:T(8,128)S(1)} %copy-done.15, f32[1,40,896]{2,1,0:T(8,128)} %collective-permute-done.11.refs_1_, f32[1,40,896]{2,1,0:T(8,128)} %collective-permute-done.12.refs_2_, f32[1,40,896]{2,1,0:T(8,128)} %collective-permute-done.13.refs_3_, ...), custom_call_target="tpu_custom_call", output_to_operand_aliasing={{}: (5, {})} | custom-call | flops 1 | bytes 1 | tf_op jit(solution)/shard_map/placed/pallas_call | solution.py:595
  (70 shorter events, 18.3 us)
Async XLA Ops:
  6.8 1.8 %collective-permute-start = (f32[4,112,128]{2,1,0:T(8,128)}, f32[4,112,128]{2,1,0:T(8,128)S(1)}, u32[]{:S(2)}, u32[]{:S(2)}) collective-permute-start(f32[4,112,128]{2,1,0:T(8,128)} %get-tuple-element.28), channel_id=1, source_target_pairs={{0,4},{4,0},{8,12},{12,8},{16,20},{20,16},{24,28},{28,24},{1,5},{5... | collective-permute-start | bytes 688136 | tf_op jit(solution)/shard_map/ppermute | solution.py:135
  9.7 9.8 %collective-permute-start.3 = (f32[2,112,128]{2,1,0:T(8,128)S(1)}, f32[2,112,128]{2,1,0:T(8,128)S(1)}, u32[]{:S(2)}, u32[]{:S(2)}) collective-permute-start(f32[2,112,128]{2,1,0:T(8,128)S(1)} %fusion.3), channel_id=1, source_target_pairs={{0,24},{4,28},{8,16},{12,20},{16,8},{20,12},{24,0},{28,4},{1,25},{... | collective-permute-start | bytes 344072 | tf_op jit(solution)/shard_map/ppermute | solution.py:135
  13.6 5.9 %collective-permute-start.2 = (f32[2,112,128]{2,1,0:T(8,128)S(1)}, f32[2,112,128]{2,1,0:T(8,128)S(1)}, u32[]{:S(2)}, u32[]{:S(2)}) collective-permute-start(f32[2,112,128]{2,1,0:T(8,128)S(1)} %fusion.3), channel_id=1, source_target_pairs={{0,16},{4,20},{8,24},{12,28},{16,0},{20,4},{24,8},{28,12},{1,17},{... | collective-permute-start | bytes 344072 | tf_op jit(solution)/shard_map/ppermute | solution.py:135
  14.2 5.6 %collective-permute-start.1 = (f32[2,112,128]{2,1,0:T(8,128)S(1)}, f32[2,112,128]{2,1,0:T(8,128)S(1)}, u32[]{:S(2)}, u32[]{:S(2)}) collective-permute-start(f32[2,112,128]{2,1,0:T(8,128)S(1)} %fusion.3), channel_id=1, source_target_pairs={{0,8},{4,12},{8,0},{12,4},{16,24},{20,28},{24,16},{28,20},{1,9},{5... | collective-permute-start | bytes 344072 | tf_op jit(solution)/shard_map/ppermute | solution.py:135
  19.8 1.4 collective-permute-start.4
  25.5 20.8 %all-to-all-start = ((f32[4,1,40,896]{3,2,1,0:T(8,128)}), f32[4,1,40,896]{3,2,1,0:T(8,128)S(1)}, u32[]{:S(2)}, u32[]{:S(2)}) async-start(f32[4,1,40,896]{3,2,1,0:T(8,128)} %get-tuple-element.30), calls=%async_computation | async-start | bytes 1146880 | tf_op jit(solution)/shard_map/all_to_all | solution.py:619
  44.6 16.3 %copy-start.8 = (f32[4,112,128]{2,1,0:T(8,128)S(1)}, f32[4,112,128]{2,1,0:T(8,128)}, u32[]{:S(2)}) copy-start(f32[4,112,128]{2,1,0:T(8,128)} %copy-done.7) | copy-start | bytes 688132
  44.7 16.3 %copy-start.10 = (f32[2,112,128]{2,1,0:T(8,128)S(1)}, f32[2,112,128]{2,1,0:T(8,128)}, u32[]{:S(2)}) copy-start(f32[2,112,128]{2,1,0:T(8,128)} %copy-done.9) | copy-start | bytes 344068
  46.3 99.8 %all-to-all-start.1 = ((f32[4,4,40,896]{3,2,1,0:T(8,128)}), f32[4,4,40,896]{3,2,1,0:T(8,128)S(1)}, u32[]{:S(2)}, u32[]{:S(2)}) async-start(f32[4,4,40,896]{3,2,1,0:T(8,128)} %get-tuple-element.51), calls=%async_computation.1 | async-start | bytes 4587520 | tf_op jit(solution)/shard_map/all_to_all | solution.py:619
  55.6 18.8 %collective-permute-start.14 = (f32[4,4,40,896]{3,2,1,0:T(8,128)}, f32[4,4,40,896]{3,2,1,0:T(8,128)}, u32[]{:S(2)}, u32[]{:S(2)}) collective-permute-start(f32[4,4,40,896]{3,2,1,0:T(8,128)} %get-tuple-element.35.rest_2_), channel_id=1, source_target_pairs={{0,4},{4,8},{8,12},{12,16},{16,20},{20,24},{24,28},{1,5},{5,9},{9,... | collective-permute-start | bytes 6881288 | tf_op jit(solution)/shard_map/ppermute | solution.py:632
  71.5 9.5 %collective-permute-start.5 = (f32[4,112,128]{2,1,0:T(8,128)}, f32[4,112,128]{2,1,0:T(8,128)S(1)}, u32[]{:S(2)}, u32[]{:S(2)}) collective-permute-start(f32[4,112,128]{2,1,0:T(8,128)} %get-tuple-element.37), channel_id=1, source_target_pairs={{0,4},{4,0},{8,12},{12,8},{16,20},{20,16},{24,28},{28,24},{1,5},{5... | collective-permute-start | bytes 688136 | tf_op jit(solution)/shard_map/ppermute | solution.py:135
  72.5 41.8 %collective-permute-start.10 = (f32[4,1,40,896]{3,2,1,0:T(8,128)}, f32[4,1,40,896]{3,2,1,0:T(8,128)S(1)}, u32[]{:S(2)}, u32[]{:S(2)}) collective-permute-start(f32[4,1,40,896]{3,2,1,0:T(8,128)} %get-tuple-element.33.rest_1_), channel_id=1, source_target_pairs={{0,4},{4,8},{8,12},{12,16},{16,20},{20,24},{24,28},{1,5},{5,9},{9,... | collective-permute-start | bytes 1720328 | tf_op jit(solution)/shard_map/ppermute | solution.py:632
  78.9 42.1 %collective-permute-start.15 = (f32[4,40,896]{2,1,0:T(8,128)}, f32[4,40,896]{2,1,0:T(8,128)}, u32[]{:S(2)}, u32[]{:S(2)}) collective-permute-start(f32[4,40,896]{2,1,0:T(8,128)} %get-tuple-element.48), channel_id=1, source_target_pairs={{0,1},{1,0},{2,3},{3,2},{4,5},{5,4},{6,7},{7,6},{8,9},{9,8},{10,11... | collective-permute-start | bytes 1720328 | tf_op jit(solution)/shard_map/ppermute | solution.py:135
  81.0 17.0 %collective-permute-start.8 = (f32[2,112,128]{2,1,0:T(8,128)S(1)}, f32[2,112,128]{2,1,0:T(8,128)S(1)}, u32[]{:S(2)}, u32[]{:S(2)}) collective-permute-start(f32[2,112,128]{2,1,0:T(8,128)S(1)} %fusion.2), channel_id=1, source_target_pairs={{0,24},{4,28},{8,16},{12,20},{16,8},{20,12},{24,0},{28,4},{1,25},{... | collective-permute-start | bytes 344072 | tf_op jit(solution)/shard_map/ppermute | solution.py:135
  94.4 6.0 %collective-permute-start.7 = (f32[2,112,128]{2,1,0:T(8,128)S(1)}, f32[2,112,128]{2,1,0:T(8,128)S(1)}, u32[]{:S(2)}, u32[]{:S(2)}) collective-permute-start(f32[2,112,128]{2,1,0:T(8,128)S(1)} %fusion.2), channel_id=1, source_target_pairs={{0,16},{4,20},{8,24},{12,28},{16,0},{20,4},{24,8},{28,12},{1,17},{... | collective-permute-start | bytes 344072 | tf_op jit(solution)/shard_map/ppermute | solution.py:135
  94.9 6.7 %collective-permute-start.6 = (f32[2,112,128]{2,1,0:T(8,128)S(1)}, f32[2,112,128]{2,1,0:T(8,128)S(1)}, u32[]{:S(2)}, u32[]{:S(2)}) collective-permute-start(f32[2,112,128]{2,1,0:T(8,128)S(1)} %fusion.2), channel_id=1, source_target_pairs={{0,8},{4,12},{8,0},{12,4},{16,24},{20,28},{24,16},{28,20},{1,9},{5... | collective-permute-start | bytes 344072 | tf_op jit(solution)/shard_map/ppermute | solution.py:135
  98.0 48.1 %collective-permute-start.16 = (f32[4,40,896]{2,1,0:T(8,128)}, f32[4,40,896]{2,1,0:T(8,128)}, u32[]{:S(2)}, u32[]{:S(2)}) collective-permute-start(f32[4,40,896]{2,1,0:T(8,128)} %get-tuple-element.49), channel_id=1, source_target_pairs={{0,2},{1,3},{2,0},{3,1},{4,6},{5,7},{6,4},{7,5},{8,10},{9,11},{10,... | collective-permute-start | bytes 1720328 | tf_op jit(solution)/shard_map/ppermute | solution.py:135
  100.3 45.8 %collective-permute-start.17 = (f32[4,40,896]{2,1,0:T(8,128)}, f32[4,40,896]{2,1,0:T(8,128)}, u32[]{:S(2)}, u32[]{:S(2)}) collective-permute-start(f32[4,40,896]{2,1,0:T(8,128)} %get-tuple-element.50), channel_id=1, source_target_pairs={{0,3},{1,2},{2,1},{3,0},{4,7},{5,6},{6,5},{7,4},{8,11},{9,10},{10,... | collective-permute-start | bytes 1720328 | tf_op jit(solution)/shard_map/ppermute | solution.py:135
  101.6 1.4 collective-permute-start.9
  103.7 42.4 %copy-start.13 = (f32[4,40,896]{2,1,0:T(8,128)S(1)}, f32[4,40,896]{2,1,0:T(8,128)}, u32[]{:S(2)}) copy-start(f32[4,40,896]{2,1,0:T(8,128)} %get-tuple-element.47.refs_0_) | copy-start | bytes 1720324
  117.8 43.7 %copy-start.6 = (f32[4,1,40,896]{3,2,1,0:T(8,128)S(1)}, f32[4,1,40,896]{3,2,1,0:T(8,128)}, u32[]{:S(2)}) copy-start(f32[4,1,40,896]{3,2,1,0:T(8,128)} %copy-done.5) | copy-start | bytes 1720324
  117.8 33.2 %collective-permute-start.11 = (f32[1,40,896]{2,1,0:T(8,128)}, f32[1,40,896]{2,1,0:T(8,128)}, u32[]{:S(2)}, u32[]{:S(2)}) collective-permute-start(f32[1,40,896]{2,1,0:T(8,128)} %get-tuple-element.43), channel_id=1, source_target_pairs={{0,1},{1,0},{2,3},{3,2},{4,5},{5,4},{6,7},{7,6},{8,9},{9,8},{10,11... | collective-permute-start | bytes 430088 | tf_op jit(solution)/shard_map/ppermute | solution.py:135
  118.4 43.1 %collective-permute-start.12 = (f32[1,40,896]{2,1,0:T(8,128)}, f32[1,40,896]{2,1,0:T(8,128)}, u32[]{:S(2)}, u32[]{:S(2)}) collective-permute-start(f32[1,40,896]{2,1,0:T(8,128)} %get-tuple-element.44), channel_id=1, source_target_pairs={{0,2},{1,3},{2,0},{3,1},{4,6},{5,7},{6,4},{7,5},{8,10},{9,11},{10,... | collective-permute-start | bytes 430088 | tf_op jit(solution)/shard_map/ppermute | solution.py:135
  121.0 40.5 %collective-permute-start.13 = (f32[1,40,896]{2,1,0:T(8,128)}, f32[1,40,896]{2,1,0:T(8,128)}, u32[]{:S(2)}, u32[]{:S(2)}) collective-permute-start(f32[1,40,896]{2,1,0:T(8,128)} %get-tuple-element.45), channel_id=1, source_target_pairs={{0,3},{1,2},{2,1},{3,0},{4,7},{5,6},{6,5},{7,4},{8,11},{9,10},{10,... | collective-permute-start | bytes 430088 | tf_op jit(solution)/shard_map/ppermute | solution.py:135
  (14 other events, 103.6 us)

commit v4 on v3

--- a/solution.py
+++ b/solution.py
@@ -638,7 +638,8 @@
     grad_key, grad_value = key_grads(key_feat, value_feat, later, part, [])
 
     def exchanged(blocks):
-        return [blocks[0]] + [xor_move(a, "head", s) for s, a in enumerate(blocks) if s]
+        moved = {s: xor_move(blocks[s], "head", s) for s in range(len(blocks) - 1, 0, -1)}
+        return [blocks[0]] + [moved[s] for s in range(1, len(blocks))]
 
     ties = [[grad_key], [grad_query]]
     arrived = [

time: 165 us -> 165 us (level)
  no operation moved by 1% of the time
where the time goes in v4:
time: 165 us; the launch traced here: 164 us
  Pallas kernels  68 us (41%)
  starting transfers between devices  44.6 us (27%)
  waiting for transfers between devices  42.4 us (26%)
  local copies, waits for them, and re-layouts  5.46 us (3%)
  other arithmetic  2.54 us (2%)
    ppermute x16, waiting for transfers between devices, xor_move(): return lax.ppermute(array, axis, [(i, i ^ by) for i in range(count)])  40.8 us
    ppermute x16, starting transfers between devices, xor_move(): return lax.ppermute(array, axis, [(i, i ^ by) for i in range(count)])  31 us
    pallas_call x2, Pallas kernels, forward(): pl.pallas_call(functools.partial(forward_kernel, start, frames, heads, he...  18 us
    pallas_call x1, Pallas kernels, key_grads(): pl.pallas_call(functools.partial(key_kernel, wins), grid=(heads,), in_spe...  10.5 us
    pallas_call x1, Pallas kernels, query_grads(): pl.pallas_call(functools.partial(query_kernel, wins), grid=(heads,), in_s...  9.77 us
    all_to_all x2, starting transfers between devices, sent(): return lax.all_to_all(a, 'head', split_axis=0, concat_axis=0, tiled=True)  8.93 us
    pallas_call x2, Pallas kernels, first_frames(): pl.pallas_call(functools.partial(early_kernel, chans), grid=(steps,), in_...  8.3 us
    pallas_call x2, Pallas kernels, placed(): pl.pallas_call(functools.partial(place_kernel, chans, count), grid=(steps...  7.27 us
  transfers between devices with their start and end apart: 20, of which 8 were waited for; matrix products, arithmetic and copies ran while one was open for 1% of the time, Pallas kernels for 34%

profile of v4, /device:TPU:0, one launch (start us, length us, event | category | flops | bytes accessed | tf_op | source)
XLA Modules:
  0.0 163.9 jit_solution(12039696338200726818)
XLA Ops:
  0.6 6.2 %local_states.1 = (f32[4,4,112,128]{3,2,1,0:T(8,128)}, f32[4,112,128]{2,1,0:T(8,128)}) custom-call(f32[448,3200]{1,0:T(8,128)} %key_ref.1, f32[448,3200]{1,0:T(8,128)} %value_ref.1), custom_call_target="tpu_custom_call" | custom-call | flops 1 | bytes 1 | tf_op jit(solution)/shard_map/local_states/pallas_call | solution.py:115
  9.7 3.9 %collective-permute-start.3 = (f32[2,112,128]{2,1,0:T(8,128)S(1)}, f32[2,112,128]{2,1,0:T(8,128)S(1)}, u32[]{:S(2)}, u32[]{:S(2)}) collective-permute-start(f32[2,112,128]{2,1,0:T(8,128)S(1)} %fusion.3), channel_id=1, source_target_pairs={{0,24},{4,28},{8,16},{12,20},{16,8},{20,12},{24,0},{28,4},{1,25},{... | collective-permute-start | bytes 344072 | tf_op jit(solution)/shard_map/ppermute | solution.py:135
  14.3 2.6 %copy-done.1 = f32[448,3200]{1,0:T(8,128)S(1)} copy-done((f32[448,3200]{1,0:T(8,128)S(1)}, f32[448,3200]{1,0:T(8,128)}, u32[]{:S(2)}) %copy-start.1) | copy-done | bytes 5734424
  16.9 2.6 %turned.1.refs_3_ = f32[3200,512]{1,0:T(8,128)S(1)} custom-call(f32[448,3200]{1,0:T(8,128)S(1)} %copy-done.1), custom_call_target="tpu_custom_call" | custom-call | flops 1 | bytes 1 | tf_op jit(solution)/shard_map/turned/pallas_call | solution.py:206
  21.4 4.1 %forward_rows.2 = (f32[4,1,40,896]{3,2,1,0:T(8,128)}, f32[4,160,512]{2,1,0:T(8,128)}, f32[16,512]{1,0:T(8,128)}) custom-call(f32[2,112,128]{2,1,0:T(8,128)S(1)} %joined.2.part_ref, f32[2,112,128]{2,1,0:T(8,128)S(1)} %collective-permute-done.4.other_ref, f32[4,112,128]{2,1,0:T(8,128)S(1)} %collective-permute-done.mate_ref, f32[4,4,112,128]{3,2,1,0:T(8,128)S(1)} %copy-done.3, ...), custom_call_target="tpu_custom_call" | custom-call | flops 1 | bytes 1 | tf_op jit(solution)/shard_map/forward_rows/pallas_call | solution.py:415
  25.5 5.3 %all-to-all-start = ((f32[4,1,40,896]{3,2,1,0:T(8,128)}), f32[4,1,40,896]{3,2,1,0:T(8,128)S(1)}, u32[]{:S(2)}, u32[]{:S(2)}) async-start(f32[4,1,40,896]{3,2,1,0:T(8,128)} %get-tuple-element.30), calls=%async_computation | async-start | bytes 1146880 | tf_op jit(solution)/shard_map/all_to_all | solution.py:619
  30.8 13.8 %forward_rows.3 = (f32[4,4,40,896]{3,2,1,0:T(8,128)}, f32[4,640,512]{2,1,0:T(8,128)}, f32[16,512]{1,0:T(8,128)}) custom-call(f32[2,112,128]{2,1,0:T(8,128)} %copy-done.9, f32[2,112,128]{2,1,0:T(8,128)} %copy-done.11, f32[4,112,128]{2,1,0:T(8,128)} %copy-done.7, f32[4,4,112,128]{3,2,1,0:T(8,128)} %get-tuple-element.29.local_ref, f32[3,3,1792]{2,1,0:T(4,128)} %spatial_ref.3, ...), custom_call_target="tpu_custom_call" | custom-call | flops 1 | bytes 1 | tf_op jit(solution)/shard_map/forward_rows/pallas_call | solution.py:415
  46.3 3.6 %all-to-all-start.1 = ((f32[4,4,40,896]{3,2,1,0:T(8,128)}), f32[4,4,40,896]{3,2,1,0:T(8,128)S(1)}, u32[]{:S(2)}, u32[]{:S(2)}) async-start(f32[4,4,40,896]{3,2,1,0:T(8,128)} %get-tuple-element.51), calls=%async_computation.1 | async-start | bytes 4587520 | tf_op jit(solution)/shard_map/all_to_all | solution.py:619
  50.0 5.6 %first_frames.3 = (f32[4,4,40,896]{3,2,1,0:T(8,128)}, f32[4,4,40,896]{3,2,1,0:T(8,128)}) custom-call(f32[4,640,512]{2,1,0:T(8,128)} %get-tuple-element.34.act_ref, f32[16,512]{1,0:T(8,128)} %get-tuple-element.32.weight_ref), custom_call_target="tpu_custom_call" | custom-call | flops 1 | bytes 1 | tf_op jit(solution)/shard_map/first_frames/pallas_call | solution.py:377
  55.6 2.7 %collective-permute-start.14 = (f32[4,4,40,896]{3,2,1,0:T(8,128)}, f32[4,4,40,896]{3,2,1,0:T(8,128)}, u32[]{:S(2)}, u32[]{:S(2)}) collective-permute-start(f32[4,4,40,896]{3,2,1,0:T(8,128)} %get-tuple-element.35.rest_2_), channel_id=1, source_target_pairs={{0,4},{4,8},{8,12},{12,16},{16,20},{20,24},{24,28},{1,5},{5,9},{9,... | collective-permute-start | bytes 6881288 | tf_op jit(solution)/shard_map/ppermute | solution.py:632
  58.3 2.7 %first_frames.2 = (f32[4,1,40,896]{3,2,1,0:T(8,128)}, f32[4,1,40,896]{3,2,1,0:T(8,128)}) custom-call(f32[4,160,512]{2,1,0:T(8,128)} %get-tuple-element.31.rest_0_.act_ref, f32[16,512]{1,0:T(8,128)} %get-tuple-element.32.weight_ref), custom_call_target="tpu_custom_call" | custom-call | flops 1 | bytes 1 | tf_op jit(solution)/shard_map/first_frames/pallas_call | solution.py:377
  61.7 9.8 %query_grads.1 = (f32[448,3200]{1,0:T(8,128)}, f32[4,4,112,128]{3,2,1,0:T(8,128)}, f32[4,112,128]{2,1,0:T(8,128)}) custom-call(f32[448,3200]{1,0:T(8,128)} %query_ref.3, f32[448,3200]{1,0:T(8,128)} %grad_ref.1, f32[4,112,128]{2,1,0:T(8,128)} %fusion.before_ref, f32[4,4,112,128]{3,2,1,0:T(8,128)} %get-tuple-element.29.local_ref, f32[4,1,40,896]{3,2,1,0:T(8,128)} %copy-done.5, ...), custom_call_target="tpu_custom_call" | custom-call | flops 1 | bytes 1 | tf_op jit(solution)/shard_map/query_grads/pallas_call | solution.py:480
  74.4 4.5 %topped.3 = (f32[4,40,896]{2,1,0:T(8,128)}, f32[4,40,896]{2,1,0:T(8,128)}, f32[4,40,896]{2,1,0:T(8,128)}, f32[4,40,896]{2,1,0:T(8,128)}) custom-call(s32[1]{0:T(128)} %bitcast.1.me_ref, f32[4,4,40,896]{3,2,1,0:T(8,128)} %get-tuple-element.46.refs_0_.refs_1_.refs_2_.refs_3_, f32[4,4,40,896]{3,2,1,0:T(8,128)} %get-tuple-element.46.refs_0_.refs_1_.refs_2_.refs_3_, ...), custom_call_target="tpu_custom_call" | custom-call | flops 1 | bytes 1 | tf_op jit(solution)/shard_map/topped/pallas_call | solution.py:552
  78.9 2.0 %collective-permute-start.15 = (f32[4,40,896]{2,1,0:T(8,128)}, f32[4,40,896]{2,1,0:T(8,128)}, u32[]{:S(2)}, u32[]{:S(2)}) collective-permute-start(f32[4,40,896]{2,1,0:T(8,128)} %get-tuple-element.48), channel_id=1, source_target_pairs={{0,1},{1,0},{2,3},{3,2},{4,5},{5,4},{6,7},{7,6},{8,9},{9,8},{10,11... | collective-permute-start | bytes 1720328 | tf_op jit(solution)/shard_map/ppermute | solution.py:135
  81.0 13.4 %collective-permute-start.8 = (f32[2,112,128]{2,1,0:T(8,128)S(1)}, f32[2,112,128]{2,1,0:T(8,128)S(1)}, u32[]{:S(2)}, u32[]{:S(2)}) collective-permute-start(f32[2,112,128]{2,1,0:T(8,128)S(1)} %fusion.2), channel_id=1, source_target_pairs={{0,24},{4,28},{8,16},{12,20},{16,8},{20,12},{24,0},{28,4},{1,25},{... | collective-permute-start | bytes 344072 | tf_op jit(solution)/shard_map/ppermute | solution.py:135
  95.8 2.2 %collective-permute-done.8.refs_2_ = f32[2,112,128]{2,1,0:T(8,128)S(1)} collective-permute-done((f32[2,112,128]{2,1,0:T(8,128)S(1)}, f32[2,112,128]{2,1,0:T(8,128)S(1)}, u32[]{:S(2)}, u32[]{:S(2)}) %collective-permute-start.8) | collective-permute-done | bytes 114720 | tf_op jit(solution)/shard_map/ppermute | solution.py:135
  98.0 2.4 %collective-permute-start.16 = (f32[4,40,896]{2,1,0:T(8,128)}, f32[4,40,896]{2,1,0:T(8,128)}, u32[]{:S(2)}, u32[]{:S(2)}) collective-permute-start(f32[4,40,896]{2,1,0:T(8,128)} %get-tuple-element.49), channel_id=1, source_target_pairs={{0,2},{1,3},{2,0},{3,1},{4,6},{5,7},{6,4},{7,5},{8,10},{9,11},{10,... | collective-permute-start | bytes 1720328 | tf_op jit(solution)/shard_map/ppermute | solution.py:135
  103.7 10.5 %key_grads.1 = (f32[448,3200]{1,0:T(8,128)}, f32[448,3200]{1,0:T(8,128)}) custom-call(f32[448,3200]{1,0:T(8,128)} %key_ref.1, f32[448,3200]{1,0:T(8,128)} %value_ref.1, f32[4,112,128]{2,1,0:T(8,128)} %fusion.1.after_ref, f32[4,4,112,128]{3,2,1,0:T(8,128)} %get-tuple-element.38.part_ref), custom_call_target="tpu_custom_call" | custom-call | flops 1 | bytes 1 | tf_op jit(solution)/shard_map/key_grads/pallas_call | solution.py:522
  114.3 2.6 %copy-done.4 = f32[448,3200]{1,0:T(8,128)S(1)} copy-done((f32[448,3200]{1,0:T(8,128)S(1)}, f32[448,3200]{1,0:T(8,128)}, u32[]{:S(2)}) %copy-start.4) | copy-done | bytes 5734424
  118.4 2.6 %collective-permute-start.12 = (f32[1,40,896]{2,1,0:T(8,128)}, f32[1,40,896]{2,1,0:T(8,128)}, u32[]{:S(2)}, u32[]{:S(2)}) collective-permute-start(f32[1,40,896]{2,1,0:T(8,128)} %get-tuple-element.44), channel_id=1, source_target_pairs={{0,2},{1,3},{2,0},{3,1},{4,6},{5,7},{6,4},{7,5},{8,10},{9,11},{10,... | collective-permute-start | bytes 430088 | tf_op jit(solution)/shard_map/ppermute | solution.py:135
  122.2 23.9 %collective-permute-done.16.refs_2_ = f32[4,40,896]{2,1,0:T(8,128)} collective-permute-done((f32[4,40,896]{2,1,0:T(8,128)}, f32[4,40,896]{2,1,0:T(8,128)}, u32[]{:S(2)}, u32[]{:S(2)}) %collective-permute-start.16) | collective-permute-done | bytes 573472 | tf_op jit(solution)/shard_map/ppermute | solution.py:135
  146.1 4.9 %placed.2.refs_5_ = f32[200,4,1792]{2,1,0:T(4,128)} custom-call(f32[4,40,896]{2,1,0:T(8,128)S(1)} %copy-done.13, f32[4,40,896]{2,1,0:T(8,128)} %collective-permute-done.15.refs_1_, f32[4,40,896]{2,1,0:T(8,128)} %collective-permute-done.16.refs_2_, f32[4,40,896]{2,1,0:T(8,128)} %collective-permute-done.17.refs_3_, f32[4,4,40,896]{3,2,1,0:T(8,128)S(1)} %all-to-all-done.1.refs_4_), custom_call_target="tpu_custom_call" | custom-call | flops 1 | bytes 1 | tf_op jit(solution)/shard_map/placed/pallas_call | solution.py:595
  151.0 10.5 %collective-permute-done.12.refs_2_ = f32[1,40,896]{2,1,0:T(8,128)} collective-permute-done((f32[1,40,896]{2,1,0:T(8,128)}, f32[1,40,896]{2,1,0:T(8,128)}, u32[]{:S(2)}, u32[]{:S(2)}) %collective-permute-start.12) | collective-permute-done | bytes 143392 | tf_op jit(solution)/shard_map/ppermute | solution.py:135
  161.5 2.4 %placed.3 = f32[200,4,1792]{2,1,0:T(4,128)} custom-call(f32[1,40,896]{2,1,0:T(8,128)S(1)} %copy-done.15, f32[1,40,896]{2,1,0:T(8,128)} %collective-permute-done.11.refs_1_, f32[1,40,896]{2,1,0:T(8,128)} %collective-permute-done.12.refs_2_, f32[1,40,896]{2,1,0:T(8,128)} %collective-permute-done.13.refs_3_, ...), custom_call_target="tpu_custom_call", output_to_operand_aliasing={{}: (5, {})} | custom-call | flops 1 | bytes 1 | tf_op jit(solution)/shard_map/placed/pallas_call | solution.py:595
  (70 shorter events, 18.3 us)
Async XLA Ops:
  6.8 1.8 %collective-permute-start = (f32[4,112,128]{2,1,0:T(8,128)}, f32[4,112,128]{2,1,0:T(8,128)S(1)}, u32[]{:S(2)}, u32[]{:S(2)}) collective-permute-start(f32[4,112,128]{2,1,0:T(8,128)} %get-tuple-element.28), channel_id=1, source_target_pairs={{0,4},{4,0},{8,12},{12,8},{16,20},{20,16},{24,28},{28,24},{1,5},{5... | collective-permute-start | bytes 688136 | tf_op jit(solution)/shard_map/ppermute | solution.py:135
  9.7 9.8 %collective-permute-start.3 = (f32[2,112,128]{2,1,0:T(8,128)S(1)}, f32[2,112,128]{2,1,0:T(8,128)S(1)}, u32[]{:S(2)}, u32[]{:S(2)}) collective-permute-start(f32[2,112,128]{2,1,0:T(8,128)S(1)} %fusion.3), channel_id=1, source_target_pairs={{0,24},{4,28},{8,16},{12,20},{16,8},{20,12},{24,0},{28,4},{1,25},{... | collective-permute-start | bytes 344072 | tf_op jit(solution)/shard_map/ppermute | solution.py:135
  13.6 5.9 %collective-permute-start.2 = (f32[2,112,128]{2,1,0:T(8,128)S(1)}, f32[2,112,128]{2,1,0:T(8,128)S(1)}, u32[]{:S(2)}, u32[]{:S(2)}) collective-permute-start(f32[2,112,128]{2,1,0:T(8,128)S(1)} %fusion.3), channel_id=1, source_target_pairs={{0,16},{4,20},{8,24},{12,28},{16,0},{20,4},{24,8},{28,12},{1,17},{... | collective-permute-start | bytes 344072 | tf_op jit(solution)/shard_map/ppermute | solution.py:135
  14.2 5.6 %collective-permute-start.1 = (f32[2,112,128]{2,1,0:T(8,128)S(1)}, f32[2,112,128]{2,1,0:T(8,128)S(1)}, u32[]{:S(2)}, u32[]{:S(2)}) collective-permute-start(f32[2,112,128]{2,1,0:T(8,128)S(1)} %fusion.3), channel_id=1, source_target_pairs={{0,8},{4,12},{8,0},{12,4},{16,24},{20,28},{24,16},{28,20},{1,9},{5... | collective-permute-start | bytes 344072 | tf_op jit(solution)/shard_map/ppermute | solution.py:135
  19.8 1.4 collective-permute-start.4
  25.5 20.8 %all-to-all-start = ((f32[4,1,40,896]{3,2,1,0:T(8,128)}), f32[4,1,40,896]{3,2,1,0:T(8,128)S(1)}, u32[]{:S(2)}, u32[]{:S(2)}) async-start(f32[4,1,40,896]{3,2,1,0:T(8,128)} %get-tuple-element.30), calls=%async_computation | async-start | bytes 1146880 | tf_op jit(solution)/shard_map/all_to_all | solution.py:619
  44.6 16.3 %copy-start.8 = (f32[4,112,128]{2,1,0:T(8,128)S(1)}, f32[4,112,128]{2,1,0:T(8,128)}, u32[]{:S(2)}) copy-start(f32[4,112,128]{2,1,0:T(8,128)} %copy-done.7) | copy-start | bytes 688132
  44.7 16.3 %copy-start.10 = (f32[2,112,128]{2,1,0:T(8,128)S(1)}, f32[2,112,128]{2,1,0:T(8,128)}, u32[]{:S(2)}) copy-start(f32[2,112,128]{2,1,0:T(8,128)} %copy-done.9) | copy-start | bytes 344068
  46.3 99.8 %all-to-all-start.1 = ((f32[4,4,40,896]{3,2,1,0:T(8,128)}), f32[4,4,40,896]{3,2,1,0:T(8,128)S(1)}, u32[]{:S(2)}, u32[]{:S(2)}) async-start(f32[4,4,40,896]{3,2,1,0:T(8,128)} %get-tuple-element.51), calls=%async_computation.1 | async-start | bytes 4587520 | tf_op jit(solution)/shard_map/all_to_all | solution.py:619
  55.6 18.8 %collective-permute-start.14 = (f32[4,4,40,896]{3,2,1,0:T(8,128)}, f32[4,4,40,896]{3,2,1,0:T(8,128)}, u32[]{:S(2)}, u32[]{:S(2)}) collective-permute-start(f32[4,4,40,896]{3,2,1,0:T(8,128)} %get-tuple-element.35.rest_2_), channel_id=1, source_target_pairs={{0,4},{4,8},{8,12},{12,16},{16,20},{20,24},{24,28},{1,5},{5,9},{9,... | collective-permute-start | bytes 6881288 | tf_op jit(solution)/shard_map/ppermute | solution.py:632
  71.5 9.5 %collective-permute-start.5 = (f32[4,112,128]{2,1,0:T(8,128)}, f32[4,112,128]{2,1,0:T(8,128)S(1)}, u32[]{:S(2)}, u32[]{:S(2)}) collective-permute-start(f32[4,112,128]{2,1,0:T(8,128)} %get-tuple-element.37), channel_id=1, source_target_pairs={{0,4},{4,0},{8,12},{12,8},{16,20},{20,16},{24,28},{28,24},{1,5},{5... | collective-permute-start | bytes 688136 | tf_op jit(solution)/shard_map/ppermute | solution.py:135
  72.5 41.8 %collective-permute-start.10 = (f32[4,1,40,896]{3,2,1,0:T(8,128)}, f32[4,1,40,896]{3,2,1,0:T(8,128)S(1)}, u32[]{:S(2)}, u32[]{:S(2)}) collective-permute-start(f32[4,1,40,896]{3,2,1,0:T(8,128)} %get-tuple-element.33.rest_1_), channel_id=1, source_target_pairs={{0,4},{4,8},{8,12},{12,16},{16,20},{20,24},{24,28},{1,5},{5,9},{9,... | collective-permute-start | bytes 1720328 | tf_op jit(solution)/shard_map/ppermute | solution.py:632
  78.9 42.1 %collective-permute-start.15 = (f32[4,40,896]{2,1,0:T(8,128)}, f32[4,40,896]{2,1,0:T(8,128)}, u32[]{:S(2)}, u32[]{:S(2)}) collective-permute-start(f32[4,40,896]{2,1,0:T(8,128)} %get-tuple-element.48), channel_id=1, source_target_pairs={{0,1},{1,0},{2,3},{3,2},{4,5},{5,4},{6,7},{7,6},{8,9},{9,8},{10,11... | collective-permute-start | bytes 1720328 | tf_op jit(solution)/shard_map/ppermute | solution.py:135
  81.0 17.0 %collective-permute-start.8 = (f32[2,112,128]{2,1,0:T(8,128)S(1)}, f32[2,112,128]{2,1,0:T(8,128)S(1)}, u32[]{:S(2)}, u32[]{:S(2)}) collective-permute-start(f32[2,112,128]{2,1,0:T(8,128)S(1)} %fusion.2), channel_id=1, source_target_pairs={{0,24},{4,28},{8,16},{12,20},{16,8},{20,12},{24,0},{28,4},{1,25},{... | collective-permute-start | bytes 344072 | tf_op jit(solution)/shard_map/ppermute | solution.py:135
  94.4 6.0 %collective-permute-start.7 = (f32[2,112,128]{2,1,0:T(8,128)S(1)}, f32[2,112,128]{2,1,0:T(8,128)S(1)}, u32[]{:S(2)}, u32[]{:S(2)}) collective-permute-start(f32[2,112,128]{2,1,0:T(8,128)S(1)} %fusion.2), channel_id=1, source_target_pairs={{0,16},{4,20},{8,24},{12,28},{16,0},{20,4},{24,8},{28,12},{1,17},{... | collective-permute-start | bytes 344072 | tf_op jit(solution)/shard_map/ppermute | solution.py:135
  94.9 6.7 %collective-permute-start.6 = (f32[2,112,128]{2,1,0:T(8,128)S(1)}, f32[2,112,128]{2,1,0:T(8,128)S(1)}, u32[]{:S(2)}, u32[]{:S(2)}) collective-permute-start(f32[2,112,128]{2,1,0:T(8,128)S(1)} %fusion.2), channel_id=1, source_target_pairs={{0,8},{4,12},{8,0},{12,4},{16,24},{20,28},{24,16},{28,20},{1,9},{5... | collective-permute-start | bytes 344072 | tf_op jit(solution)/shard_map/ppermute | solution.py:135
  98.0 48.1 %collective-permute-start.16 = (f32[4,40,896]{2,1,0:T(8,128)}, f32[4,40,896]{2,1,0:T(8,128)}, u32[]{:S(2)}, u32[]{:S(2)}) collective-permute-start(f32[4,40,896]{2,1,0:T(8,128)} %get-tuple-element.49), channel_id=1, source_target_pairs={{0,2},{1,3},{2,0},{3,1},{4,6},{5,7},{6,4},{7,5},{8,10},{9,11},{10,... | collective-permute-start | bytes 1720328 | tf_op jit(solution)/shard_map/ppermute | solution.py:135
  100.3 45.8 %collective-permute-start.17 = (f32[4,40,896]{2,1,0:T(8,128)}, f32[4,40,896]{2,1,0:T(8,128)}, u32[]{:S(2)}, u32[]{:S(2)}) collective-permute-start(f32[4,40,896]{2,1,0:T(8,128)} %get-tuple-element.50), channel_id=1, source_target_pairs={{0,3},{1,2},{2,1},{3,0},{4,7},{5,6},{6,5},{7,4},{8,11},{9,10},{10,... | collective-permute-start | bytes 1720328 | tf_op jit(solution)/shard_map/ppermute | solution.py:135
  101.6 1.4 collective-permute-start.9
  103.7 42.4 %copy-start.13 = (f32[4,40,896]{2,1,0:T(8,128)S(1)}, f32[4,40,896]{2,1,0:T(8,128)}, u32[]{:S(2)}) copy-start(f32[4,40,896]{2,1,0:T(8,128)} %get-tuple-element.47.refs_0_) | copy-start | bytes 1720324
  117.8 43.7 %copy-start.6 = (f32[4,1,40,896]{3,2,1,0:T(8,128)S(1)}, f32[4,1,40,896]{3,2,1,0:T(8,128)}, u32[]{:S(2)}) copy-start(f32[4,1,40,896]{3,2,1,0:T(8,128)} %copy-done.5) | copy-start | bytes 1720324
  117.8 33.2 %collective-permute-start.11 = (f32[1,40,896]{2,1,0:T(8,128)}, f32[1,40,896]{2,1,0:T(8,128)}, u32[]{:S(2)}, u32[]{:S(2)}) collective-permute-start(f32[1,40,896]{2,1,0:T(8,128)} %get-tuple-element.43), channel_id=1, source_target_pairs={{0,1},{1,0},{2,3},{3,2},{4,5},{5,4},{6,7},{7,6},{8,9},{9,8},{10,11... | collective-permute-start | bytes 430088 | tf_op jit(solution)/shard_map/ppermute | solution.py:135
  118.4 43.1 %collective-permute-start.12 = (f32[1,40,896]{2,1,0:T(8,128)}, f32[1,40,896]{2,1,0:T(8,128)}, u32[]{:S(2)}, u32[]{:S(2)}) collective-permute-start(f32[1,40,896]{2,1,0:T(8,128)} %get-tuple-element.44), channel_id=1, source_target_pairs={{0,2},{1,3},{2,0},{3,1},{4,6},{5,7},{6,4},{7,5},{8,10},{9,11},{10,... | collective-permute-start | bytes 430088 | tf_op jit(solution)/shard_map/ppermute | solution.py:135
  121.0 40.5 %collective-permute-start.13 = (f32[1,40,896]{2,1,0:T(8,128)}, f32[1,40,896]{2,1,0:T(8,128)}, u32[]{:S(2)}, u32[]{:S(2)}) collective-permute-start(f32[1,40,896]{2,1,0:T(8,128)} %get-tuple-element.45), channel_id=1, source_target_pairs={{0,3},{1,2},{2,1},{3,0},{4,7},{5,6},{6,5},{7,4},{8,11},{9,10},{10,... | collective-permute-start | bytes 430088 | tf_op jit(solution)/shard_map/ppermute | solution.py:135
  (14 other events, 103.6 us)
